TPU v7x, 32 devices: a whole 2x2x4 slice. The times are simulated.
32 devices in a mesh: groups: 2 (over y), wide: 4 (over z), tail: 2 (over x), sub: 2 (over core).
Axes of the slice: x: 2, y: 2, z: 4, core: 2. Of those that a mesh axis runs over, the one named last changes fastest.
Arguments:
- head_embed: float32 [512, 512], P(('groups', 'wide')), parts along dimension 0, may hold values from -2.1 to 2.1
- tail_embed: float32 [512, 512], P(('groups', 'tail'), 'sub'), parts along dimension 0, may hold values from -2.1 to 2.1
- core_mats: float32 [8, 512, 512], P(('groups', 'wide'), None, 'sub'), parts along dimension 0, may hold values from -0.25 to 0.25
- labels: int32 [512, 8, 256], P(('groups', 'wide'), None, 'tail'), parts along dimension 0, may hold values 0 or 1
- core_lists: int32 [4, 8], P(('groups', 'tail')), parts along dimension 0, may hold values from 0 to 3, as said below
Outputs:
- grad_head: float32 [512, 512], P(('groups', 'wide', 'tail', 'sub')), parts along dimension 0
- grad_tail: float32 [4, 128, 512], P(('groups', 'tail'), 'wide', 'sub'), parts along dimension 0
- grad_cores: float32 [8, 512, 512], P(('groups', 'tail'), 'wide', 'sub'), parts along dimension 0
There are 2 independent parts, one for each index of `groups`. A program takes and returns all parts, laid end to end along the dimension named above; each array names one. Nothing has to cross between parts.
Inputs may be any that keep to these rules, and one draw needn't show every extreme that they name: `core_lists`: every one of the 4 core ids stands somewhere in the lists; ids may repeat.
All inputs are finite; a program needn't handle non-finite values. No bound on the sum of `labels` on one device may be relied on, other than what follows from the above.
Results may differ from a plain program's by a relative error of at most 0.0001.
Values sent between devices are 32-bit elements; how exact they have to be, the bound alone decides.
No kernel may reach another device: no remote copies, remote signals or barrier semaphores. Data moves between devices by JAX's collectives and lax.ppermute only.
A program may use at most 64 MiB of HBM per device.

v0:
```python
import math

import jax
import jax.numpy as jnp
from jax import lax
from jax.sharding import PartitionSpec as P


def broadcast(value, axis, source):
    kept = jnp.where(lax.axis_index(axis) == source, value, 0).astype(value.dtype)
    return lax.psum(kept, axis)


def body(head_embed, tail_embed, core_mats, labels, core_lists):
    highest = lax.Precision.HIGHEST
    slot_count = core_lists.shape[1]
    half_width = tail_embed.shape[1]
    listed = core_lists[0]
    wide_count = lax.axis_size("wide")
    tail_acc = jnp.zeros((tail_embed.shape[0], half_width), jnp.float32)
    head_acc = jnp.zeros(head_embed.shape, jnp.float32)
    core_terms = []
    for slot_index in range(slot_count):
        relation = listed[slot_index]
        owned_count = core_mats.shape[0]
        local_core = lax.dynamic_index_in_dim(core_mats, relation % owned_count, 0, keepdims=False)
        matrix = broadcast(local_core, "wide", relation // owned_count)
        projected = jnp.dot(
            head_embed, matrix, precision=highest, preferred_element_type=jnp.float32
        )
        partial_score = lax.dot_general(
            projected, tail_embed, (((1,), (1,)), ((), ())), precision=highest
        )
        score_tile = lax.psum(partial_score, "sub")
        residual = jax.nn.sigmoid(score_tile) - labels[:, slot_index, :].astype(jnp.float32)
        tail_acc = tail_acc + lax.dot_general(
            residual, projected, (((0,), (0,)), ((), ())), precision=highest
        )
        weighted = jnp.dot(
            residual, tail_embed, precision=highest, preferred_element_type=jnp.float32
        )
        head_acc = head_acc + lax.dot_general(
            weighted, matrix, (((1,), (1,)), ((), ())), precision=highest
        )
        core_term = lax.dot_general(
            head_embed, weighted, (((0,), (0,)), ((), ())), precision=highest
        )
        core_terms.append(core_term)
    core_rows, tail_stack = (
        lax.psum_scatter(jnp.stack(core_terms), "wide", scatter_dimension=1, tiled=True),
        lax.psum_scatter(tail_acc[None], "wide", scatter_dimension=1, tiled=True),
    )
    tail_part = tail_stack[0]
    relation_count = core_mats.shape[0] * wide_count
    selector = (jnp.arange(relation_count, dtype=jnp.int32)[:, None] == listed[None, :]).astype(
        jnp.float32
    )
    combined = jnp.einsum("rj,jab->rab", selector, core_rows, precision=highest)
    heads_total = head_embed.shape[0] * wide_count
    tails_total = tail_embed.shape[0] * lax.axis_size("tail")
    core_grad = lax.psum_scatter(combined, "tail", scatter_dimension=0, tiled=True) * (
        1.0 / math.sqrt(heads_total * tail_embed.shape[0])
    )
    head_grad = lax.psum_scatter(head_acc, ("tail", "sub"), scatter_dimension=0, tiled=True) * (
        1.0 / math.sqrt(slot_count * tails_total)
    )
    tail_grad = (tail_part * (1.0 / math.sqrt(slot_count * heads_total)))[None]
    return (head_grad, tail_grad, core_grad)


def solution(mesh):
    in_specs = (
        P(("groups", "wide"), None),
        P(("groups", "tail"), "sub"),
        P(("groups", "wide"), None, "sub"),
        P(("groups", "wide"), None, "tail"),
        P(("groups", "tail"), None),
    )
    out_specs = (
        P(("groups", "wide", "tail", "sub"), None),
        P(("groups", "tail"), "wide", "sub"),
        P(("groups", "tail"), "wide", "sub"),
    )
    return jax.shard_map(body, mesh=mesh, in_specs=in_specs, out_specs=out_specs, check_vma=False)
```

profile of v0, /device:TPU:0, one launch (start us, length us, event | category | flops | bytes accessed | tf_op | source)
XLA Modules:
  0.0 376.8 jit_solution(4680497996379933882)
XLA Ops:
  7.2 1.6 fusion.23
  13.9 3.2 select_bitcast_fusion
  17.2 160.3 %all-reduce.5.cloned.1.call-done = (f32[512,256]{1,0:T(8,128)}, f32[512,256]{1,0:T(8,128)}, f32[512,256]{1,0:T(8,128)}, f32[512,256]{1,0:T(8,128)}, f32[512,256]...) async-done(((f32[512,256]{1,0:T(8,128)}, f32[512,256]{1,0:T(8,128)}, f32[512,256]{1,0:T(8,128)}, f32[512,256]{1,0:T(8,128)}, ...) | async-done | bytes 4194320 | tf_op jit(solution)/shard_map/psum | solution.py:11
  177.5 1.6 fusion.24
  179.1 1.5 fusion.27
  182.4 1.5 fusion.29
  184.8 1.5 fusion.31
  187.1 1.5 fusion.33
  193.7 17.4 %all-reduce.7.cloned.1.call-done = (f32[64,128]{1,0:T(8,128)}, f32[64,128]{1,0:T(8,128)}, f32[64,128]{1,0:T(8,128)}, f32[64,128]{1,0:T(8,128)}, f32[64,128]{1,0:...) async-done(((f32[64,128]{1,0:T(8,128)}, f32[64,128]{1,0:T(8,128)}, f32[64,128]{1,0:T(8,128)}, f32[64,128]{1,0:T(8,128)}, f32[64,128]{1,0:T(8,128)}, ...) | async-done | bytes 262160 | tf_op jit(solution)/shard_map/psum | solution.py:34
  220.6 1.5 fusion.6
  222.1 1.4 fusion.5
  223.5 1.4 fusion.4
  225.0 1.4 fusion.3
  237.1 1.8 convolution_add_fusion.9
  238.9 1.7 fusion.26
  240.6 1.7 convolution_add_fusion.6
  242.3 1.5 convolution_add_fusion.5
  248.7 1.8 fusion.8
  250.6 58.4 %reduce-scatter.9.cloned.1.call-done = f32[8,128,256]{1,2,0:T(8,128)} async-done(((f32[8,512,256]{1,2,0:T(8,128)}), f32[8,128,256]{1,2,0:T(8,128)}) %reduce-scatter.9.cloned.1.call-update) | async-done | bytes 1048592 | tf_op jit(solution)/shard_map/reduce_scatter | solution.py:50
  308.9 1.7 copy.26
  312.2 19.8 %reduce-scatter.5.cloned.1.call-done = f32[16,512]{1,0:T(8,128)} async-done(((f32[64,512]{1,0:T(8,128)}), f32[16,512]{1,0:T(8,128)}) %reduce-scatter.5.cloned.1.call-update) | async-done | bytes 32784 | tf_op jit(solution)/shard_map/reduce_scatter | solution.py:64
  333.4 19.9 %reduce-scatter.7.cloned.1.call-done = f32[1,32,256]{2,1,0:T(8,128)} async-done(((f32[1,128,256]{2,1,0:T(8,128)}), f32[1,32,256]{2,1,0:T(8,128)}) %reduce-scatter.7.cloned.1.call-update) | async-done | bytes 32784 | tf_op jit(solution)/shard_map/reduce_scatter | solution.py:51
  354.7 13.6 %reduce-scatter.11.cloned.1.call-done = f32[2,128,256]{2,1,0:T(8,128)} async-done(((f32[4,128,256]{2,1,0:T(8,128)}), f32[2,128,256]{2,1,0:T(8,128)}) %reduce-scatter.11.cloned.1.call-update) | async-done | bytes 262160 | tf_op jit(solution)/shard_map/reduce_scatter | solution.py:61
  368.3 1.7 broadcast_multiply_fusion
  (131 shorter events, 37.8 us)
Async XLA Ops:
  7.2 170.4 %copy-start = (f32[64,512]{1,0:T(8,128)S(1)}, f32[64,512]{1,0:T(8,128)}, u32[]{:S(2)}) copy-start(f32[64,512]{1,0:T(8,128)} %param.5) | copy-start | bytes 393220
  7.2 170.3 %all-reduce.5.cloned.1.call-start = ((), (), s32[]{:S(2)}) async-start(), calls=%async_computation.8 | async-start | bytes 8388608 | tf_op jit(solution)/shard_map/psum | solution.py:11
  13.9 166.7 %copy-start.1 = (f32[128,256]{1,0:T(8,128)S(1)}, f32[128,256]{1,0:T(8,128)}, u32[]{:S(2)}) copy-start(f32[128,256]{1,0:T(8,128)} %param.6) | copy-start | bytes 393220
  17.1 176.3 %copy-start.38 = (s32[64,8,128]{2,1,0:T(8,128)S(1)}, s32[64,8,128]{2,1,0:T(8,128)}, u32[]{:S(2)}) copy-start(s32[64,8,128]{2,1,0:T(8,128)} %param.8) | copy-start | bytes 786436
  17.1 194.0 %all-reduce.7.cloned.1.call-start = ((), (), s32[]{:S(2)}) async-start(), calls=%async_computation.9 | async-start | bytes 524288 | tf_op jit(solution)/shard_map/psum | solution.py:34
  177.5 14.6 %copy-start.2 = (f32[512,256]{1,0:T(8,128)S(1)}, f32[512,256]{1,0:T(8,128)}, u32[]{:S(2)}) copy-start(f32[512,256]{1,0:T(8,128)} %get-tuple-element.13) | copy-start | bytes 1572868
  193.4 115.5 %reduce-scatter.9.cloned.1.call-start = ((), (), s32[]{:S(2)}) async-start(), calls=%async_computation.6 | async-start | bytes 5242880 | tf_op jit(solution)/shard_map/reduce_scatter | solution.py:50
  193.7 34.2 %copy-start.30 = (s32[64,1,128]{2,1,0:T(1,128)}, s32[64,1,128]{2,1,0:T(1,128)S(1)}, u32[]{:S(2)}) copy-start(s32[64,1,128]{2,1,0:T(1,128)S(1)} %get-tuple-element.30) | copy-start | bytes 98308
  193.7 34.2 %copy-start.31 = (s32[64,1,128]{2,1,0:T(1,128)}, s32[64,1,128]{2,1,0:T(1,128)S(1)}, u32[]{:S(2)}) copy-start(s32[64,1,128]{2,1,0:T(1,128)S(1)} %get-tuple-element.31) | copy-start | bytes 98308
  193.7 34.1 %copy-start.32 = (s32[64,1,128]{2,1,0:T(1,128)}, s32[64,1,128]{2,1,0:T(1,128)S(1)}, u32[]{:S(2)}) copy-start(s32[64,1,128]{2,1,0:T(1,128)S(1)} %get-tuple-element.32) | copy-start | bytes 98308
  193.7 34.1 %copy-start.33 = (s32[64,1,128]{2,1,0:T(1,128)}, s32[64,1,128]{2,1,0:T(1,128)S(1)}, u32[]{:S(2)}) copy-start(s32[64,1,128]{2,1,0:T(1,128)S(1)} %get-tuple-element.33) | copy-start | bytes 98308
  193.7 34.1 %copy-start.34 = (s32[64,1,128]{2,1,0:T(1,128)}, s32[64,1,128]{2,1,0:T(1,128)S(1)}, u32[]{:S(2)}) copy-start(s32[64,1,128]{2,1,0:T(1,128)S(1)} %get-tuple-element.34) | copy-start | bytes 98308
  193.7 34.1 %copy-start.35 = (s32[64,1,128]{2,1,0:T(1,128)}, s32[64,1,128]{2,1,0:T(1,128)S(1)}, u32[]{:S(2)}) copy-start(s32[64,1,128]{2,1,0:T(1,128)S(1)} %get-tuple-element.35) | copy-start | bytes 98308
  193.7 34.1 %copy-start.36 = (s32[64,1,128]{2,1,0:T(1,128)}, s32[64,1,128]{2,1,0:T(1,128)S(1)}, u32[]{:S(2)}) copy-start(s32[64,1,128]{2,1,0:T(1,128)S(1)} %get-tuple-element.36) | copy-start | bytes 98308
  193.7 34.1 %copy-start.37 = (s32[64,1,128]{2,1,0:T(1,128)}, s32[64,1,128]{2,1,0:T(1,128)S(1)}, u32[]{:S(2)}) copy-start(s32[64,1,128]{2,1,0:T(1,128)S(1)} %get-tuple-element.37) | copy-start | bytes 98308
  214.5 14.8 %copy-start.16 = (f32[64,256]{1,0:T(8,128)}, f32[64,256]{1,0:T(8,128)S(1)}, u32[]{:S(2)}) copy-start(f32[64,256]{1,0:T(8,128)S(1)} %fusion.21) | copy-start | bytes 196612
  230.8 13.6 %copy-start.5 = (f32[512,256]{1,0:T(8,128)S(1)}, f32[512,256]{1,0:T(8,128)}, u32[]{:S(2)}) copy-start(f32[512,256]{1,0:T(8,128)} %get-tuple-element.10) | copy-start | bytes 1572868
  230.8 101.2 %reduce-scatter.5.cloned.1.call-start = ((), (), s32[]{:S(2)}) async-start(), calls=%async_computation.4 | async-start | bytes 163840 | tf_op jit(solution)/shard_map/reduce_scatter | solution.py:64
  231.0 14.0 %copy-start.21 = (f32[64,256]{1,0:T(8,128)S(1)}, f32[64,256]{1,0:T(8,128)}, u32[]{:S(2)}) copy-start(f32[64,256]{1,0:T(8,128)} %copy-done.20) | copy-start | bytes 196612
  231.1 14.6 %copy-start.19 = (f32[64,256]{1,0:T(8,128)S(1)}, f32[64,256]{1,0:T(8,128)}, u32[]{:S(2)}) copy-start(f32[64,256]{1,0:T(8,128)} %copy-done.18) | copy-start | bytes 196612
  231.1 15.2 %copy-start.17 = (f32[64,256]{1,0:T(8,128)S(1)}, f32[64,256]{1,0:T(8,128)}, u32[]{:S(2)}) copy-start(f32[64,256]{1,0:T(8,128)} %copy-done.16) | copy-start | bytes 196612
  242.3 68.3 %copy-start.39 = (s32[1,8]{1,0:T(1,128)S(1)}, s32[1,8]{1,0:T(1,128)}, u32[]{:S(2)}) copy-start(s32[1,8]{1,0:T(1,128)} %param.9) | copy-start | bytes 100
  247.6 105.7 %reduce-scatter.7.cloned.1.call-start = ((), (), s32[]{:S(2)}) async-start(), calls=%async_computation.5 | async-start | bytes 163840 | tf_op jit(solution)/shard_map/reduce_scatter | solution.py:51
  250.5 117.8 %reduce-scatter.11.cloned.1.call-start = ((), (), s32[]{:S(2)}) async-start(), calls=%async_computation.7 | async-start | bytes 786432 | tf_op jit(solution)/shard_map/reduce_scatter | solution.py:61
  (22 other events, 194.9 us)
Sparse Core Ops, SparseCore 0:
  17.2 160.2 all-reduce.4
  193.5 17.5 all-reduce.6
  230.9 77.9 reduce-scatter.8
  311.9 20.0 reduce-scatter.4
  334.1 19.1 reduce-scatter.6
  355.5 12.7 reduce-scatter.10
where the time goes:
time: 379 us; the launch traced here: 377 us
  waiting for transfers between devices  290 us (77%)
  matrix products  54.9 us (14%)
  between operations  19.7 us (5%)
  other arithmetic  7.64 us (2%)
  local copies, waits for them, and re-layouts  4.56 us (1%)
    psum x1, waiting for transfers between devices, broadcast(): return lax.psum(kept, axis)  160 us
    reduce_scatter x1, waiting for transfers between devices, body(): lax.psum_scatter(jnp.stack(core_terms), 'wide', scatter_dimension=1, tile...  58.4 us
    reduce_scatter x1, waiting for transfers between devices, body(): lax.psum_scatter(tail_acc[None], 'wide', scatter_dimension=1, tiled=True)  19.9 us
    reduce_scatter x1, waiting for transfers between devices, body(): lax.psum_scatter(head_acc, ('tail', 'sub'), scatter_dimension=0, tiled=True)  19.8 us
    psum x1, waiting for transfers between devices, body(): score_tile = lax.psum(partial_score, 'sub')  17.4 us
    reduce_scatter x1, waiting for transfers between devices, body(): lax.psum_scatter(combined, 'tail', scatter_dimension=0, tiled=True)  13.6 us
    dot_general x8, matrix products, body(): lax.dot_general(head_embed, weighted, (((0,), (0,)), ((), ())), precision...  11.5 us
    dot_general x8, matrix products, body(): lax.dot_general(residual, projected, (((0,), (0,)), ((), ())), precision=...  10.6 us
  transfers between devices with their start and end apart: 6, of which 6 were waited for; matrix products, arithmetic and copies ran while one was open for 7% of the time, Pallas kernels for 0%

commit v1 on v0

v1 whole, which is shorter than its diff:
```python
import functools
import math

import jax
import jax.numpy as jnp
from jax import lax
from jax.experimental import pallas as pl
from jax.experimental.pallas import tpu as pltpu
from jax.sharding import PartitionSpec as P


F32 = jnp.float32
VMEM_LIMIT = 48 * 1024 * 1024
NN = (((1,), (0,)), ((), ()))
NT = (((1,), (1,)), ((), ()))
TN = (((0,), (0,)), ((), ()))


def split(value):
    high = value.astype(jnp.bfloat16)
    low = (value - high.astype(F32)).astype(jnp.bfloat16)
    return high, low


def dot3(left, right, dims):
    lh, ll = left
    rh, rl = right
    mul = functools.partial(lax.dot_general, dimension_numbers=dims, preferred_element_type=F32)
    return mul(lh, rh) + (mul(lh, rl) + mul(ll, rh))


def rows_at(ref, index, count):
    if count % 8 == 0:
        return ref[pl.ds(pl.multiple_of(index * count, count), count), :]
    per = 8 // count
    window = ref[pl.ds(pl.multiple_of(index // per * 8, 8), 8), :]
    found = window[0:count]
    for i in range(1, per):
        found = jnp.where(index % per == i, window[i * count : (i + 1) * count], found)
    return found


def place():
    return lax.axis_index("wide"), lax.axis_index("tail"), lax.axis_index("sub")


def pack_kernel(wide, cols, list_ref, label_ref, head_ref, tail_ref, *outs):
    z_refs, x_ref, head_own, label_own = outs[: wide - 1], outs[-3], outs[-2], outs[-1]
    w, t, s = place()
    block, slots, width = label_ref.shape
    chunk = block // (2 * cols)
    rows = block // 2
    half = tail_ref.shape[1]
    for part in range(2):
        for col in range(cols):
            start = pl.multiple_of((col * 2 + (s ^ part)) * chunk, chunk)
            at = part * rows + col * chunk
            embed = head_ref[pl.ds(start, chunk), :]
            head_own[at : at + chunk, :] = embed
            slot_labels = [label_ref[pl.ds(start, chunk), j, :] for j in range(slots)]
            for k in range(wide):
                total = jnp.zeros((chunk, width), jnp.int32)
                for j in range(slots):
                    total = total + jnp.where(list_ref[0, j] == (w ^ k), slot_labels[j], 0)
                total = total.astype(F32)
                if k == 0:
                    label_own[at : at + chunk, :] = total
                    lane = (at // rows) * width
                    row = tail_ref.shape[0] + at % rows
                    x_ref[row : row + chunk, lane : lane + width] = total
                else:
                    z_refs[k - 1][at : at + chunk, half : half + width] = total
                    if part == 0:
                        z_refs[k - 1][at : at + chunk, 0:half] = embed[:, 0:half]
                        z_refs[k - 1][rows + at : rows + at + chunk, 0:half] = embed[:, half:]
    x_ref[0 : tail_ref.shape[0], :] = tail_ref[...]
    count = jnp.int32(0)
    for j in range(slots):
        count = count + (list_ref[0, j] == w).astype(jnp.int32)
    x_ref[tail_ref.shape[0] + rows :, :] = jnp.full((8, half), count.astype(F32), F32)


def query_kernel(core_ref, tail_ref, *refs):
    x_refs, out_ref = refs[:-1], refs[-1]
    depth = tail_ref.shape[0]
    tails = [tail_ref[...]] + [x[0:depth, :] for x in x_refs]
    out_ref[...] = dot3(split(core_ref[0]), split(jnp.concatenate(tails, axis=0)), NT)


def grad_kernel(wide, cols, refs):
    (list_ref, core_ref, query_ref, query_other, head_own, label_own, x_refs, z_refs, swap_refs, outs, own_ref,
     heads, resid, outer, tails) = refs
    w, t, s = place()
    block, dim = head_own.shape
    width = label_own.shape[1]
    rows = block // 2
    chunk = rows // cols
    half = core_ref.shape[2]
    heads[0:block, :] = head_own[...]
    for k in range(1, wide):
        at = k * block
        for part, ref in enumerate((z_refs[k - 1][0], swap_refs[k - 1][0])):
            heads[at + part * rows : at + part * rows + rows, 0:half] = ref[0:rows, 0:half]
            heads[at + part * rows : at + part * rows + rows, half:] = ref[rows:, 0:half]
    query = split(query_ref[...] + query_other[...])
    head_parts = split(heads[...])
    score = dot3(head_parts, query, NN)
    prob = jax.nn.sigmoid(score)
    count = jnp.int32(0)
    for j in range(list_ref.shape[1]):
        count = count + (list_ref[0, j] == w).astype(jnp.int32)
    depth = x_refs[0].shape[0] - 8 - rows if x_refs else 0
    for o in range(cols):
        lanes = slice(o * width, (o + 1) * width)
        times = count.astype(F32) if o == 0 else x_refs[o - 1][depth + rows : depth + rows + 1, 0:width]
        if o == 0:
            resid[0:block, lanes] = times * prob[0:block, lanes] - label_own[...]
        else:
            ref = x_refs[o - 1]
            for part in range(2):
                resid[part * rows : part * rows + rows, lanes] = (
                    times * prob[part * rows : part * rows + rows, lanes]
                    - ref[depth : depth + rows, part * width : (part + 1) * width]
                )
        for k in range(1, wide):
            first, last = (half, half + width) if o < 2 else (0, width)
            mine = z_refs[k - 1][o // 2][:, first:last]
            other = swap_refs[k - 1][o // 2]
            other = jnp.concatenate([other[rows:, first:last], other[0:rows, first:last]], axis=0)
            label = jnp.where(s == o % 2, mine, other)
            resid[k * block : (k + 1) * block, lanes] = times * prob[k * block : (k + 1) * block, lanes] - label
    resid_parts = split(resid[...])
    outer[...] = dot3(head_parts, resid_parts, TN)
    tails[...] = dot3(split(outer[:, 0:width]), split(core_ref[0]), TN)
    picked = [resid[pl.ds(pl.multiple_of(k * block + t * chunk, chunk), chunk), :] for k in range(wide)]
    head_sum = dot3(split(jnp.concatenate(picked, axis=0)), query, NT)
    core_rows = dim // wide
    tail_rows = width // wide
    span = core_rows // 2
    chunks = cols * width // half
    for k in range(wide):
        ref = own_ref if k == 0 else outs[k - 1]
        take = core_rows if k == 0 else span
        start = (w ^ k) * core_rows if k == 0 else (w ^ k) * core_rows + s * span
        piece = outer[pl.ds(pl.multiple_of(start, take), take), :]
        at = 0
        for i in range(chunks):
            ref[at : at + take, :] = piece[:, i * half : (i + 1) * half]
            at += take
        for i in range(dim // half):
            ref[at : at + chunk, :] = head_sum[k * chunk : (k + 1) * chunk, i * half : (i + 1) * half]
            at += chunk
        ref[at : at + tail_rows, :] = rows_at(tails, w ^ k, tail_rows)


def finish_kernel(wide, cols, scales, tail_ref, x_refs, own_ref, z_refs, swap_refs, head_out, tail_out, core_out, pieces):
    w, t, s = place()
    depth, half = tail_ref.shape
    core_rows = core_out.shape[1]
    span = core_rows // 2
    chunk, dim = head_out.shape
    tail_rows = tail_out.shape[1]
    chunks = cols * depth // half
    each = wide // cols
    for k in range(wide):
        relation = w ^ k

        @pl.when(relation // each == t)
        def _(k=k, at=relation % each):
            for i in range(chunks):
                lanes = slice(i * half, (i + 1) * half)
                if k == 0:
                    pieces[at, :, lanes] = own_ref[i * core_rows : (i + 1) * core_rows, :]
                else:
                    pieces[at, pl.ds(pl.multiple_of(s * span, span), span), lanes] = (
                        z_refs[k - 1][i * span : (i + 1) * span, :]
                    )
                    pieces[at, pl.ds(pl.multiple_of((1 - s) * span, span), span), lanes] = (
                        swap_refs[k - 1][i * span : (i + 1) * span, :]
                    )

    tails = split(jnp.concatenate([tail_ref[...]] + [x[0:depth, :] for x in x_refs], axis=0))
    for i in range(each):
        core_out[i] = dot3(split(pieces[i]), tails, NN) * scales[2]
    for i in range(dim // half):
        at = chunks * core_rows + i * chunk
        total = own_ref[at : at + chunk, :]
        for ref in z_refs:
            at = chunks * span + i * chunk
            total = total + ref[at : at + chunk, :]
        head_out[:, i * half : (i + 1) * half] = total * scales[0]
    at = chunks * core_rows + dim // half * chunk
    total = own_ref[at : at + tail_rows, :]
    for ref in z_refs:
        at = chunks * span + dim // half * chunk
        total = total + ref[at : at + tail_rows, :]
    tail_out[0] = total * scales[1]


def call(kernel, inputs, outputs, scratch=(), scalars=0, flops=0):
    vmem, smem = pl.BlockSpec(memory_space=pltpu.VMEM), pl.BlockSpec(memory_space=pltpu.SMEM)
    return pl.pallas_call(
        kernel,
        out_shape=tuple(jax.ShapeDtypeStruct(shape, F32) for shape in outputs),
        in_specs=[smem] * scalars + [vmem] * (len(inputs) - scalars),
        out_specs=tuple(vmem for _ in outputs),
        scratch_shapes=[pltpu.VMEM(shape, F32) for shape in scratch],
        compiler_params=pltpu.CompilerParams(vmem_limit_bytes=VMEM_LIMIT),
        cost_estimate=pl.CostEstimate(flops=flops, bytes_accessed=4 * sum(x.size for x in inputs), transcendentals=0),
    )(*inputs)


def body(head_embed, tail_embed, core_mats, labels, core_lists):
    wide, cols = lax.axis_size("wide"), lax.axis_size("tail")
    block, dim = head_embed.shape
    depth, half = tail_embed.shape
    slots = core_lists.shape[1]
    rows = block // 2
    chunk = rows // cols
    axes = ("wide", "tail", "sub")

    def move(value, k, offsets=(0, 0), flip=0):
        pairs = []
        for w in range(wide):
            for t in range(cols):
                for s in range(2):
                    target = ((w ^ k) * cols + (t ^ offsets[s])) * 2 + (s ^ flip)
                    pairs.append(((w * cols + t) * 2 + s, target))
        return lax.ppermute(value, axes, pairs)

    order = list(range(wide - 1, 0, -1))
    packed = call(
        functools.partial(pack_kernel, wide, cols),
        (core_lists, labels, head_embed, tail_embed),
        [(block, half + depth)] * (wide - 1) + [(depth + rows + 8, half), (block, dim), (block, depth)],
        scalars=1,
    )
    z_out, x_out, head_own, label_own = packed[: wide - 1], packed[-3], packed[-2], packed[-1]
    z_in, z_swap = {}, {}
    for k in order:
        got = []
        for j in range(max(1, cols // 2)):
            sent = z_out[k - 1] if j == 0 else z_out[k - 1][:, half:]
            got.append(move(sent, k, (2 * j, (2 * j + 1) % cols)))
        z_in[k] = got
    x_in = [move(x_out, 0, (o, o)) for o in range(1, cols)]
    (query,) = call(
        query_kernel, (core_mats, tail_embed, *x_in), [(dim, cols * depth)], flops=6 * dim * half * cols * depth
    )
    query_other = move(query, 0, flip=1)
    for k in order:
        z_swap[k] = [move(value, 0, flip=1) for value in z_in[k]]

    per = len(z_in[1])
    flat_in = [value for k in range(1, wide) for value in z_in[k]]
    flat_swap = [value for k in range(1, wide) for value in z_swap[k]]
    core_rows, tail_rows = dim // wide, depth // wide
    chunks = cols * depth // half
    small = dim // half * chunk + -(-tail_rows // 8) * 8
    send_shape = (chunks * core_rows // 2 + small, half)
    own_shape = (chunks * core_rows + small, half)

    def grads(list_ref, core_ref, query_ref, other_ref, head_ref, label_ref, *rest):
        x_refs, rest = rest[: cols - 1], rest[cols - 1 :]
        count = len(flat_in)
        group = lambda refs: [refs[i : i + per] for i in range(0, count, per)]
        z_refs, swap_refs, rest = group(rest[:count]), group(rest[count : 2 * count]), rest[2 * count :]
        outs, own_ref, scratch = rest[: wide - 1], rest[wide - 1], rest[wide:]
        grad_kernel(
            wide, cols,
            (list_ref, core_ref, query_ref, other_ref, head_ref, label_ref, x_refs, z_refs, swap_refs, outs, own_ref)
            + tuple(scratch),
        )

    made = call(
        grads,
        (core_lists, core_mats, query, query_other, head_own, label_own, *x_in, *flat_in, *flat_swap),
        [send_shape] * (wide - 1) + [own_shape],
        scratch=[(wide * block, dim), (wide * block, cols * depth), (dim, cols * depth), (depth, half)],
        scalars=1,
        flops=6 * wide * block * dim * cols * depth * 2,
    )
    own = made[-1]
    back = {k: move(made[k - 1], k) for k in order}
    back_swap = {k: move(back[k], 0, flip=1) for k in order}
    heads_total, tails_total = block * wide, depth * cols
    scales = (
        1.0 / math.sqrt(slots * tails_total),
        1.0 / math.sqrt(slots * heads_total),
        1.0 / math.sqrt(heads_total * depth),
    )
    each = wide // cols

    def finish(tail_ref, *rest):
        x_refs, rest = rest[: cols - 1], rest[cols - 1 :]
        finish_kernel(
            wide, cols, scales, tail_ref, x_refs, rest[0], rest[1:wide], rest[wide : 2 * wide - 1], *rest[2 * wide - 1 :]
        )

    return call(
        finish,
        (tail_embed, *x_in, own, *[back[k] for k in range(1, wide)], *[back_swap[k] for k in range(1, wide)]),
        [(chunk, dim), (1, tail_rows, half), (each, core_rows, half)],
        scratch=[(each, core_rows, cols * depth)],
        flops=6 * each * core_rows * cols * depth * half,
    )


def solution(mesh):
    in_specs = (
        P(("groups", "wide"), None),
        P(("groups", "tail"), "sub"),
        P(("groups", "wide"), None, "sub"),
        P(("groups", "wide"), None, "tail"),
        P(("groups", "tail"), None),
    )
    out_specs = (
        P(("groups", "wide", "tail", "sub"), None),
        P(("groups", "tail"), "wide", "sub"),
        P(("groups", "tail"), "wide", "sub"),
    )
    return jax.shard_map(body, mesh=mesh, in_specs=in_specs, out_specs=out_specs, check_vma=False)
```

time: 379 us -> 48 us (0.13)
  waiting for transfers between devices: 290 us -> 24.2 us
  matrix products: 54.9 us -> 0 us
  between operations: 19.7 us -> 0.68 us
  starting transfers between devices: 0.43 us -> 14.8 us
  other arithmetic: 7.64 us -> 0 us
  Pallas kernels: 0 us -> 4.74 us
    psum x2 -> x0, waiting for transfers between devices: 178 us -> none  [the longest x1 160 us: broadcast(): return lax.psum(kept, axis)]
    reduce_scatter x4 -> x0, waiting for transfers between devices: 112 us -> none  [the longest x1 58.4 us: body(): lax.psum_scatter(jnp.stack(core_terms), 'wide', scatter_dimension=1, tile...]
    dot_general x49 -> x0, matrix products: 54.9 us -> none  [the longest x8 11.5 us: body(): lax.dot_general(head_embed, weighted, (((0,), (0,)), ((), ())), precision...]
    ppermute x0 -> x14, waiting for transfers between devices: none -> 24.2 us  [move(): return lax.ppermute(value, axes, pairs)]
    ppermute x0 -> x14, starting transfers between devices: none -> 14.8 us  [move(): return lax.ppermute(value, axes, pairs)]
    pallas_call x0 -> x4, Pallas kernels: none -> 4.74 us  [call(): pl.pallas_call(kernel, out_shape=tuple((jax.ShapeDtypeStruct(shape, F32)...]
    mul x3 -> x0, other arithmetic: 4.43 us -> none  [the longest x1 1.67 us: body(): lax.psum_scatter(combined, 'tail', scatter_dimension=0, tiled=True)]
  transfers between devices with their start and end apart: 6 -> 14, of which waited for: 6 -> 9; matrix products, arithmetic and copies ran while one was open for 7% -> 0% of each run, Pallas kernels for 0% -> 0%
where the time goes in v1:
time: 48 us; the launch traced here: 47.8 us
  waiting for transfers between devices  24.2 us (50%)
  starting transfers between devices  14.8 us (31%)
  Pallas kernels  4.74 us (10%)
  local copies, waits for them, and re-layouts  3.41 us (7%)
  between operations  0.68 us (1%)
    ppermute x14, waiting for transfers between devices, move(): return lax.ppermute(value, axes, pairs)  24.2 us
    ppermute x14, starting transfers between devices, move(): return lax.ppermute(value, axes, pairs)  14.8 us
    pallas_call x4, Pallas kernels, call(): pl.pallas_call(kernel, out_shape=tuple((jax.ShapeDtypeStruct(shape, F32)...  4.74 us
    unnamed x12, local copies, waits for them, and re-layouts  3.41 us
  transfers between devices with their start and end apart: 14, of which 9 were waited for; matrix products, arithmetic and copies ran while one was open for 0% of the time, Pallas kernels for 0%

profile of v1, /device:TPU:0, one launch (start us, length us, event | category | flops | bytes accessed | tf_op | source)
XLA Modules:
  0.0 47.8 jit_solution(2870048011914091865)
XLA Ops:
  0.6 0.9 %copy-done.1 = f32[128,256]{1,0:T(8,128)S(1)} copy-done((f32[128,256]{1,0:T(8,128)S(1)}, f32[128,256]{1,0:T(8,128)}, u32[]{:S(2)}) %copy-start.1) | copy-done | bytes 131096
  1.5 0.9 %copy-done.3 = s32[64,8,128]{2,1,0:T(8,128)S(1)} copy-done((s32[64,8,128]{2,1,0:T(8,128)S(1)}, s32[64,8,128]{2,1,0:T(8,128)}, u32[]{:S(2)}) %copy-start.3) | copy-done | bytes 262168
  2.5 0.9 %copy-done.4 = f32[64,512]{1,0:T(8,128)S(1)} copy-done((f32[64,512]{1,0:T(8,128)S(1)}, f32[64,512]{1,0:T(8,128)}, u32[]{:S(2)}) %copy-start.4) | copy-done | bytes 131096
  3.4 0.7 %copy-done.5 = s32[1,8]{1,0:T(1,128)S(1)} copy-done((s32[1,8]{1,0:T(1,128)S(1)}, s32[1,8]{1,0:T(1,128)}, u32[]{:S(2)}) %copy-start.5) | copy-done | bytes 56
  4.1 1.3 %shard_map.76 = (f32[64,384]{1,0:T(8,128)S(1)}, f32[64,384]{1,0:T(8,128)S(1)}, f32[64,384]{1,0:T(8,128)S(1)}, f32[168,256]{1,0:T(8,128)S(1)}, f32[64,512]{1,0:T(8,128)S(1)}, /*index=5*/f32[64,128]{1,0:T(8,128)S(1)}) custom-call(s32[1,8]{1,0:T(1,128)S(1)} %copy-done.5, s32[64,8,128]{2,1,0:T(8,128)S(1)} %copy-done.3, f32[64,512]{1,0:T(8,128)S(1)} %copy-done.4, ...), custom_call_target="tpu_custom_call" | custom-call | bytes 524320 | tf_op jit(solution)/shard_map/pallas_call | solution.py:202
  5.3 3.0 %collective-permute-start = (f32[168,256]{1,0:T(8,128)S(1)}, f32[168,256]{1,0:T(8,128)S(1)}, u32[]{:S(2)}, u32[]{:S(2)}) collective-permute-start(f32[168,256]{1,0:T(8,128)S(1)} %get-tuple-element.13), channel_id=1, source_target_pairs={{0,2},{1,3},{2,0},{3,1},{4,6},{5,7},{6,4},{7,5},{8,10},{9,11},{10,... | collective-permute-start | bytes 516104 | tf_op jit(solution)/shard_map/ppermute | solution.py:229
  8.3 4.4 %collective-permute-done.refs_0_.rest_0_ = f32[168,256]{1,0:T(8,128)S(1)} collective-permute-done((f32[168,256]{1,0:T(8,128)S(1)}, f32[168,256]{1,0:T(8,128)S(1)}, u32[]{:S(2)}, u32[]{:S(2)}) %collective-permute-start) | collective-permute-done | bytes 172064 | tf_op jit(solution)/shard_map/ppermute | solution.py:229
  12.7 0.4 shard_map.77.query_ref
  13.2 1.9 %collective-permute-start.2 = (f32[64,384]{1,0:T(8,128)S(1)}, f32[64,384]{1,0:T(8,128)S(1)}, u32[]{:S(2)}, u32[]{:S(2)}) collective-permute-start(f32[64,384]{1,0:T(8,128)S(1)} %get-tuple-element.16), channel_id=1, source_target_pairs={{0,4},{1,7},{2,6},{3,5},{4,0},{5,3},{6,2},{7,1},{8,12},{9,15},{10,... | collective-permute-start | bytes 294920 | tf_op jit(solution)/shard_map/ppermute | solution.py:229
  15.1 2.6 %collective-permute-start.3 = (f32[64,384]{1,0:T(8,128)S(1)}, f32[64,384]{1,0:T(8,128)S(1)}, u32[]{:S(2)}, u32[]{:S(2)}) collective-permute-start(f32[64,384]{1,0:T(8,128)S(1)} %get-tuple-element.17), channel_id=1, source_target_pairs={{0,8},{1,11},{2,10},{3,9},{4,12},{5,15},{6,14},{7,13},{8,0},{9,3},... | collective-permute-start | bytes 294920 | tf_op jit(solution)/shard_map/ppermute | solution.py:229
  17.7 0.7 %collective-permute-done.2.rest_1_ = f32[64,384]{1,0:T(8,128)S(1)} collective-permute-done((f32[64,384]{1,0:T(8,128)S(1)}, f32[64,384]{1,0:T(8,128)S(1)}, u32[]{:S(2)}, u32[]{:S(2)}) %collective-permute-start.2) | collective-permute-done | bytes 98336 | tf_op jit(solution)/shard_map/ppermute | solution.py:229
  18.3 1.0 %collective-permute-start.5 = (f32[64,384]{1,0:T(8,128)S(1)}, f32[64,384]{1,0:T(8,128)S(1)}, u32[]{:S(2)}, u32[]{:S(2)}) collective-permute-start(f32[64,384]{1,0:T(8,128)S(1)} %collective-permute-done.2.rest_1_), channel_id=1, source_target_pairs={{0,1},{1,0},{2,3},{3,2},{4,5},{5,4},{6,7},{7,6},{8,9},{9,8},{10,11... | collective-permute-start | bytes 294920 | tf_op jit(solution)/shard_map/ppermute | solution.py:229
  19.3 6.5 %collective-permute-done.3.rest_2_ = f32[64,384]{1,0:T(8,128)S(1)} collective-permute-done((f32[64,384]{1,0:T(8,128)S(1)}, f32[64,384]{1,0:T(8,128)S(1)}, u32[]{:S(2)}, u32[]{:S(2)}) %collective-permute-start.3) | collective-permute-done | bytes 98336 | tf_op jit(solution)/shard_map/ppermute | solution.py:229
  25.8 0.9 %collective-permute-start.6 = (f32[64,384]{1,0:T(8,128)S(1)}, f32[64,384]{1,0:T(8,128)S(1)}, u32[]{:S(2)}, u32[]{:S(2)}) collective-permute-start(f32[64,384]{1,0:T(8,128)S(1)} %collective-permute-done.3.rest_2_), channel_id=1, source_target_pairs={{0,1},{1,0},{2,3},{3,2},{4,5},{5,4},{6,7},{7,6},{8,9},{9,8},{10,11... | collective-permute-start | bytes 294920 | tf_op jit(solution)/shard_map/ppermute | solution.py:229
  26.7 0.9 %collective-permute-done.6.rest_5_ = f32[64,384]{1,0:T(8,128)S(1)} collective-permute-done((f32[64,384]{1,0:T(8,128)S(1)}, f32[64,384]{1,0:T(8,128)S(1)}, u32[]{:S(2)}, u32[]{:S(2)}) %collective-permute-start.6) | collective-permute-done | bytes 98336 | tf_op jit(solution)/shard_map/ppermute | solution.py:229
  28.0 2.0 %shard_map.78 = (f32[128,256]{1,0:T(8,128)S(1)}, f32[128,256]{1,0:T(8,128)S(1)}, f32[128,256]{1,0:T(8,128)S(1)}, f32[192,256]{1,0:T(8,128)S(1)}) custom-call(s32[1,8]{1,0:T(1,128)S(1)} %copy-done.5, f32[1,512,256]{2,1,0:T(8,128)S(1)} %copy-done, f32[512,256]{1,0:T(8,128)S(1)} %shard_map.77.query_ref, f32[512,256]{1,0:T(8,128)S(1)} %collective-permute-done.1.other_ref, ...), custom_call_target="tpu_custom_call" | custom-call | flops 402653184 | bytes 2498592 | tf_op jit(solution)/shard_map/pallas_call | solution.py:202
  30.0 2.3 %collective-permute-start.8 = (f32[128,256]{1,0:T(8,128)S(1)}, f32[128,256]{1,0:T(8,128)S(1)}, u32[]{:S(2)}, u32[]{:S(2)}) collective-permute-start(f32[128,256]{1,0:T(8,128)S(1)} %get-tuple-element.20), channel_id=1, source_target_pairs={{0,4},{1,5},{2,6},{3,7},{4,0},{5,1},{6,2},{7,3},{8,12},{9,13},{10,... | collective-permute-start | bytes 393224 | tf_op jit(solution)/shard_map/ppermute | solution.py:229
  32.4 1.1 %collective-permute-start.9 = (f32[128,256]{1,0:T(8,128)S(1)}, f32[128,256]{1,0:T(8,128)S(1)}, u32[]{:S(2)}, u32[]{:S(2)}) collective-permute-start(f32[128,256]{1,0:T(8,128)S(1)} %get-tuple-element.21), channel_id=1, source_target_pairs={{0,8},{1,9},{2,10},{3,11},{4,12},{5,13},{6,14},{7,15},{8,0},{9,1},... | collective-permute-start | bytes 393224 | tf_op jit(solution)/shard_map/ppermute | solution.py:229
  33.5 1.4 %collective-permute-start.10 = (f32[128,256]{1,0:T(8,128)S(1)}, f32[128,256]{1,0:T(8,128)S(1)}, u32[]{:S(2)}, u32[]{:S(2)}) collective-permute-start(f32[128,256]{1,0:T(8,128)S(1)} %get-tuple-element.22), channel_id=1, source_target_pairs={{0,12},{1,13},{2,14},{3,15},{4,8},{5,9},{6,10},{7,11},{8,4},{9,5},... | collective-permute-start | bytes 393224 | tf_op jit(solution)/shard_map/ppermute | solution.py:229
  34.9 3.6 %collective-permute-done.8.rest_2_ = f32[128,256]{1,0:T(8,128)S(1)} collective-permute-done((f32[128,256]{1,0:T(8,128)S(1)}, f32[128,256]{1,0:T(8,128)S(1)}, u32[]{:S(2)}, u32[]{:S(2)}) %collective-permute-start.8) | collective-permute-done | bytes 131104 | tf_op jit(solution)/shard_map/ppermute | solution.py:229
  38.5 6.8 %collective-permute-done.9.rest_3_ = f32[128,256]{1,0:T(8,128)S(1)} collective-permute-done((f32[128,256]{1,0:T(8,128)S(1)}, f32[128,256]{1,0:T(8,128)S(1)}, u32[]{:S(2)}, u32[]{:S(2)}) %collective-permute-start.9) | collective-permute-done | bytes 131104 | tf_op jit(solution)/shard_map/ppermute | solution.py:229
  45.3 0.5 %collective-permute-start.13 = (f32[128,256]{1,0:T(8,128)S(1)}, f32[128,256]{1,0:T(8,128)S(1)}, u32[]{:S(2)}, u32[]{:S(2)}) collective-permute-start(f32[128,256]{1,0:T(8,128)S(1)} %collective-permute-done.10.rest_4_), channel_id=1, source_target_pairs={{0,1},{1,0},{2,3},{3,2},{4,5},{5,4},{6,7},{7,6},{8,9},{9,8},{10,11... | collective-permute-start | bytes 393224 | tf_op jit(solution)/shard_map/ppermute | solution.py:229
  45.8 0.8 %collective-permute-done.12.rest_6_ = f32[128,256]{1,0:T(8,128)S(1)} collective-permute-done((f32[128,256]{1,0:T(8,128)S(1)}, f32[128,256]{1,0:T(8,128)S(1)}, u32[]{:S(2)}, u32[]{:S(2)}) %collective-permute-start.12) | collective-permute-done | bytes 131104 | tf_op jit(solution)/shard_map/ppermute | solution.py:229
  46.8 1.0 %shard_map.79 = (f32[16,512]{1,0:T(8,128)}, f32[1,32,256]{2,1,0:T(8,128)}, f32[2,128,256]{2,1,0:T(8,128)}) custom-call(f32[128,256]{1,0:T(8,128)S(1)} %copy-done.2, f32[168,256]{1,0:T(8,128)S(1)} %collective-permute-done.refs_0_.rest_0_, f32[192,256]{1,0:T(8,128)S(1)} %get-tuple-element.19.rest_1_, f32[128,256]{1,0:T(8,128)S(1)} %collective-permute-done.8.rest_2_, ...), custom_call_target="tpu_custom_call" | custom-call | flops 100663296 | bytes 1286144 | tf_op jit(solution)/shard_map/pallas_call | solution.py:202
  (20 shorter events, 0.7 us)
Async XLA Ops:
  0.6 0.9 %copy-start.1 = (f32[128,256]{1,0:T(8,128)S(1)}, f32[128,256]{1,0:T(8,128)}, u32[]{:S(2)}) copy-start(f32[128,256]{1,0:T(8,128)} %tail_ref.5) | copy-start | bytes 393220
  1.5 0.9 %copy-start.3 = (s32[64,8,128]{2,1,0:T(8,128)S(1)}, s32[64,8,128]{2,1,0:T(8,128)}, u32[]{:S(2)}) copy-start(s32[64,8,128]{2,1,0:T(8,128)} %label_ref.1) | copy-start | bytes 786436
  2.5 0.9 %copy-start.4 = (f32[64,512]{1,0:T(8,128)S(1)}, f32[64,512]{1,0:T(8,128)}, u32[]{:S(2)}) copy-start(f32[64,512]{1,0:T(8,128)} %head_ref.1) | copy-start | bytes 393220
  3.4 0.7 %copy-start.5 = (s32[1,8]{1,0:T(1,128)S(1)}, s32[1,8]{1,0:T(1,128)}, u32[]{:S(2)}) copy-start(s32[1,8]{1,0:T(1,128)} %list_ref.3) | copy-start | bytes 100
  4.0 8.6 %copy-start = (f32[1,512,256]{2,1,0:T(8,128)S(1)}, f32[1,512,256]{2,1,0:T(8,128)}, u32[]{:S(2)}) copy-start(f32[1,512,256]{2,1,0:T(8,128)} %core_ref.3) | copy-start | bytes 1572868
  5.3 7.4 %collective-permute-start = (f32[168,256]{1,0:T(8,128)S(1)}, f32[168,256]{1,0:T(8,128)S(1)}, u32[]{:S(2)}, u32[]{:S(2)}) collective-permute-start(f32[168,256]{1,0:T(8,128)S(1)} %get-tuple-element.13), channel_id=1, source_target_pairs={{0,2},{1,3},{2,0},{3,1},{4,6},{5,7},{6,4},{7,5},{8,10},{9,11},{10,... | collective-permute-start | bytes 516104 | tf_op jit(solution)/shard_map/ppermute | solution.py:229
  13.1 14.9 %collective-permute-start.1 = (f32[512,256]{1,0:T(8,128)S(1)}, f32[512,256]{1,0:T(8,128)S(1)}, u32[]{:S(2)}, u32[]{:S(2)}) collective-permute-start(f32[512,256]{1,0:T(8,128)S(1)} %shard_map.77.query_ref), channel_id=1, source_target_pairs={{0,1},{1,0},{2,3},{3,2},{4,5},{5,4},{6,7},{7,6},{8,9},{9,8},{10,11... | collective-permute-start | bytes 1572872 | tf_op jit(solution)/shard_map/ppermute | solution.py:229
  13.2 5.1 %collective-permute-start.2 = (f32[64,384]{1,0:T(8,128)S(1)}, f32[64,384]{1,0:T(8,128)S(1)}, u32[]{:S(2)}, u32[]{:S(2)}) collective-permute-start(f32[64,384]{1,0:T(8,128)S(1)} %get-tuple-element.16), channel_id=1, source_target_pairs={{0,4},{1,7},{2,6},{3,5},{4,0},{5,3},{6,2},{7,1},{8,12},{9,15},{10,... | collective-permute-start | bytes 294920 | tf_op jit(solution)/shard_map/ppermute | solution.py:229
  15.1 10.7 %collective-permute-start.3 = (f32[64,384]{1,0:T(8,128)S(1)}, f32[64,384]{1,0:T(8,128)S(1)}, u32[]{:S(2)}, u32[]{:S(2)}) collective-permute-start(f32[64,384]{1,0:T(8,128)S(1)} %get-tuple-element.17), channel_id=1, source_target_pairs={{0,8},{1,11},{2,10},{3,9},{4,12},{5,15},{6,14},{7,13},{8,0},{9,3},... | collective-permute-start | bytes 294920 | tf_op jit(solution)/shard_map/ppermute | solution.py:229
  17.7 9.0 %collective-permute-start.4 = (f32[64,384]{1,0:T(8,128)S(1)}, f32[64,384]{1,0:T(8,128)S(1)}, u32[]{:S(2)}, u32[]{:S(2)}) collective-permute-start(f32[64,384]{1,0:T(8,128)S(1)} %get-tuple-element.18), channel_id=1, source_target_pairs={{0,12},{1,15},{2,14},{3,13},{4,8},{5,11},{6,10},{7,9},{8,4},{9,7},... | collective-permute-start | bytes 294920 | tf_op jit(solution)/shard_map/ppermute | solution.py:229
  18.3 8.4 %collective-permute-start.5 = (f32[64,384]{1,0:T(8,128)S(1)}, f32[64,384]{1,0:T(8,128)S(1)}, u32[]{:S(2)}, u32[]{:S(2)}) collective-permute-start(f32[64,384]{1,0:T(8,128)S(1)} %collective-permute-done.2.rest_1_), channel_id=1, source_target_pairs={{0,1},{1,0},{2,3},{3,2},{4,5},{5,4},{6,7},{7,6},{8,9},{9,8},{10,11... | collective-permute-start | bytes 294920 | tf_op jit(solution)/shard_map/ppermute | solution.py:229
  25.8 1.9 %collective-permute-start.6 = (f32[64,384]{1,0:T(8,128)S(1)}, f32[64,384]{1,0:T(8,128)S(1)}, u32[]{:S(2)}, u32[]{:S(2)}) collective-permute-start(f32[64,384]{1,0:T(8,128)S(1)} %collective-permute-done.3.rest_2_), channel_id=1, source_target_pairs={{0,1},{1,0},{2,3},{3,2},{4,5},{5,4},{6,7},{7,6},{8,9},{9,8},{10,11... | collective-permute-start | bytes 294920 | tf_op jit(solution)/shard_map/ppermute | solution.py:229
  26.7 1.3 %collective-permute-start.7 = (f32[64,384]{1,0:T(8,128)S(1)}, f32[64,384]{1,0:T(8,128)S(1)}, u32[]{:S(2)}, u32[]{:S(2)}) collective-permute-start(f32[64,384]{1,0:T(8,128)S(1)} %collective-permute-done.4.rest_3_), channel_id=1, source_target_pairs={{0,1},{1,0},{2,3},{3,2},{4,5},{5,4},{6,7},{7,6},{8,9},{9,8},{10,11... | collective-permute-start | bytes 294920 | tf_op jit(solution)/shard_map/ppermute | solution.py:229
  28.0 18.8 %copy-start.2 = (f32[128,256]{1,0:T(8,128)S(1)}, f32[128,256]{1,0:T(8,128)}, u32[]{:S(2)}) copy-start(f32[128,256]{1,0:T(8,128)} %tail_ref.5) | copy-start | bytes 393220
  30.0 8.4 %collective-permute-start.8 = (f32[128,256]{1,0:T(8,128)S(1)}, f32[128,256]{1,0:T(8,128)S(1)}, u32[]{:S(2)}, u32[]{:S(2)}) collective-permute-start(f32[128,256]{1,0:T(8,128)S(1)} %get-tuple-element.20), channel_id=1, source_target_pairs={{0,4},{1,5},{2,6},{3,7},{4,0},{5,1},{6,2},{7,3},{8,12},{9,13},{10,... | collective-permute-start | bytes 393224 | tf_op jit(solution)/shard_map/ppermute | solution.py:229
  32.4 12.9 %collective-permute-start.9 = (f32[128,256]{1,0:T(8,128)S(1)}, f32[128,256]{1,0:T(8,128)S(1)}, u32[]{:S(2)}, u32[]{:S(2)}) collective-permute-start(f32[128,256]{1,0:T(8,128)S(1)} %get-tuple-element.21), channel_id=1, source_target_pairs={{0,8},{1,9},{2,10},{3,11},{4,12},{5,13},{6,14},{7,15},{8,0},{9,1},... | collective-permute-start | bytes 393224 | tf_op jit(solution)/shard_map/ppermute | solution.py:229
  33.5 11.8 %collective-permute-start.10 = (f32[128,256]{1,0:T(8,128)S(1)}, f32[128,256]{1,0:T(8,128)S(1)}, u32[]{:S(2)}, u32[]{:S(2)}) collective-permute-start(f32[128,256]{1,0:T(8,128)S(1)} %get-tuple-element.22), channel_id=1, source_target_pairs={{0,12},{1,13},{2,14},{3,15},{4,8},{5,9},{6,10},{7,11},{8,4},{9,5},... | collective-permute-start | bytes 393224 | tf_op jit(solution)/shard_map/ppermute | solution.py:229
  38.5 7.3 %collective-permute-start.11 = (f32[128,256]{1,0:T(8,128)S(1)}, f32[128,256]{1,0:T(8,128)S(1)}, u32[]{:S(2)}, u32[]{:S(2)}) collective-permute-start(f32[128,256]{1,0:T(8,128)S(1)} %collective-permute-done.8.rest_2_), channel_id=1, source_target_pairs={{0,1},{1,0},{2,3},{3,2},{4,5},{5,4},{6,7},{7,6},{8,9},{9,8},{10,11... | collective-permute-start | bytes 393224 | tf_op jit(solution)/shard_map/ppermute | solution.py:229
  45.3 1.3 %collective-permute-start.12 = (f32[128,256]{1,0:T(8,128)S(1)}, f32[128,256]{1,0:T(8,128)S(1)}, u32[]{:S(2)}, u32[]{:S(2)}) collective-permute-start(f32[128,256]{1,0:T(8,128)S(1)} %collective-permute-done.9.rest_3_), channel_id=1, source_target_pairs={{0,1},{1,0},{2,3},{3,2},{4,5},{5,4},{6,7},{7,6},{8,9},{9,8},{10,11... | collective-permute-start | bytes 393224 | tf_op jit(solution)/shard_map/ppermute | solution.py:229
  45.3 1.5 %collective-permute-start.13 = (f32[128,256]{1,0:T(8,128)S(1)}, f32[128,256]{1,0:T(8,128)S(1)}, u32[]{:S(2)}, u32[]{:S(2)}) collective-permute-start(f32[128,256]{1,0:T(8,128)S(1)} %collective-permute-done.10.rest_4_), channel_id=1, source_target_pairs={{0,1},{1,0},{2,3},{3,2},{4,5},{5,4},{6,7},{7,6},{8,9},{9,8},{10,11... | collective-permute-start | bytes 393224 | tf_op jit(solution)/shard_map/ppermute | solution.py:229

commit v2 on v1

--- a/solution.py
+++ b/solution.py
@@ -11,6 +11,8 @@
 
 F32 = jnp.float32
 VMEM_LIMIT = 48 * 1024 * 1024
+QUERY_PARTS = 4
+FULL_LIMIT = 62 * 1024 * 1024
 NN = (((1,), (0,)), ((), ()))
 NT = (((1,), (1,)), ((), ()))
 TN = (((0,), (0,)), ((), ()))
@@ -44,13 +46,29 @@
     return lax.axis_index("wide"), lax.axis_index("tail"), lax.axis_index("sub")
 
 
-def pack_kernel(wide, cols, list_ref, label_ref, head_ref, tail_ref, *outs):
-    z_refs, x_ref, head_own, label_own = outs[: wide - 1], outs[-3], outs[-2], outs[-1]
+def pack_kernel(wide, cols, list_hbm, label_hbm, head_hbm, tail_hbm, *refs):
+    z_refs, (x_ref, head_own, label_own, listed, label_ref, head_ref, sems) = refs[: wide - 1], refs[wide - 1 :]
     w, t, s = place()
     block, slots, width = label_ref.shape
     chunk = block // (2 * cols)
     rows = block // 2
-    half = tail_ref.shape[1]
+    depth, half = tail_hbm.shape
+    copies = [
+        pltpu.make_async_copy(source, target, sems.at[i])
+        for i, (source, target) in enumerate(
+            ((list_hbm, listed), (label_hbm, label_ref), (head_hbm, head_ref), (tail_hbm, x_ref.at[0:depth]))
+        )
+    ]
+    for copy in copies:
+        copy.start()
+    copies[0].wait()
+    count = jnp.int32(0)
+    for j in range(slots):
+        count = count + (listed[0, j] == w).astype(jnp.int32)
+    x_ref[depth + rows :, :] = jnp.full((8, half), count.astype(F32), F32)
+    label_own[block:, :] = jnp.full((8, width), count.astype(F32), F32)
+    copies[1].wait()
+    copies[2].wait()
     for part in range(2):
         for col in range(cols):
             start = pl.multiple_of((col * 2 + (s ^ part)) * chunk, chunk)
@@ -61,34 +79,33 @@
             for k in range(wide):
                 total = jnp.zeros((chunk, width), jnp.int32)
                 for j in range(slots):
-                    total = total + jnp.where(list_ref[0, j] == (w ^ k), slot_labels[j], 0)
+                    total = total + jnp.where(listed[0, j] == (w ^ k), slot_labels[j], 0)
                 total = total.astype(F32)
                 if k == 0:
                     label_own[at : at + chunk, :] = total
                     lane = (at // rows) * width
-                    row = tail_ref.shape[0] + at % rows
+                    row = depth + at % rows
                     x_ref[row : row + chunk, lane : lane + width] = total
                 else:
                     z_refs[k - 1][at : at + chunk, half : half + width] = total
                     if part == 0:
                         z_refs[k - 1][at : at + chunk, 0:half] = embed[:, 0:half]
                         z_refs[k - 1][rows + at : rows + at + chunk, 0:half] = embed[:, half:]
-    x_ref[0 : tail_ref.shape[0], :] = tail_ref[...]
-    count = jnp.int32(0)
-    for j in range(slots):
-        count = count + (list_ref[0, j] == w).astype(jnp.int32)
-    x_ref[tail_ref.shape[0] + rows :, :] = jnp.full((8, half), count.astype(F32), F32)
+    copies[3].wait()
 
 
 def query_kernel(core_ref, tail_ref, *refs):
-    x_refs, out_ref = refs[:-1], refs[-1]
+    x_refs, outs = refs[: -1 - QUERY_PARTS], refs[-QUERY_PARTS:]
     depth = tail_ref.shape[0]
     tails = [tail_ref[...]] + [x[0:depth, :] for x in x_refs]
-    out_ref[...] = dot3(split(core_ref[0]), split(jnp.concatenate(tails, axis=0)), NT)
+    value = dot3(split(core_ref[0]), split(jnp.concatenate(tails, axis=0)), NT)
+    size = outs[0].shape[0]
+    for i, ref in enumerate(outs):
+        ref[...] = value[i * size : (i + 1) * size]
 
 
 def grad_kernel(wide, cols, refs):
-    (list_ref, core_ref, query_ref, query_other, head_own, label_own, x_refs, z_refs, swap_refs, outs, own_ref,
+    (core_ref, query_refs, query_others, head_own, label_own, x_refs, z_refs, swap_refs, outs, own_ref,
      heads, resid, outer, tails) = refs
     w, t, s = place()
     block, dim = head_own.shape
@@ -102,19 +119,16 @@
         for part, ref in enumerate((z_refs[k - 1][0], swap_refs[k - 1][0])):
             heads[at + part * rows : at + part * rows + rows, 0:half] = ref[0:rows, 0:half]
             heads[at + part * rows : at + part * rows + rows, half:] = ref[rows:, 0:half]
-    query = split(query_ref[...] + query_other[...])
+    query = split(jnp.concatenate([a[...] + b[...] for a, b in zip(query_refs, query_others)], axis=0))
     head_parts = split(heads[...])
     score = dot3(head_parts, query, NN)
     prob = jax.nn.sigmoid(score)
-    count = jnp.int32(0)
-    for j in range(list_ref.shape[1]):
-        count = count + (list_ref[0, j] == w).astype(jnp.int32)
     depth = x_refs[0].shape[0] - 8 - rows if x_refs else 0
     for o in range(cols):
         lanes = slice(o * width, (o + 1) * width)
-        times = count.astype(F32) if o == 0 else x_refs[o - 1][depth + rows : depth + rows + 1, 0:width]
+        times = label_own[block : block + 1, :] if o == 0 else x_refs[o - 1][depth + rows : depth + rows + 1, 0:width]
         if o == 0:
-            resid[0:block, lanes] = times * prob[0:block, lanes] - label_own[...]
+            resid[0:block, lanes] = times * prob[0:block, lanes] - label_own[0:block, :]
         else:
             ref = x_refs[o - 1]
             for part in range(2):
@@ -197,15 +211,15 @@
     tail_out[0] = total * scales[1]
 
 
-def call(kernel, inputs, outputs, scratch=(), scalars=0, flops=0):
-    vmem, smem = pl.BlockSpec(memory_space=pltpu.VMEM), pl.BlockSpec(memory_space=pltpu.SMEM)
+def call(kernel, inputs, outputs, scratch=(), hbm=(), flops=0, limit=VMEM_LIMIT):
+    vmem, far = pl.BlockSpec(memory_space=pltpu.VMEM), pl.BlockSpec(memory_space=pltpu.HBM)
     return pl.pallas_call(
         kernel,
         out_shape=tuple(jax.ShapeDtypeStruct(shape, F32) for shape in outputs),
-        in_specs=[smem] * scalars + [vmem] * (len(inputs) - scalars),
+        in_specs=[far if i in hbm else vmem for i in range(len(inputs))],
         out_specs=tuple(vmem for _ in outputs),
-        scratch_shapes=[pltpu.VMEM(shape, F32) for shape in scratch],
-        compiler_params=pltpu.CompilerParams(vmem_limit_bytes=VMEM_LIMIT),
+        scratch_shapes=[pltpu.VMEM(item, F32) if isinstance(item, tuple) else item for item in scratch],
+        compiler_params=pltpu.CompilerParams(vmem_limit_bytes=limit),
         cost_estimate=pl.CostEstimate(flops=flops, bytes_accessed=4 * sum(x.size for x in inputs), transcendentals=0),
     )(*inputs)
 
@@ -232,8 +246,15 @@
     packed = call(
         functools.partial(pack_kernel, wide, cols),
         (core_lists, labels, head_embed, tail_embed),
-        [(block, half + depth)] * (wide - 1) + [(depth + rows + 8, half), (block, dim), (block, depth)],
-        scalars=1,
+        [(block, half + depth)] * (wide - 1) + [(depth + rows + 8, half), (block, dim), (block + 8, depth)],
+        scratch=[
+            pltpu.SMEM(core_lists.shape, jnp.int32),
+            pltpu.VMEM(labels.shape, jnp.int32),
+            head_embed.shape,
+            pltpu.SemaphoreType.DMA((4,)),
+        ],
+        hbm=range(4),
+        limit=FULL_LIMIT,
     )
     z_out, x_out, head_own, label_own = packed[: wide - 1], packed[-3], packed[-2], packed[-1]
     z_in, z_swap = {}, {}
@@ -244,10 +265,14 @@
             got.append(move(sent, k, (2 * j, (2 * j + 1) % cols)))
         z_in[k] = got
     x_in = [move(x_out, 0, (o, o)) for o in range(1, cols)]
-    (query,) = call(
-        query_kernel, (core_mats, tail_embed, *x_in), [(dim, cols * depth)], flops=6 * dim * half * cols * depth
-    )
-    query_other = move(query, 0, flip=1)
+    query = call(
+        query_kernel,
+        (core_mats, tail_embed, *x_in, z_in[order[0]][0]),
+        [(dim // QUERY_PARTS, cols * depth)] * QUERY_PARTS,
+        hbm=(cols + 1,),
+        flops=6 * dim * half * cols * depth,
+    )
+    query_other = [move(value, 0, flip=1) for value in query]
     for k in order:
         z_swap[k] = [move(value, 0, flip=1) for value in z_in[k]]
 
@@ -260,7 +285,9 @@
     send_shape = (chunks * core_rows // 2 + small, half)
     own_shape = (chunks * core_rows + small, half)
 
-    def grads(list_ref, core_ref, query_ref, other_ref, head_ref, label_ref, *rest):
+    def grads(core_ref, *rest):
+        query_refs, other_refs, rest = rest[:QUERY_PARTS], rest[QUERY_PARTS : 2 * QUERY_PARTS], rest[2 * QUERY_PARTS :]
+        head_ref, label_ref, *rest = rest
         x_refs, rest = rest[: cols - 1], rest[cols - 1 :]
         count = len(flat_in)
         group = lambda refs: [refs[i : i + per] for i in range(0, count, per)]
@@ -268,16 +295,15 @@
         outs, own_ref, scratch = rest[: wide - 1], rest[wide - 1], rest[wide:]
         grad_kernel(
             wide, cols,
-            (list_ref, core_ref, query_ref, other_ref, head_ref, label_ref, x_refs, z_refs, swap_refs, outs, own_ref)
+            (core_ref, query_refs, other_refs, head_ref, label_ref, x_refs, z_refs, swap_refs, outs, own_ref)
             + tuple(scratch),
         )
 
     made = call(
         grads,
-        (core_lists, core_mats, query, query_other, head_own, label_own, *x_in, *flat_in, *flat_swap),
+        (core_mats, *query, *query_other, head_own, label_own, *x_in, *flat_in, *flat_swap),
         [send_shape] * (wide - 1) + [own_shape],
         scratch=[(wide * block, dim), (wide * block, cols * depth), (dim, cols * depth), (depth, half)],
-        scalars=1,
         flops=6 * wide * block * dim * cols * depth * 2,
     )
     own = made[-1]

time: 48 us -> 38.4 us (0.80)
  waiting for transfers between devices: 24.2 us -> 17.3 us
  local copies, waits for them, and re-layouts: 3.41 us -> 0.92 us
  starting transfers between devices: 14.8 us -> 13.9 us
  Pallas kernels: 4.74 us -> 5.46 us
    ppermute x14 -> x17, waiting for transfers between devices: 24.2 us -> 17.3 us  [move(): return lax.ppermute(value, axes, pairs)]
    unnamed x12 -> x10, local copies, waits for them, and re-layouts: 3.41 us -> 0.92 us
    ppermute x14 -> x17, starting transfers between devices: 14.8 us -> 13.9 us  [move(): return lax.ppermute(value, axes, pairs)]
    pallas_call x4, Pallas kernels: 4.74 us -> 5.46 us  [call(): pl.pallas_call(kernel, out_shape=tuple((jax.ShapeDtypeStruct(shape, F32)...]
  transfers between devices with their start and end apart: 14 -> 17, of which waited for: 9 -> 8; matrix products, arithmetic and copies ran while one was open for 0% -> 0% of each run, Pallas kernels for 0% -> 1%
where the time goes in v2:
time: 38.4 us; the launch traced here: 38.3 us
  waiting for transfers between devices  17.3 us (45%)
  starting transfers between devices  13.9 us (36%)
  Pallas kernels  5.46 us (14%)
  local copies, waits for them, and re-layouts  0.92 us (2%)
  between operations  0.72 us (2%)
    ppermute x17, waiting for transfers between devices, move(): return lax.ppermute(value, axes, pairs)  17.3 us
    ppermute x17, starting transfers between devices, move(): return lax.ppermute(value, axes, pairs)  13.9 us
    pallas_call x4, Pallas kernels, call(): pl.pallas_call(kernel, out_shape=tuple((jax.ShapeDtypeStruct(shape, F32)...  5.46 us
    unnamed x10, local copies, waits for them, and re-layouts  0.92 us
  transfers between devices with their start and end apart: 17, of which 8 were waited for; matrix products, arithmetic and copies ran while one was open for 0% of the time, Pallas kernels for 1%

profile of v2, /device:TPU:0, one launch (start us, length us, event | category | flops | bytes accessed | tf_op | source)
XLA Modules:
  0.0 38.3 jit_solution(16590586208228111503)
XLA Ops:
  0.6 2.5 %shard_map.76 = (f32[64,384]{1,0:T(8,128)}, f32[64,384]{1,0:T(8,128)}, f32[64,384]{1,0:T(8,128)}, f32[168,256]{1,0:T(8,128)}, f32[64,512]{1,0:T(8,128)}, /*index=5*/f32[72,128]{1,0:T(8,128)}) custom-call(s32[1,8]{1,0:T(1,128)} %list_hbm.1, s32[64,8,128]{2,1,0:T(8,128)} %label_hbm.1, f32[64,512]{1,0:T(8,128)} %head_hbm.1, f32[128,256]{1,0:T(8,128)} %tail_ref.3), custom_call_target="tpu_custom_call" | custom-call | bytes 524320 | tf_op jit(solution)/shard_map/pallas_call | solution.py:216
  3.2 5.1 %collective-permute-start.1 = (f32[64,384]{1,0:T(8,128)}, f32[64,384]{1,0:T(8,128)S(1)}, u32[]{:S(2)}, u32[]{:S(2)}) collective-permute-start(f32[64,384]{1,0:T(8,128)} %get-tuple-element.18), channel_id=1, source_target_pairs={{0,12},{1,15},{2,14},{3,13},{4,8},{5,11},{6,10},{7,9},{8,4},{9,7},... | collective-permute-start | bytes 294920 | tf_op jit(solution)/shard_map/ppermute | solution.py:243
  8.3 1.5 %collective-permute-start = (f32[168,256]{1,0:T(8,128)}, f32[168,256]{1,0:T(8,128)S(1)}, u32[]{:S(2)}, u32[]{:S(2)}) collective-permute-start(f32[168,256]{1,0:T(8,128)} %get-tuple-element.17), channel_id=1, source_target_pairs={{0,2},{1,3},{2,0},{3,1},{4,6},{5,7},{6,4},{7,5},{8,10},{9,11},{10,... | collective-permute-start | bytes 516104 | tf_op jit(solution)/shard_map/ppermute | solution.py:243
  9.8 0.8 %collective-permute-start.7 = (f32[64,384]{1,0:T(8,128)}, f32[64,384]{1,0:T(8,128)S(1)}, u32[]{:S(2)}, u32[]{:S(2)}) collective-permute-start(f32[64,384]{1,0:T(8,128)} %get-tuple-element.26), channel_id=1, source_target_pairs={{0,8},{1,11},{2,10},{3,9},{4,12},{5,15},{6,14},{7,13},{8,0},{9,3},... | collective-permute-start | bytes 294920 | tf_op jit(solution)/shard_map/ppermute | solution.py:243
  10.6 1.7 %collective-permute-done.1.refs_1_.rest_13_ = f32[64,384]{1,0:T(8,128)S(1)} collective-permute-done((f32[64,384]{1,0:T(8,128)}, f32[64,384]{1,0:T(8,128)S(1)}, u32[]{:S(2)}, u32[]{:S(2)}) %collective-permute-start.1) | collective-permute-done | bytes 98336 | tf_op jit(solution)/shard_map/ppermute | solution.py:243
  12.3 3.8 %collective-permute-done.6.rest_11_ = f32[64,384]{1,0:T(8,128)S(1)} collective-permute-done((f32[64,384]{1,0:T(8,128)}, f32[64,384]{1,0:T(8,128)S(1)}, u32[]{:S(2)}, u32[]{:S(2)}) %collective-permute-start.6) | collective-permute-done | bytes 98336 | tf_op jit(solution)/shard_map/ppermute | solution.py:243
  16.1 0.4 collective-permute-start.8
  16.5 0.9 %collective-permute-done.refs_0_.rest_10_.rest_0_ = f32[168,256]{1,0:T(8,128)S(1)} collective-permute-done((f32[168,256]{1,0:T(8,128)}, f32[168,256]{1,0:T(8,128)S(1)}, u32[]{:S(2)}, u32[]{:S(2)}) %collective-permute-start) | collective-permute-done | bytes 172064 | tf_op jit(solution)/shard_map/ppermute | solution.py:243
  17.4 0.9 %copy-done.1 = f32[128,256]{1,0:T(8,128)S(1)} copy-done((f32[128,256]{1,0:T(8,128)S(1)}, f32[128,256]{1,0:T(8,128)}, u32[]{:S(2)}) %copy-start.1) | copy-done | bytes 131096
  18.3 0.4 %shard_map.77 = (f32[128,256]{1,0:T(8,128)S(1)}, f32[128,256]{1,0:T(8,128)S(1)}, f32[128,256]{1,0:T(8,128)S(1)}, f32[128,256]{1,0:T(8,128)S(1)}) custom-call(f32[1,512,256]{2,1,0:T(8,128)S(1)} %copy-done, f32[128,256]{1,0:T(8,128)S(1)} %copy-done.1, f32[168,256]{1,0:T(8,128)S(1)} %collective-permute-done.refs_0_.rest_10_.rest_0_, ...), custom_call_target="tpu_custom_call" | custom-call | flops 201326592 | bytes 925696 | tf_op jit(solution)/shard_map/pallas_call | solution.py:216
  18.8 0.5 %collective-permute-start.3 = (f32[128,256]{1,0:T(8,128)S(1)}, f32[128,256]{1,0:T(8,128)S(1)}, u32[]{:S(2)}, u32[]{:S(2)}) collective-permute-start(f32[128,256]{1,0:T(8,128)S(1)} %get-tuple-element.20.rest_1_), channel_id=1, source_target_pairs={{0,1},{1,0},{2,3},{3,2},{4,5},{5,4},{6,7},{7,6},{8,9},{9,8},{10,11... | collective-permute-start | bytes 393224 | tf_op jit(solution)/shard_map/ppermute | solution.py:243
  19.3 0.1 collective-permute-start.4
  19.4 0.4 %collective-permute-start.5 = (f32[128,256]{1,0:T(8,128)S(1)}, f32[128,256]{1,0:T(8,128)S(1)}, u32[]{:S(2)}, u32[]{:S(2)}) collective-permute-start(f32[128,256]{1,0:T(8,128)S(1)} %get-tuple-element.22.rest_3_), channel_id=1, source_target_pairs={{0,1},{1,0},{2,3},{3,2},{4,5},{5,4},{6,7},{7,6},{8,9},{9,8},{10,11... | collective-permute-start | bytes 393224 | tf_op jit(solution)/shard_map/ppermute | solution.py:243
  19.8 0.1 collective-permute-start.9
  19.9 1.2 %collective-permute-done.9.rest_15_ = f32[64,384]{1,0:T(8,128)S(1)} collective-permute-done((f32[64,384]{1,0:T(8,128)S(1)}, f32[64,384]{1,0:T(8,128)S(1)}, u32[]{:S(2)}, u32[]{:S(2)}) %collective-permute-start.9) | collective-permute-done | bytes 98336 | tf_op jit(solution)/shard_map/ppermute | solution.py:243
  21.2 1.5 %shard_map.78 = (f32[128,256]{1,0:T(8,128)S(1)}, f32[128,256]{1,0:T(8,128)S(1)}, f32[128,256]{1,0:T(8,128)S(1)}, f32[192,256]{1,0:T(8,128)S(1)}) custom-call(f32[1,512,256]{2,1,0:T(8,128)S(1)} %copy-done, f32[128,256]{1,0:T(8,128)S(1)} %get-tuple-element.19.rest_0_, f32[128,256]{1,0:T(8,128)S(1)} %get-tuple-element.20.rest_1_, ...), custom_call_target="tpu_custom_call" | custom-call | flops 402653184 | bytes 2502656 | tf_op jit(solution)/shard_map/pallas_call | solution.py:216
  22.7 2.6 %collective-permute-start.12 = (f32[128,256]{1,0:T(8,128)S(1)}, f32[128,256]{1,0:T(8,128)S(1)}, u32[]{:S(2)}, u32[]{:S(2)}) collective-permute-start(f32[128,256]{1,0:T(8,128)S(1)} %get-tuple-element.29), channel_id=1, source_target_pairs={{0,8},{1,9},{2,10},{3,11},{4,12},{5,13},{6,14},{7,15},{8,0},{9,1},... | collective-permute-start | bytes 393224 | tf_op jit(solution)/shard_map/ppermute | solution.py:243
  25.4 1.7 %collective-permute-start.13 = (f32[128,256]{1,0:T(8,128)S(1)}, f32[128,256]{1,0:T(8,128)S(1)}, u32[]{:S(2)}, u32[]{:S(2)}) collective-permute-start(f32[128,256]{1,0:T(8,128)S(1)} %get-tuple-element.30), channel_id=1, source_target_pairs={{0,12},{1,13},{2,14},{3,15},{4,8},{5,9},{6,10},{7,11},{8,4},{9,5},... | collective-permute-start | bytes 393224 | tf_op jit(solution)/shard_map/ppermute | solution.py:243
  27.1 3.4 %collective-permute-done.11.rest_2_ = f32[128,256]{1,0:T(8,128)S(1)} collective-permute-done((f32[128,256]{1,0:T(8,128)S(1)}, f32[128,256]{1,0:T(8,128)S(1)}, u32[]{:S(2)}, u32[]{:S(2)}) %collective-permute-start.11) | collective-permute-done | bytes 131104 | tf_op jit(solution)/shard_map/ppermute | solution.py:243
  30.5 5.2 %collective-permute-done.12.rest_3_ = f32[128,256]{1,0:T(8,128)S(1)} collective-permute-done((f32[128,256]{1,0:T(8,128)S(1)}, f32[128,256]{1,0:T(8,128)S(1)}, u32[]{:S(2)}, u32[]{:S(2)}) %collective-permute-start.12) | collective-permute-done | bytes 131104 | tf_op jit(solution)/shard_map/ppermute | solution.py:243
  35.7 0.5 %collective-permute-start.16 = (f32[128,256]{1,0:T(8,128)S(1)}, f32[128,256]{1,0:T(8,128)S(1)}, u32[]{:S(2)}, u32[]{:S(2)}) collective-permute-start(f32[128,256]{1,0:T(8,128)S(1)} %collective-permute-done.13.rest_4_), channel_id=1, source_target_pairs={{0,1},{1,0},{2,3},{3,2},{4,5},{5,4},{6,7},{7,6},{8,9},{9,8},{10,11... | collective-permute-start | bytes 393224 | tf_op jit(solution)/shard_map/ppermute | solution.py:243
  36.2 0.8 %collective-permute-done.15.rest_6_ = f32[128,256]{1,0:T(8,128)S(1)} collective-permute-done((f32[128,256]{1,0:T(8,128)S(1)}, f32[128,256]{1,0:T(8,128)S(1)}, u32[]{:S(2)}, u32[]{:S(2)}) %collective-permute-start.15) | collective-permute-done | bytes 131104 | tf_op jit(solution)/shard_map/ppermute | solution.py:243
  37.0 0.2 collective-permute-done.16.rest_7_
  37.2 1.0 %shard_map.79 = (f32[16,512]{1,0:T(8,128)}, f32[1,32,256]{2,1,0:T(8,128)}, f32[2,128,256]{2,1,0:T(8,128)}) custom-call(f32[128,256]{1,0:T(8,128)S(1)} %copy-done.2, f32[168,256]{1,0:T(8,128)S(1)} %collective-permute-done.refs_0_.rest_10_.rest_0_, f32[192,256]{1,0:T(8,128)S(1)} %get-tuple-element.27.rest_1_, f32[128,256]{1,0:T(8,128)S(1)} %collective-permute-done.11.rest_2_, ...), custom_call_target="tpu_custom_call" | custom-call | flops 100663296 | bytes 1286144 | tf_op jit(solution)/shard_map/pallas_call | solution.py:216
  (24 shorter events, 0.2 us)
Async XLA Ops:
  0.6 16.8 %copy-start = (f32[1,512,256]{2,1,0:T(8,128)S(1)}, f32[1,512,256]{2,1,0:T(8,128)}, u32[]{:S(2)}) copy-start(f32[1,512,256]{2,1,0:T(8,128)} %core_ref.3) | copy-start | bytes 1572868
  3.2 9.1 %collective-permute-start.1 = (f32[64,384]{1,0:T(8,128)}, f32[64,384]{1,0:T(8,128)S(1)}, u32[]{:S(2)}, u32[]{:S(2)}) collective-permute-start(f32[64,384]{1,0:T(8,128)} %get-tuple-element.18), channel_id=1, source_target_pairs={{0,12},{1,15},{2,14},{3,13},{4,8},{5,11},{6,10},{7,9},{8,4},{9,7},... | collective-permute-start | bytes 294920 | tf_op jit(solution)/shard_map/ppermute | solution.py:243
  8.3 9.1 %collective-permute-start = (f32[168,256]{1,0:T(8,128)}, f32[168,256]{1,0:T(8,128)S(1)}, u32[]{:S(2)}, u32[]{:S(2)}) collective-permute-start(f32[168,256]{1,0:T(8,128)} %get-tuple-element.17), channel_id=1, source_target_pairs={{0,2},{1,3},{2,0},{3,1},{4,6},{5,7},{6,4},{7,5},{8,10},{9,11},{10,... | collective-permute-start | bytes 516104 | tf_op jit(solution)/shard_map/ppermute | solution.py:243
  9.8 6.3 %collective-permute-start.6 = (f32[64,384]{1,0:T(8,128)}, f32[64,384]{1,0:T(8,128)S(1)}, u32[]{:S(2)}, u32[]{:S(2)}) collective-permute-start(f32[64,384]{1,0:T(8,128)} %get-tuple-element.25), channel_id=1, source_target_pairs={{0,4},{1,7},{2,6},{3,5},{4,0},{5,3},{6,2},{7,1},{8,12},{9,15},{10,... | collective-permute-start | bytes 294920 | tf_op jit(solution)/shard_map/ppermute | solution.py:243
  9.8 9.5 %collective-permute-start.7 = (f32[64,384]{1,0:T(8,128)}, f32[64,384]{1,0:T(8,128)S(1)}, u32[]{:S(2)}, u32[]{:S(2)}) collective-permute-start(f32[64,384]{1,0:T(8,128)} %get-tuple-element.26), channel_id=1, source_target_pairs={{0,8},{1,11},{2,10},{3,9},{4,12},{5,15},{6,14},{7,13},{8,0},{9,3},... | collective-permute-start | bytes 294920 | tf_op jit(solution)/shard_map/ppermute | solution.py:243
  12.3 7.1 %collective-permute-start.10 = (f32[64,384]{1,0:T(8,128)S(1)}, f32[64,384]{1,0:T(8,128)S(1)}, u32[]{:S(2)}, u32[]{:S(2)}) collective-permute-start(f32[64,384]{1,0:T(8,128)S(1)} %collective-permute-done.1.refs_1_.rest_13_), channel_id=1, source_target_pairs={{0,1},{1,0},{2,3},{3,2},{4,5},{5,4},{6,7},{7,6},{8,9},{9,8},{10,11... | collective-permute-start | bytes 294920 | tf_op jit(solution)/shard_map/ppermute | solution.py:243
  16.1 3.7 %collective-permute-start.8 = (f32[64,384]{1,0:T(8,128)S(1)}, f32[64,384]{1,0:T(8,128)S(1)}, u32[]{:S(2)}, u32[]{:S(2)}) collective-permute-start(f32[64,384]{1,0:T(8,128)S(1)} %collective-permute-done.6.rest_11_), channel_id=1, source_target_pairs={{0,1},{1,0},{2,3},{3,2},{4,5},{5,4},{6,7},{7,6},{8,9},{9,8},{10,11... | collective-permute-start | bytes 294920 | tf_op jit(solution)/shard_map/ppermute | solution.py:243
  17.4 0.9 %copy-start.1 = (f32[128,256]{1,0:T(8,128)S(1)}, f32[128,256]{1,0:T(8,128)}, u32[]{:S(2)}) copy-start(f32[128,256]{1,0:T(8,128)} %tail_ref.3) | copy-start | bytes 393220
  18.3 2.8 %copy-start.3 = (f32[64,512]{1,0:T(8,128)S(1)}, f32[64,512]{1,0:T(8,128)}, u32[]{:S(2)}) copy-start(f32[64,512]{1,0:T(8,128)} %get-tuple-element.23.rest_8_) | copy-start | bytes 393220
  18.3 2.9 %copy-start.4 = (f32[72,128]{1,0:T(8,128)S(1)}, f32[72,128]{1,0:T(8,128)}, u32[]{:S(2)}) copy-start(f32[72,128]{1,0:T(8,128)} %get-tuple-element.24.rest_9_) | copy-start | bytes 110596
  18.7 2.4 %collective-permute-start.2 = (f32[128,256]{1,0:T(8,128)S(1)}, f32[128,256]{1,0:T(8,128)S(1)}, u32[]{:S(2)}, u32[]{:S(2)}) collective-permute-start(f32[128,256]{1,0:T(8,128)S(1)} %get-tuple-element.19.rest_0_), channel_id=1, source_target_pairs={{0,1},{1,0},{2,3},{3,2},{4,5},{5,4},{6,7},{7,6},{8,9},{9,8},{10,11... | collective-permute-start | bytes 393224 | tf_op jit(solution)/shard_map/ppermute | solution.py:243
  18.8 2.3 %collective-permute-start.3 = (f32[128,256]{1,0:T(8,128)S(1)}, f32[128,256]{1,0:T(8,128)S(1)}, u32[]{:S(2)}, u32[]{:S(2)}) collective-permute-start(f32[128,256]{1,0:T(8,128)S(1)} %get-tuple-element.20.rest_1_), channel_id=1, source_target_pairs={{0,1},{1,0},{2,3},{3,2},{4,5},{5,4},{6,7},{7,6},{8,9},{9,8},{10,11... | collective-permute-start | bytes 393224 | tf_op jit(solution)/shard_map/ppermute | solution.py:243
  19.3 1.8 %collective-permute-start.4 = (f32[128,256]{1,0:T(8,128)S(1)}, f32[128,256]{1,0:T(8,128)S(1)}, u32[]{:S(2)}, u32[]{:S(2)}) collective-permute-start(f32[128,256]{1,0:T(8,128)S(1)} %get-tuple-element.21.rest_2_), channel_id=1, source_target_pairs={{0,1},{1,0},{2,3},{3,2},{4,5},{5,4},{6,7},{7,6},{8,9},{9,8},{10,11... | collective-permute-start | bytes 393224 | tf_op jit(solution)/shard_map/ppermute | solution.py:243
  19.4 1.8 %collective-permute-start.5 = (f32[128,256]{1,0:T(8,128)S(1)}, f32[128,256]{1,0:T(8,128)S(1)}, u32[]{:S(2)}, u32[]{:S(2)}) collective-permute-start(f32[128,256]{1,0:T(8,128)S(1)} %get-tuple-element.22.rest_3_), channel_id=1, source_target_pairs={{0,1},{1,0},{2,3},{3,2},{4,5},{5,4},{6,7},{7,6},{8,9},{9,8},{10,11... | collective-permute-start | bytes 393224 | tf_op jit(solution)/shard_map/ppermute | solution.py:243
  19.8 1.3 %collective-permute-start.9 = (f32[64,384]{1,0:T(8,128)S(1)}, f32[64,384]{1,0:T(8,128)S(1)}, u32[]{:S(2)}, u32[]{:S(2)}) collective-permute-start(f32[64,384]{1,0:T(8,128)S(1)} %collective-permute-done.7.rest_12_), channel_id=1, source_target_pairs={{0,1},{1,0},{2,3},{3,2},{4,5},{5,4},{6,7},{7,6},{8,9},{9,8},{10,11... | collective-permute-start | bytes 294920 | tf_op jit(solution)/shard_map/ppermute | solution.py:243
  21.2 16.1 %copy-start.2 = (f32[128,256]{1,0:T(8,128)S(1)}, f32[128,256]{1,0:T(8,128)}, u32[]{:S(2)}) copy-start(f32[128,256]{1,0:T(8,128)} %tail_ref.3) | copy-start | bytes 393220
  22.6 7.9 %collective-permute-start.11 = (f32[128,256]{1,0:T(8,128)S(1)}, f32[128,256]{1,0:T(8,128)S(1)}, u32[]{:S(2)}, u32[]{:S(2)}) collective-permute-start(f32[128,256]{1,0:T(8,128)S(1)} %get-tuple-element.28), channel_id=1, source_target_pairs={{0,4},{1,5},{2,6},{3,7},{4,0},{5,1},{6,2},{7,3},{8,12},{9,13},{10,... | collective-permute-start | bytes 393224 | tf_op jit(solution)/shard_map/ppermute | solution.py:243
  22.7 13.0 %collective-permute-start.12 = (f32[128,256]{1,0:T(8,128)S(1)}, f32[128,256]{1,0:T(8,128)S(1)}, u32[]{:S(2)}, u32[]{:S(2)}) collective-permute-start(f32[128,256]{1,0:T(8,128)S(1)} %get-tuple-element.29), channel_id=1, source_target_pairs={{0,8},{1,9},{2,10},{3,11},{4,12},{5,13},{6,14},{7,15},{8,0},{9,1},... | collective-permute-start | bytes 393224 | tf_op jit(solution)/shard_map/ppermute | solution.py:243
  25.4 10.3 %collective-permute-start.13 = (f32[128,256]{1,0:T(8,128)S(1)}, f32[128,256]{1,0:T(8,128)S(1)}, u32[]{:S(2)}, u32[]{:S(2)}) collective-permute-start(f32[128,256]{1,0:T(8,128)S(1)} %get-tuple-element.30), channel_id=1, source_target_pairs={{0,12},{1,13},{2,14},{3,15},{4,8},{5,9},{6,10},{7,11},{8,4},{9,5},... | collective-permute-start | bytes 393224 | tf_op jit(solution)/shard_map/ppermute | solution.py:243
  30.5 5.7 %collective-permute-start.14 = (f32[128,256]{1,0:T(8,128)S(1)}, f32[128,256]{1,0:T(8,128)S(1)}, u32[]{:S(2)}, u32[]{:S(2)}) collective-permute-start(f32[128,256]{1,0:T(8,128)S(1)} %collective-permute-done.11.rest_2_), channel_id=1, source_target_pairs={{0,1},{1,0},{2,3},{3,2},{4,5},{5,4},{6,7},{7,6},{8,9},{9,8},{10,11... | collective-permute-start | bytes 393224 | tf_op jit(solution)/shard_map/ppermute | solution.py:243
  35.7 1.3 %collective-permute-start.15 = (f32[128,256]{1,0:T(8,128)S(1)}, f32[128,256]{1,0:T(8,128)S(1)}, u32[]{:S(2)}, u32[]{:S(2)}) collective-permute-start(f32[128,256]{1,0:T(8,128)S(1)} %collective-permute-done.12.rest_3_), channel_id=1, source_target_pairs={{0,1},{1,0},{2,3},{3,2},{4,5},{5,4},{6,7},{7,6},{8,9},{9,8},{10,11... | collective-permute-start | bytes 393224 | tf_op jit(solution)/shard_map/ppermute | solution.py:243
  35.7 1.5 %collective-permute-start.16 = (f32[128,256]{1,0:T(8,128)S(1)}, f32[128,256]{1,0:T(8,128)S(1)}, u32[]{:S(2)}, u32[]{:S(2)}) collective-permute-start(f32[128,256]{1,0:T(8,128)S(1)} %collective-permute-done.13.rest_4_), channel_id=1, source_target_pairs={{0,1},{1,0},{2,3},{3,2},{4,5},{5,4},{6,7},{7,6},{8,9},{9,8},{10,11... | collective-permute-start | bytes 393224 | tf_op jit(solution)/shard_map/ppermute | solution.py:243

commit v3 on v2

--- a/solution.py
+++ b/solution.py
@@ -95,7 +95,7 @@
 
 
 def query_kernel(core_ref, tail_ref, *refs):
-    x_refs, outs = refs[: -1 - QUERY_PARTS], refs[-QUERY_PARTS:]
+    x_refs, outs = refs[: -2 - QUERY_PARTS], refs[-QUERY_PARTS:]
     depth = tail_ref.shape[0]
     tails = [tail_ref[...]] + [x[0:depth, :] for x in x_refs]
     value = dot3(split(core_ref[0]), split(jnp.concatenate(tails, axis=0)), NT)
@@ -105,8 +105,8 @@
 
 
 def grad_kernel(wide, cols, refs):
-    (core_ref, query_refs, query_others, head_own, label_own, x_refs, z_refs, swap_refs, outs, own_ref,
-     heads, resid, outer, tails) = refs
+    (core_ref, core_other, query_refs, query_others, head_own, label_own, x_refs, z_refs, swap_refs, own_ref, joint_ref, fars,
+     heads, resid, outer, tails, tails_other) = refs
     w, t, s = place()
     block, dim = head_own.shape
     width = label_own.shape[1]
@@ -145,29 +145,49 @@
             resid[k * block : (k + 1) * block, lanes] = times * prob[k * block : (k + 1) * block, lanes] - label
     resid_parts = split(resid[...])
     outer[...] = dot3(head_parts, resid_parts, TN)
-    tails[...] = dot3(split(outer[:, 0:width]), split(core_ref[0]), TN)
-    picked = [resid[pl.ds(pl.multiple_of(k * block + t * chunk, chunk), chunk), :] for k in range(wide)]
+    tails[...] = dot3(split(outer[...]), split(core_ref[0]), TN)
+    across = jnp.where(s == 0, outer[:, 0:width], outer[:, width : 2 * width])
+    tails_other[...] = dot3(split(across), split(core_other[0]), TN)
+    starts = [k * block + t * chunk for k in range(2)]
+    for j in range(1, wide // 2):
+        starts += [(2 * j + 1 - s) * block + part * rows + (t ^ s) * chunk for part in range(2)]
+    picked = [resid[pl.ds(pl.multiple_of(start, chunk), chunk), :] for start in starts]
     head_sum = dot3(split(jnp.concatenate(picked, axis=0)), query, NT)
     core_rows = dim // wide
     tail_rows = width // wide
     span = core_rows // 2
-    chunks = cols * width // half
-    for k in range(wide):
-        ref = own_ref if k == 0 else outs[k - 1]
+
+    def put_outer(ref, start, take, flip):
+        piece = outer[pl.ds(pl.multiple_of(start, take), take), :]
+        for i in range(cols // 2):
+            first, last = piece[:, 2 * i * width : (2 * i + 1) * width], piece[:, (2 * i + 1) * width : 2 * (i + 1) * width]
+            if flip:
+                first, last = jnp.where(s == 0, first, last), jnp.where(s == 0, last, first)
+            ref[i * take : (i + 1) * take, 0:width] = first
+            ref[i * take : (i + 1) * take, width:] = last
+        return cols // 2 * take
+
+    def put_head(ref, at, item):
+        for i in range(dim // half):
+            ref[at : at + chunk, :] = head_sum[item * chunk : (item + 1) * chunk, i * half : (i + 1) * half]
+            at += chunk
+        return at
+
+    for k, ref in enumerate((own_ref, joint_ref)):
         take = core_rows if k == 0 else span
-        start = (w ^ k) * core_rows if k == 0 else (w ^ k) * core_rows + s * span
-        piece = outer[pl.ds(pl.multiple_of(start, take), take), :]
-        at = 0
-        for i in range(chunks):
-            ref[at : at + take, :] = piece[:, i * half : (i + 1) * half]
-            at += take
-        for i in range(dim // half):
-            ref[at : at + chunk, :] = head_sum[k * chunk : (k + 1) * chunk, i * half : (i + 1) * half]
-            at += chunk
+        at = put_outer(ref, (w ^ k) * core_rows + (0 if k == 0 else s * span), take, False)
+        at = put_head(ref, at, k)
         ref[at : at + tail_rows, :] = rows_at(tails, w ^ k, tail_rows)
-
-
-def finish_kernel(wide, cols, scales, tail_ref, x_refs, own_ref, z_refs, swap_refs, head_out, tail_out, core_out, pieces):
+    for j, (outer_ref, sum_ref) in enumerate(fars, 1):
+        target = w ^ (2 * j + 1 - s)
+        put_outer(outer_ref, target * core_rows, core_rows, True)
+        at = put_head(sum_ref, put_head(sum_ref, 0, 2 * j), 2 * j + 1)
+        pitch = -(-tail_rows // 8) * 8
+        sum_ref[at : at + tail_rows, :] = rows_at(tails, s * wide + target, tail_rows)
+        sum_ref[at + pitch : at + pitch + tail_rows, :] = rows_at(tails_other, target, tail_rows)
+
+
+def finish_kernel(wide, cols, scales, tail_ref, x_refs, own_ref, joint, fars, head_out, tail_out, core_out, pieces):
     w, t, s = place()
     depth, half = tail_ref.shape
     core_rows = core_out.shape[1]
@@ -176,39 +196,37 @@
     tail_rows = tail_out.shape[1]
     chunks = cols * depth // half
     each = wide // cols
-    for k in range(wide):
-        relation = w ^ k
-
+
+    def keep(relation, parts):
         @pl.when(relation // each == t)
-        def _(k=k, at=relation % each):
-            for i in range(chunks):
-                lanes = slice(i * half, (i + 1) * half)
-                if k == 0:
-                    pieces[at, :, lanes] = own_ref[i * core_rows : (i + 1) * core_rows, :]
-                else:
-                    pieces[at, pl.ds(pl.multiple_of(s * span, span), span), lanes] = (
-                        z_refs[k - 1][i * span : (i + 1) * span, :]
+        def _():
+            at = relation % each
+            for ref, start, take in parts:
+                for i in range(chunks):
+                    pieces[at, pl.ds(pl.multiple_of(start, take), take), i * half : (i + 1) * half] = (
+                        ref[i * take : (i + 1) * take, :]
                     )
-                    pieces[at, pl.ds(pl.multiple_of((1 - s) * span, span), span), lanes] = (
-                        swap_refs[k - 1][i * span : (i + 1) * span, :]
-                    )
-
+
+    keep(w, [(own_ref, 0, core_rows)])
+    keep(w ^ 1, [(joint[0], s * span, span), (joint[1], (1 - s) * span, span)])
+    lead = [(own_ref, chunks * core_rows, 0), (joint[0], chunks * span, 0)]
+    for j, (outer_in, outer_swap, sum_in, sum_swap) in enumerate(fars, 1):
+        keep(w ^ (2 * j + 1 - s), [(outer_in, 0, core_rows)])
+        keep(w ^ (2 * j + s), [(outer_swap, 0, core_rows)])
+        lead += [(sum_in, 0, 0), (sum_swap, 0, 1)]
+    heads = dim // half * chunk
+    pitch = -(-tail_rows // 8) * 8
+    for i in range(dim // half):
+        total = sum(ref[at + part * heads + i * chunk : at + part * heads + (i + 1) * chunk, :] for ref, at, part in lead)
+        head_out[:, i * half : (i + 1) * half] = total * scales[0]
+    total = 0.0
+    for n, (ref, at, part) in enumerate(lead):
+        at += heads if n < 2 else 2 * heads + part * pitch
+        total = total + ref[at : at + tail_rows, :]
+    tail_out[0] = total * scales[1]
     tails = split(jnp.concatenate([tail_ref[...]] + [x[0:depth, :] for x in x_refs], axis=0))
     for i in range(each):
         core_out[i] = dot3(split(pieces[i]), tails, NN) * scales[2]
-    for i in range(dim // half):
-        at = chunks * core_rows + i * chunk
-        total = own_ref[at : at + chunk, :]
-        for ref in z_refs:
-            at = chunks * span + i * chunk
-            total = total + ref[at : at + chunk, :]
-        head_out[:, i * half : (i + 1) * half] = total * scales[0]
-    at = chunks * core_rows + dim // half * chunk
-    total = own_ref[at : at + tail_rows, :]
-    for ref in z_refs:
-        at = chunks * span + dim // half * chunk
-        total = total + ref[at : at + tail_rows, :]
-    tail_out[0] = total * scales[1]
 
 
 def call(kernel, inputs, outputs, scratch=(), hbm=(), flops=0, limit=VMEM_LIMIT):
@@ -233,16 +251,20 @@
     chunk = rows // cols
     axes = ("wide", "tail", "sub")
 
-    def move(value, k, offsets=(0, 0), flip=0):
+    def move(value, k, offsets=(0, 0), flip=0, owners=False):
+        steps = k if isinstance(k, tuple) else (k, k)
         pairs = []
         for w in range(wide):
             for t in range(cols):
                 for s in range(2):
-                    target = ((w ^ k) * cols + (t ^ offsets[s])) * 2 + (s ^ flip)
-                    pairs.append(((w * cols + t) * 2 + s, target))
+                    line = t ^ offsets[s]
+                    if not owners or line == w // (wide // cols):
+                        target = ((w ^ steps[s]) * cols + line) * 2 + (s ^ flip)
+                        pairs.append(((w * cols + t) * 2 + s, target))
         return lax.ppermute(value, axes, pairs)
 
     order = list(range(wide - 1, 0, -1))
+    core_other = move(core_mats, 0, flip=1)
     packed = call(
         functools.partial(pack_kernel, wide, cols),
         (core_lists, labels, head_embed, tail_embed),
@@ -267,14 +289,15 @@
     x_in = [move(x_out, 0, (o, o)) for o in range(1, cols)]
     query = call(
         query_kernel,
-        (core_mats, tail_embed, *x_in, z_in[order[0]][0]),
+        (core_mats, tail_embed, *x_in, z_in[order[0]][0], core_other),
         [(dim // QUERY_PARTS, cols * depth)] * QUERY_PARTS,
-        hbm=(cols + 1,),
+        hbm=(cols + 1, cols + 2),
         flops=6 * dim * half * cols * depth,
     )
     query_other = [move(value, 0, flip=1) for value in query]
     for k in order:
-        z_swap[k] = [move(value, 0, flip=1) for value in z_in[k]]
+        ready = z_in[k] if k == order[0] else lax.optimization_barrier((z_in[k], query[0]))[0]
+        z_swap[k] = [move(value, 0, flip=1) for value in ready]
 
     per = len(z_in[1])
     flat_in = [value for k in range(1, wide) for value in z_in[k]]
@@ -282,33 +305,41 @@
     core_rows, tail_rows = dim // wide, depth // wide
     chunks = cols * depth // half
     small = dim // half * chunk + -(-tail_rows // 8) * 8
-    send_shape = (chunks * core_rows // 2 + small, half)
     own_shape = (chunks * core_rows + small, half)
-
-    def grads(core_ref, *rest):
-        query_refs, other_refs, rest = rest[:QUERY_PARTS], rest[QUERY_PARTS : 2 * QUERY_PARTS], rest[2 * QUERY_PARTS :]
+    joint_shape = (chunks * core_rows // 2 + small, half)
+    pairs = range(1, wide // 2)
+
+    def grads(core_ref, other_ref, *rest):
+        query_refs, query_others, rest = rest[:QUERY_PARTS], rest[QUERY_PARTS : 2 * QUERY_PARTS], rest[2 * QUERY_PARTS :]
         head_ref, label_ref, *rest = rest
         x_refs, rest = rest[: cols - 1], rest[cols - 1 :]
         count = len(flat_in)
         group = lambda refs: [refs[i : i + per] for i in range(0, count, per)]
         z_refs, swap_refs, rest = group(rest[:count]), group(rest[count : 2 * count]), rest[2 * count :]
-        outs, own_ref, scratch = rest[: wide - 1], rest[wide - 1], rest[wide:]
+        own_ref, joint_ref, rest = rest[0], rest[1], rest[2:]
+        fars, scratch = list(zip(rest[0 : 2 * len(pairs) : 2], rest[1 : 2 * len(pairs) : 2])), rest[2 * len(pairs) :]
         grad_kernel(
             wide, cols,
-            (core_ref, query_refs, other_refs, head_ref, label_ref, x_refs, z_refs, swap_refs, outs, own_ref)
+            (core_ref, other_ref, query_refs, query_others, head_ref, label_ref, x_refs, z_refs, swap_refs, own_ref, joint_ref, fars)
             + tuple(scratch),
         )
 
     made = call(
         grads,
-        (core_mats, *query, *query_other, head_own, label_own, *x_in, *flat_in, *flat_swap),
-        [send_shape] * (wide - 1) + [own_shape],
-        scratch=[(wide * block, dim), (wide * block, cols * depth), (dim, cols * depth), (depth, half)],
+        (core_mats, core_other, *query, *query_other, head_own, label_own, *x_in, *flat_in, *flat_swap),
+        [own_shape, joint_shape] + [(chunks * core_rows, half), (2 * small, half)] * len(pairs),
+        scratch=[
+            (wide * block, dim), (wide * block, cols * depth), (dim, cols * depth), (cols * depth, half), (depth, half),
+        ],
         flops=6 * wide * block * dim * cols * depth * 2,
     )
-    own = made[-1]
-    back = {k: move(made[k - 1], k) for k in order}
-    back_swap = {k: move(back[k], 0, flip=1) for k in order}
+    own, far = made[0], []
+    for j in pairs:
+        steps = (2 * j + 1, 2 * j)
+        far.append([move(made[2 * j], steps, (0, 1), owners=True), move(made[2 * j + 1], steps, (0, 1))])
+    joint = move(made[1], 1)
+    far = [(a, move(a, 0, flip=1), b, move(b, 0, flip=1)) for a, b in far]
+    joint_swap = move(joint, 0, flip=1)
     heads_total, tails_total = block * wide, depth * cols
     scales = (
         1.0 / math.sqrt(slots * tails_total),
@@ -319,13 +350,16 @@
 
     def finish(tail_ref, *rest):
         x_refs, rest = rest[: cols - 1], rest[cols - 1 :]
-        finish_kernel(
-            wide, cols, scales, tail_ref, x_refs, rest[0], rest[1:wide], rest[wide : 2 * wide - 1], *rest[2 * wide - 1 :]
-        )
+        own_ref, rest = rest[0], rest[1:]
+        far_s, rest = rest[: 2 * len(pairs)], rest[2 * len(pairs) :]
+        joint_refs, rest = rest[:2], rest[2:]
+        far_u, rest = rest[: 2 * len(pairs)], rest[2 * len(pairs) :]
+        fars = [far_u[2 * i : 2 * i + 2] + far_s[2 * i : 2 * i + 2] for i in range(len(pairs))]
+        finish_kernel(wide, cols, scales, tail_ref, x_refs, own_ref, joint_refs, fars, *rest)
 
     return call(
         finish,
-        (tail_embed, *x_in, own, *[back[k] for k in range(1, wide)], *[back_swap[k] for k in range(1, wide)]),
+        (tail_embed, *x_in, own, *[v for g in far for v in g[2:]], joint, joint_swap, *[v for g in far for v in g[:2]]),
         [(chunk, dim), (1, tail_rows, half), (each, core_rows, half)],
         scratch=[(each, core_rows, cols * depth)],
         flops=6 * each * core_rows * cols * depth * half,

time: 38.4 us -> 36 us (0.938)
  waiting for transfers between devices: 17.3 us -> 12.1 us
  starting transfers between devices: 13.9 us -> 16.3 us
    ppermute x17 -> x18, waiting for transfers between devices: 17.3 us -> 12.1 us  [move(): return lax.ppermute(value, axes, pairs)]
    ppermute x17 -> x18, starting transfers between devices: 13.9 us -> 16.3 us  [move(): return lax.ppermute(value, axes, pairs)]
  transfers between devices with their start and end apart: 17 -> 18, of which waited for: 8 -> 8; matrix products, arithmetic and copies ran while one was open for 0% -> 0% of each run, Pallas kernels for 1% -> 8%
where the time goes in v3:
time: 36 us; the launch traced here: 35.8 us
  starting transfers between devices  16.3 us (45%)
  waiting for transfers between devices  12.1 us (34%)
  Pallas kernels  5.78 us (16%)
  local copies, waits for them, and re-layouts  0.92 us (3%)
  between operations  0.74 us (2%)
    ppermute x18, starting transfers between devices, move(): return lax.ppermute(value, axes, pairs)  16.3 us
    ppermute x18, waiting for transfers between devices, move(): return lax.ppermute(value, axes, pairs)  12.1 us
    pallas_call x4, Pallas kernels, call(): pl.pallas_call(kernel, out_shape=tuple((jax.ShapeDtypeStruct(shape, F32)...  5.78 us
    unnamed x10, local copies, waits for them, and re-layouts  0.92 us
  transfers between devices with their start and end apart: 18, of which 8 were waited for; matrix products, arithmetic and copies ran while one was open for 0% of the time, Pallas kernels for 8%

profile of v3, /device:TPU:0, one launch (start us, length us, event | category | flops | bytes accessed | tf_op | source)
XLA Modules:
  0.0 35.8 jit_solution(14627804554569188577)
XLA Ops:
  0.6 0.5 %collective-permute-start.1 = (f32[1,512,256]{2,1,0:T(8,128)}, f32[1,512,256]{2,1,0:T(8,128)S(1)}, u32[]{:S(2)}, u32[]{:S(2)}) collective-permute-start(f32[1,512,256]{2,1,0:T(8,128)} %core_ref.3), channel_id=1, source_target_pairs={{0,1},{1,0},{2,3},{3,2},{4,5},{5,4},{6,7},{7,6},{8,9},{9,8},{10,11... | collective-permute-start | bytes 1572872 | tf_op jit(solution)/shard_map/ppermute | solution.py:264
  1.2 2.5 %shard_map.76 = (f32[64,384]{1,0:T(8,128)}, f32[64,384]{1,0:T(8,128)}, f32[64,384]{1,0:T(8,128)}, f32[168,256]{1,0:T(8,128)}, f32[64,512]{1,0:T(8,128)}, /*index=5*/f32[72,128]{1,0:T(8,128)}) custom-call(s32[1,8]{1,0:T(1,128)} %list_hbm.1, s32[64,8,128]{2,1,0:T(8,128)} %label_hbm.1, f32[64,512]{1,0:T(8,128)} %head_hbm.1, f32[128,256]{1,0:T(8,128)} %tail_ref.3), custom_call_target="tpu_custom_call" | custom-call | bytes 524320 | tf_op jit(solution)/shard_map/pallas_call | solution.py:234
  3.7 2.6 %collective-permute-start = (f32[168,256]{1,0:T(8,128)}, f32[168,256]{1,0:T(8,128)S(1)}, u32[]{:S(2)}, u32[]{:S(2)}) collective-permute-start(f32[168,256]{1,0:T(8,128)} %get-tuple-element.19), channel_id=1, source_target_pairs={{0,2},{1,3},{2,0},{3,1},{4,6},{5,7},{6,4},{7,5},{8,10},{9,11},{10,... | collective-permute-start | bytes 516104 | tf_op jit(solution)/shard_map/ppermute | solution.py:264
  6.3 3.6 %collective-permute-start.2 = (f32[64,384]{1,0:T(8,128)}, f32[64,384]{1,0:T(8,128)S(1)}, u32[]{:S(2)}, u32[]{:S(2)}) collective-permute-start(f32[64,384]{1,0:T(8,128)} %get-tuple-element.20), channel_id=1, source_target_pairs={{0,12},{1,15},{2,14},{3,13},{4,8},{5,11},{6,10},{7,9},{8,4},{9,7},... | collective-permute-start | bytes 294920 | tf_op jit(solution)/shard_map/ppermute | solution.py:264
  9.9 0.8 %collective-permute-start.8 = (f32[64,384]{1,0:T(8,128)}, f32[64,384]{1,0:T(8,128)S(1)}, u32[]{:S(2)}, u32[]{:S(2)}) collective-permute-start(f32[64,384]{1,0:T(8,128)} %get-tuple-element.28), channel_id=1, source_target_pairs={{0,8},{1,11},{2,10},{3,9},{4,12},{5,15},{6,14},{7,13},{8,0},{9,3},... | collective-permute-start | bytes 294920 | tf_op jit(solution)/shard_map/ppermute | solution.py:264
  10.7 3.3 %collective-permute-done.2.refs_1_.rest_13_ = f32[64,384]{1,0:T(8,128)S(1)} collective-permute-done((f32[64,384]{1,0:T(8,128)}, f32[64,384]{1,0:T(8,128)S(1)}, u32[]{:S(2)}, u32[]{:S(2)}) %collective-permute-start.2) | collective-permute-done | bytes 98336 | tf_op jit(solution)/shard_map/ppermute | solution.py:264
  14.0 0.9 %copy-done.1 = f32[128,256]{1,0:T(8,128)S(1)} copy-done((f32[128,256]{1,0:T(8,128)S(1)}, f32[128,256]{1,0:T(8,128)}, u32[]{:S(2)}) %copy-start.1) | copy-done | bytes 131096
  14.9 0.4 %shard_map.77 = (f32[128,256]{1,0:T(8,128)S(1)}, f32[128,256]{1,0:T(8,128)S(1)}, f32[128,256]{1,0:T(8,128)S(1)}, f32[128,256]{1,0:T(8,128)S(1)}) custom-call(f32[1,512,256]{2,1,0:T(8,128)S(1)} %copy-done, f32[128,256]{1,0:T(8,128)S(1)} %copy-done.1, f32[168,256]{1,0:T(8,128)S(1)} %collective-permute-done.refs_0_.rest_10_.rest_0_, ...), custom_call_target="tpu_custom_call" | custom-call | flops 201326592 | bytes 1449984 | tf_op jit(solution)/shard_map/pallas_call | solution.py:234
  15.3 1.6 %collective-permute-done.7.rest_11_ = f32[64,384]{1,0:T(8,128)S(1)} collective-permute-done((f32[64,384]{1,0:T(8,128)}, f32[64,384]{1,0:T(8,128)S(1)}, u32[]{:S(2)}, u32[]{:S(2)}) %collective-permute-start.7) | collective-permute-done | bytes 98336 | tf_op jit(solution)/shard_map/ppermute | solution.py:264
  17.0 0.5 %collective-permute-start.4 = (f32[128,256]{1,0:T(8,128)S(1)}, f32[128,256]{1,0:T(8,128)S(1)}, u32[]{:S(2)}, u32[]{:S(2)}) collective-permute-start(f32[128,256]{1,0:T(8,128)S(1)} %get-tuple-element.22.rest_1_), channel_id=1, source_target_pairs={{0,1},{1,0},{2,3},{3,2},{4,5},{5,4},{6,7},{7,6},{8,9},{9,8},{10,11... | collective-permute-start | bytes 393224 | tf_op jit(solution)/shard_map/ppermute | solution.py:264
  17.5 1.2 %collective-permute-done.8.rest_12_ = f32[64,384]{1,0:T(8,128)S(1)} collective-permute-done((f32[64,384]{1,0:T(8,128)}, f32[64,384]{1,0:T(8,128)S(1)}, u32[]{:S(2)}, u32[]{:S(2)}) %collective-permute-start.8) | collective-permute-done | bytes 98336 | tf_op jit(solution)/shard_map/ppermute | solution.py:264
  18.7 0.6 %collective-permute-start.6 = (f32[128,256]{1,0:T(8,128)S(1)}, f32[128,256]{1,0:T(8,128)S(1)}, u32[]{:S(2)}, u32[]{:S(2)}) collective-permute-start(f32[128,256]{1,0:T(8,128)S(1)} %get-tuple-element.24.rest_3_), channel_id=1, source_target_pairs={{0,1},{1,0},{2,3},{3,2},{4,5},{5,4},{6,7},{7,6},{8,9},{9,8},{10,11... | collective-permute-start | bytes 393224 | tf_op jit(solution)/shard_map/ppermute | solution.py:264
  19.3 0.5 %collective-permute-start.10 = (f32[64,384]{1,0:T(8,128)S(1)}, f32[64,384]{1,0:T(8,128)S(1)}, u32[]{:S(2)}, u32[]{:S(2)}) collective-permute-start(f32[64,384]{1,0:T(8,128)S(1)} %collective-permute-done.8.rest_12_), channel_id=1, source_target_pairs={{0,1},{1,0},{2,3},{3,2},{4,5},{5,4},{6,7},{7,6},{8,9},{9,8},{10,11... | collective-permute-start | bytes 294920 | tf_op jit(solution)/shard_map/ppermute | solution.py:264
  19.8 1.0 %collective-permute-done.10.rest_15_ = f32[64,384]{1,0:T(8,128)S(1)} collective-permute-done((f32[64,384]{1,0:T(8,128)S(1)}, f32[64,384]{1,0:T(8,128)S(1)}, u32[]{:S(2)}, u32[]{:S(2)}) %collective-permute-start.10) | collective-permute-done | bytes 98336 | tf_op jit(solution)/shard_map/ppermute | solution.py:264
  20.8 1.9 %shard_map.78 = (f32[192,256]{1,0:T(8,128)S(1)}, f32[128,256]{1,0:T(8,128)S(1)}, f32[128,256]{1,0:T(8,128)S(1)}, f32[128,256]{1,0:T(8,128)S(1)}) custom-call(f32[1,512,256]{2,1,0:T(8,128)S(1)} %copy-done, f32[1,512,256]{2,1,0:T(8,128)S(1)} %collective-permute-done.1.refs_2_.other_ref, f32[128,256]{1,0:T(8,128)S(1)} %get-tuple-element.21.rest_0_, ...), custom_call_target="tpu_custom_call" | custom-call | flops 402653184 | bytes 3026944 | tf_op jit(solution)/shard_map/pallas_call | solution.py:234
  22.7 2.5 %collective-permute-start.12 = (f32[128,256]{1,0:T(8,128)S(1)}, f32[128,256]{1,0:T(8,128)S(1)}, u32[]{:S(2)}, u32[]{:S(2)}) collective-permute-start(f32[128,256]{1,0:T(8,128)S(1)} %get-tuple-element.32), channel_id=1, source_target_pairs={{0,12},{1,11},{2,14},{3,9},{4,8},{5,15},{6,10},{7,13},{8,4},{9,3},... | collective-permute-start | bytes 393224 | tf_op jit(solution)/shard_map/ppermute | solution.py:264
  25.2 3.2 %collective-permute-start.16 = (f32[128,256]{1,0:T(8,128)S(1)}, f32[128,256]{1,0:T(8,128)S(1)}, u32[]{:S(2)}, u32[]{:S(2)}) collective-permute-start(f32[128,256]{1,0:T(8,128)S(1)} %get-tuple-element.34), channel_id=1, source_target_pairs={{0,12},{3,9},{4,8},{7,13},{9,3},{10,6},{13,7},{14,2},{16,28},{19,2... | collective-permute-start | bytes 393224 | tf_op jit(solution)/shard_map/ppermute | solution.py:264
  28.5 2.3 %collective-permute-done.12.rest_2_ = f32[128,256]{1,0:T(8,128)S(1)} collective-permute-done((f32[128,256]{1,0:T(8,128)S(1)}, f32[128,256]{1,0:T(8,128)S(1)}, u32[]{:S(2)}, u32[]{:S(2)}) %collective-permute-start.12) | collective-permute-done | bytes 131104 | tf_op jit(solution)/shard_map/ppermute | solution.py:264
  30.8 0.9 %collective-permute-start.13 = (f32[128,256]{1,0:T(8,128)S(1)}, f32[128,256]{1,0:T(8,128)S(1)}, u32[]{:S(2)}, u32[]{:S(2)}) collective-permute-start(f32[128,256]{1,0:T(8,128)S(1)} %collective-permute-done.12.rest_2_), channel_id=1, source_target_pairs={{0,1},{1,0},{2,3},{3,2},{4,5},{5,4},{6,7},{7,6},{8,9},{9,8},{10,11... | collective-permute-start | bytes 393224 | tf_op jit(solution)/shard_map/ppermute | solution.py:264
  31.7 1.5 %collective-permute-done.14.rest_4_ = f32[128,256]{1,0:T(8,128)S(1)} collective-permute-done((f32[128,256]{1,0:T(8,128)S(1)}, f32[128,256]{1,0:T(8,128)S(1)}, u32[]{:S(2)}, u32[]{:S(2)}) %collective-permute-start.14) | collective-permute-done | bytes 131104 | tf_op jit(solution)/shard_map/ppermute | solution.py:264
  33.2 0.5 %collective-permute-start.17 = (f32[128,256]{1,0:T(8,128)S(1)}, f32[128,256]{1,0:T(8,128)S(1)}, u32[]{:S(2)}, u32[]{:S(2)}) collective-permute-start(f32[128,256]{1,0:T(8,128)S(1)} %collective-permute-done.16.rest_6_), channel_id=1, source_target_pairs={{0,1},{1,0},{2,3},{3,2},{4,5},{5,4},{6,7},{7,6},{8,9},{9,8},{10,11... | collective-permute-start | bytes 393224 | tf_op jit(solution)/shard_map/ppermute | solution.py:264
  33.8 0.8 %collective-permute-done.15.rest_5_ = f32[128,256]{1,0:T(8,128)S(1)} collective-permute-done((f32[128,256]{1,0:T(8,128)S(1)}, f32[128,256]{1,0:T(8,128)S(1)}, u32[]{:S(2)}, u32[]{:S(2)}) %collective-permute-start.15) | collective-permute-done | bytes 131104 | tf_op jit(solution)/shard_map/ppermute | solution.py:264
  34.6 0.2 collective-permute-done.17.rest_7_
  34.8 1.0 %shard_map.79 = (f32[16,512]{1,0:T(8,128)}, f32[1,32,256]{2,1,0:T(8,128)}, f32[2,128,256]{2,1,0:T(8,128)}) custom-call(f32[128,256]{1,0:T(8,128)S(1)} %copy-done.2, f32[168,256]{1,0:T(8,128)S(1)} %collective-permute-done.refs_0_.rest_10_.rest_0_, f32[192,256]{1,0:T(8,128)S(1)} %get-tuple-element.31.rest_1_, f32[128,256]{1,0:T(8,128)S(1)} %collective-permute-done.12.rest_2_, ...), custom_call_target="tpu_custom_call" | custom-call | flops 100663296 | bytes 1286144 | tf_op jit(solution)/shard_map/pallas_call | solution.py:234
  (26 shorter events, 0.1 us)
Async XLA Ops:
  0.6 13.3 %copy-start = (f32[1,512,256]{2,1,0:T(8,128)S(1)}, f32[1,512,256]{2,1,0:T(8,128)}, u32[]{:S(2)}) copy-start(f32[1,512,256]{2,1,0:T(8,128)} %core_ref.3) | copy-start | bytes 1572868
  0.6 13.3 %collective-permute-start.1 = (f32[1,512,256]{2,1,0:T(8,128)}, f32[1,512,256]{2,1,0:T(8,128)S(1)}, u32[]{:S(2)}, u32[]{:S(2)}) collective-permute-start(f32[1,512,256]{2,1,0:T(8,128)} %core_ref.3), channel_id=1, source_target_pairs={{0,1},{1,0},{2,3},{3,2},{4,5},{5,4},{6,7},{7,6},{8,9},{9,8},{10,11... | collective-permute-start | bytes 1572872 | tf_op jit(solution)/shard_map/ppermute | solution.py:264
  3.7 10.3 %collective-permute-start = (f32[168,256]{1,0:T(8,128)}, f32[168,256]{1,0:T(8,128)S(1)}, u32[]{:S(2)}, u32[]{:S(2)}) collective-permute-start(f32[168,256]{1,0:T(8,128)} %get-tuple-element.19), channel_id=1, source_target_pairs={{0,2},{1,3},{2,0},{3,1},{4,6},{5,7},{6,4},{7,5},{8,10},{9,11},{10,... | collective-permute-start | bytes 516104 | tf_op jit(solution)/shard_map/ppermute | solution.py:264
  6.3 7.7 %collective-permute-start.2 = (f32[64,384]{1,0:T(8,128)}, f32[64,384]{1,0:T(8,128)S(1)}, u32[]{:S(2)}, u32[]{:S(2)}) collective-permute-start(f32[64,384]{1,0:T(8,128)} %get-tuple-element.20), channel_id=1, source_target_pairs={{0,12},{1,15},{2,14},{3,13},{4,8},{5,11},{6,10},{7,9},{8,4},{9,7},... | collective-permute-start | bytes 294920 | tf_op jit(solution)/shard_map/ppermute | solution.py:264
  9.9 7.1 %collective-permute-start.7 = (f32[64,384]{1,0:T(8,128)}, f32[64,384]{1,0:T(8,128)S(1)}, u32[]{:S(2)}, u32[]{:S(2)}) collective-permute-start(f32[64,384]{1,0:T(8,128)} %get-tuple-element.27), channel_id=1, source_target_pairs={{0,4},{1,7},{2,6},{3,5},{4,0},{5,3},{6,2},{7,1},{8,12},{9,15},{10,... | collective-permute-start | bytes 294920 | tf_op jit(solution)/shard_map/ppermute | solution.py:264
  9.9 8.8 %collective-permute-start.8 = (f32[64,384]{1,0:T(8,128)}, f32[64,384]{1,0:T(8,128)S(1)}, u32[]{:S(2)}, u32[]{:S(2)}) collective-permute-start(f32[64,384]{1,0:T(8,128)} %get-tuple-element.28), channel_id=1, source_target_pairs={{0,8},{1,11},{2,10},{3,9},{4,12},{5,15},{6,14},{7,13},{8,0},{9,3},... | collective-permute-start | bytes 294920 | tf_op jit(solution)/shard_map/ppermute | solution.py:264
  14.0 5.3 %collective-permute-start.11 = (f32[64,384]{1,0:T(8,128)S(1)}, f32[64,384]{1,0:T(8,128)S(1)}, u32[]{:S(2)}, u32[]{:S(2)}) collective-permute-start(f32[64,384]{1,0:T(8,128)S(1)} %collective-permute-done.2.refs_1_.rest_13_), channel_id=1, source_target_pairs={{0,1},{1,0},{2,3},{3,2},{4,5},{5,4},{6,7},{7,6},{8,9},{9,8},{10,11... | collective-permute-start | bytes 294920 | tf_op jit(solution)/shard_map/ppermute | solution.py:264
  14.0 0.9 %copy-start.1 = (f32[128,256]{1,0:T(8,128)S(1)}, f32[128,256]{1,0:T(8,128)}, u32[]{:S(2)}) copy-start(f32[128,256]{1,0:T(8,128)} %tail_ref.3) | copy-start | bytes 393220
  14.9 5.9 %copy-start.3 = (f32[64,512]{1,0:T(8,128)S(1)}, f32[64,512]{1,0:T(8,128)}, u32[]{:S(2)}) copy-start(f32[64,512]{1,0:T(8,128)} %get-tuple-element.25.rest_8_) | copy-start | bytes 393220
  14.9 5.9 %copy-start.4 = (f32[72,128]{1,0:T(8,128)S(1)}, f32[72,128]{1,0:T(8,128)}, u32[]{:S(2)}) copy-start(f32[72,128]{1,0:T(8,128)} %get-tuple-element.26.rest_9_) | copy-start | bytes 110596
  16.9 2.3 %collective-permute-start.9 = (f32[64,384]{1,0:T(8,128)S(1)}, f32[64,384]{1,0:T(8,128)S(1)}, u32[]{:S(2)}, u32[]{:S(2)}) collective-permute-start(f32[64,384]{1,0:T(8,128)S(1)} %collective-permute-done.7.rest_11_), channel_id=1, source_target_pairs={{0,1},{1,0},{2,3},{3,2},{4,5},{5,4},{6,7},{7,6},{8,9},{9,8},{10,11... | collective-permute-start | bytes 294920 | tf_op jit(solution)/shard_map/ppermute | solution.py:264
  17.0 3.8 %collective-permute-start.4 = (f32[128,256]{1,0:T(8,128)S(1)}, f32[128,256]{1,0:T(8,128)S(1)}, u32[]{:S(2)}, u32[]{:S(2)}) collective-permute-start(f32[128,256]{1,0:T(8,128)S(1)} %get-tuple-element.22.rest_1_), channel_id=1, source_target_pairs={{0,1},{1,0},{2,3},{3,2},{4,5},{5,4},{6,7},{7,6},{8,9},{9,8},{10,11... | collective-permute-start | bytes 393224 | tf_op jit(solution)/shard_map/ppermute | solution.py:264
  17.5 3.3 %collective-permute-start.5 = (f32[128,256]{1,0:T(8,128)S(1)}, f32[128,256]{1,0:T(8,128)S(1)}, u32[]{:S(2)}, u32[]{:S(2)}) collective-permute-start(f32[128,256]{1,0:T(8,128)S(1)} %get-tuple-element.23.rest_2_), channel_id=1, source_target_pairs={{0,1},{1,0},{2,3},{3,2},{4,5},{5,4},{6,7},{7,6},{8,9},{9,8},{10,11... | collective-permute-start | bytes 393224 | tf_op jit(solution)/shard_map/ppermute | solution.py:264
  18.7 2.1 %collective-permute-start.6 = (f32[128,256]{1,0:T(8,128)S(1)}, f32[128,256]{1,0:T(8,128)S(1)}, u32[]{:S(2)}, u32[]{:S(2)}) collective-permute-start(f32[128,256]{1,0:T(8,128)S(1)} %get-tuple-element.24.rest_3_), channel_id=1, source_target_pairs={{0,1},{1,0},{2,3},{3,2},{4,5},{5,4},{6,7},{7,6},{8,9},{9,8},{10,11... | collective-permute-start | bytes 393224 | tf_op jit(solution)/shard_map/ppermute | solution.py:264
  19.3 1.5 %collective-permute-start.3 = (f32[128,256]{1,0:T(8,128)S(1)}, f32[128,256]{1,0:T(8,128)S(1)}, u32[]{:S(2)}, u32[]{:S(2)}) collective-permute-start(f32[128,256]{1,0:T(8,128)S(1)} %get-tuple-element.21.rest_0_), channel_id=1, source_target_pairs={{0,1},{1,0},{2,3},{3,2},{4,5},{5,4},{6,7},{7,6},{8,9},{9,8},{10,11... | collective-permute-start | bytes 393224 | tf_op jit(solution)/shard_map/ppermute | solution.py:264
  19.3 1.5 %collective-permute-start.10 = (f32[64,384]{1,0:T(8,128)S(1)}, f32[64,384]{1,0:T(8,128)S(1)}, u32[]{:S(2)}, u32[]{:S(2)}) collective-permute-start(f32[64,384]{1,0:T(8,128)S(1)} %collective-permute-done.8.rest_12_), channel_id=1, source_target_pairs={{0,1},{1,0},{2,3},{3,2},{4,5},{5,4},{6,7},{7,6},{8,9},{9,8},{10,11... | collective-permute-start | bytes 294920 | tf_op jit(solution)/shard_map/ppermute | solution.py:264
  20.8 14.0 %copy-start.2 = (f32[128,256]{1,0:T(8,128)S(1)}, f32[128,256]{1,0:T(8,128)}, u32[]{:S(2)}) copy-start(f32[128,256]{1,0:T(8,128)} %tail_ref.3) | copy-start | bytes 393220
  22.7 8.1 %collective-permute-start.12 = (f32[128,256]{1,0:T(8,128)S(1)}, f32[128,256]{1,0:T(8,128)S(1)}, u32[]{:S(2)}, u32[]{:S(2)}) collective-permute-start(f32[128,256]{1,0:T(8,128)S(1)} %get-tuple-element.32), channel_id=1, source_target_pairs={{0,12},{1,11},{2,14},{3,9},{4,8},{5,15},{6,10},{7,13},{8,4},{9,3},... | collective-permute-start | bytes 393224 | tf_op jit(solution)/shard_map/ppermute | solution.py:264
  25.2 8.0 %collective-permute-start.14 = (f32[128,256]{1,0:T(8,128)S(1)}, f32[128,256]{1,0:T(8,128)S(1)}, u32[]{:S(2)}, u32[]{:S(2)}) collective-permute-start(f32[128,256]{1,0:T(8,128)S(1)} %get-tuple-element.33), channel_id=1, source_target_pairs={{0,4},{1,5},{2,6},{3,7},{4,0},{5,1},{6,2},{7,3},{8,12},{9,13},{10,... | collective-permute-start | bytes 393224 | tf_op jit(solution)/shard_map/ppermute | solution.py:264
  25.2 8.0 %collective-permute-start.16 = (f32[128,256]{1,0:T(8,128)S(1)}, f32[128,256]{1,0:T(8,128)S(1)}, u32[]{:S(2)}, u32[]{:S(2)}) collective-permute-start(f32[128,256]{1,0:T(8,128)S(1)} %get-tuple-element.34), channel_id=1, source_target_pairs={{0,12},{3,9},{4,8},{7,13},{9,3},{10,6},{13,7},{14,2},{16,28},{19,2... | collective-permute-start | bytes 393224 | tf_op jit(solution)/shard_map/ppermute | solution.py:264
  30.8 2.9 %collective-permute-start.13 = (f32[128,256]{1,0:T(8,128)S(1)}, f32[128,256]{1,0:T(8,128)S(1)}, u32[]{:S(2)}, u32[]{:S(2)}) collective-permute-start(f32[128,256]{1,0:T(8,128)S(1)} %collective-permute-done.12.rest_2_), channel_id=1, source_target_pairs={{0,1},{1,0},{2,3},{3,2},{4,5},{5,4},{6,7},{7,6},{8,9},{9,8},{10,11... | collective-permute-start | bytes 393224 | tf_op jit(solution)/shard_map/ppermute | solution.py:264
  33.2 1.3 %collective-permute-start.15 = (f32[128,256]{1,0:T(8,128)S(1)}, f32[128,256]{1,0:T(8,128)S(1)}, u32[]{:S(2)}, u32[]{:S(2)}) collective-permute-start(f32[128,256]{1,0:T(8,128)S(1)} %collective-permute-done.14.rest_4_), channel_id=1, source_target_pairs={{0,1},{1,0},{2,3},{3,2},{4,5},{5,4},{6,7},{7,6},{8,9},{9,8},{10,11... | collective-permute-start | bytes 393224 | tf_op jit(solution)/shard_map/ppermute | solution.py:264
  33.2 1.5 %collective-permute-start.17 = (f32[128,256]{1,0:T(8,128)S(1)}, f32[128,256]{1,0:T(8,128)S(1)}, u32[]{:S(2)}, u32[]{:S(2)}) collective-permute-start(f32[128,256]{1,0:T(8,128)S(1)} %collective-permute-done.16.rest_6_), channel_id=1, source_target_pairs={{0,1},{1,0},{2,3},{3,2},{4,5},{5,4},{6,7},{7,6},{8,9},{9,8},{10,11... | collective-permute-start | bytes 393224 | tf_op jit(solution)/shard_map/ppermute | solution.py:264

commit v4 on v3

--- a/solution.py
+++ b/solution.py
@@ -11,7 +11,6 @@
 
 F32 = jnp.float32
 VMEM_LIMIT = 48 * 1024 * 1024
-QUERY_PARTS = 4
 FULL_LIMIT = 62 * 1024 * 1024
 NN = (((1,), (0,)), ((), ()))
 NT = (((1,), (1,)), ((), ()))
@@ -28,17 +27,24 @@
     lh, ll = left
     rh, rl = right
     mul = functools.partial(lax.dot_general, dimension_numbers=dims, preferred_element_type=F32)
-    return mul(lh, rh) + (mul(lh, rl) + mul(ll, rh))
-
-
-def rows_at(ref, index, count):
+    free = 1 - dims[0][0][0]
+    size = lh.shape[free]
+    both = mul(jnp.concatenate([lh, ll], axis=free), rh)
+    return both[:size] + (mul(lh, rl) + both[size:])
+
+
+def window(ref, index, count):
+    size = max(count, 8)
+    return ref[pl.ds(pl.multiple_of(index * count // size * size, size), size), :]
+
+
+def pick(value, index, count):
     if count % 8 == 0:
-        return ref[pl.ds(pl.multiple_of(index * count, count), count), :]
+        return value
     per = 8 // count
-    window = ref[pl.ds(pl.multiple_of(index // per * 8, 8), 8), :]
-    found = window[0:count]
+    found = value[0:count]
     for i in range(1, per):
-        found = jnp.where(index % per == i, window[i * count : (i + 1) * count], found)
+        found = jnp.where(index % per == i, value[i * count : (i + 1) * count], found)
     return found
 
 
@@ -46,7 +52,7 @@
     return lax.axis_index("wide"), lax.axis_index("tail"), lax.axis_index("sub")
 
 
-def pack_kernel(wide, cols, list_hbm, label_hbm, head_hbm, tail_hbm, *refs):
+def pack_kernel(wide, cols, list_hbm, label_hbm, head_hbm, tail_hbm, core_hbm, *refs):
     z_refs, (x_ref, head_own, label_own, listed, label_ref, head_ref, sems) = refs[: wide - 1], refs[wide - 1 :]
     w, t, s = place()
     block, slots, width = label_ref.shape
@@ -56,7 +62,12 @@
     copies = [
         pltpu.make_async_copy(source, target, sems.at[i])
         for i, (source, target) in enumerate(
-            ((list_hbm, listed), (label_hbm, label_ref), (head_hbm, head_ref), (tail_hbm, x_ref.at[0:depth]))
+            (
+                (list_hbm, listed),
+                (label_hbm, label_ref),
+                (head_hbm, head_ref),
+                (tail_hbm, x_ref.at[0:depth]),
+            )
         )
     ]
     for copy in copies:
@@ -94,19 +105,20 @@
     copies[3].wait()
 
 
-def query_kernel(core_ref, tail_ref, *refs):
-    x_refs, outs = refs[: -2 - QUERY_PARTS], refs[-QUERY_PARTS:]
-    depth = tail_ref.shape[0]
-    tails = [tail_ref[...]] + [x[0:depth, :] for x in x_refs]
-    value = dot3(split(core_ref[0]), split(jnp.concatenate(tails, axis=0)), NT)
-    size = outs[0].shape[0]
-    for i, ref in enumerate(outs):
-        ref[...] = value[i * size : (i + 1) * size]
+def query_kernel(core_ref, core_other, *refs):
+    tails, others, out_ref = refs[: len(refs) // 2], refs[len(refs) // 2 : -1], refs[-1]
+    depth = tails[0].shape[0]
+    total = None
+    for core, parts in ((core_ref, tails), (core_other, others)):
+        tail = jnp.concatenate([ref[0:depth, :] for ref in parts], axis=0)
+        value = dot3(split(core[0]), split(tail), NT)
+        total = value if total is None else total + value
+    out_ref[...] = total
 
 
 def grad_kernel(wide, cols, refs):
-    (core_ref, core_other, query_refs, query_others, head_own, label_own, x_refs, z_refs, swap_refs, own_ref, joint_ref, fars,
-     heads, resid, outer, tails, tails_other) = refs
+    (core_ref, core_other, query_ref, head_own, label_own, x_refs, z_refs, swap_refs, own_ref, joint_ref, fars,
+     heads, resid, outer, turned) = refs
     w, t, s = place()
     block, dim = head_own.shape
     width = label_own.shape[1]
@@ -119,7 +131,7 @@
         for part, ref in enumerate((z_refs[k - 1][0], swap_refs[k - 1][0])):
             heads[at + part * rows : at + part * rows + rows, 0:half] = ref[0:rows, 0:half]
             heads[at + part * rows : at + part * rows + rows, half:] = ref[rows:, 0:half]
-    query = split(jnp.concatenate([a[...] + b[...] for a, b in zip(query_refs, query_others)], axis=0))
+    query = split(query_ref[...])
     head_parts = split(heads[...])
     score = dot3(head_parts, query, NN)
     prob = jax.nn.sigmoid(score)
@@ -145,16 +157,19 @@
             resid[k * block : (k + 1) * block, lanes] = times * prob[k * block : (k + 1) * block, lanes] - label
     resid_parts = split(resid[...])
     outer[...] = dot3(head_parts, resid_parts, TN)
-    tails[...] = dot3(split(outer[...]), split(core_ref[0]), TN)
-    across = jnp.where(s == 0, outer[:, 0:width], outer[:, width : 2 * width])
-    tails_other[...] = dot3(split(across), split(core_other[0]), TN)
+    turned[...] = resid[...].T
+    tail_rows = width // wide
+    pitch = max(tail_rows, 8)
+    asked = [w, w ^ 1] + [s * wide + (w ^ (2 * j + 1 - s)) for j in range(1, wide // 2)]
+    mixed = dot3(split(jnp.concatenate([window(turned, index, tail_rows) for index in asked], axis=0)), head_parts, NN)
+    tails = dot3(split(mixed), split(core_ref[0]), NN)
+    tails_other = dot3(split(mixed[2 * pitch :]), split(core_other[0]), NN)
     starts = [k * block + t * chunk for k in range(2)]
     for j in range(1, wide // 2):
         starts += [(2 * j + 1 - s) * block + part * rows + (t ^ s) * chunk for part in range(2)]
     picked = [resid[pl.ds(pl.multiple_of(start, chunk), chunk), :] for start in starts]
     head_sum = dot3(split(jnp.concatenate(picked, axis=0)), query, NT)
     core_rows = dim // wide
-    tail_rows = width // wide
     span = core_rows // 2
 
     def put_outer(ref, start, take, flip):
@@ -177,14 +192,14 @@
         take = core_rows if k == 0 else span
         at = put_outer(ref, (w ^ k) * core_rows + (0 if k == 0 else s * span), take, False)
         at = put_head(ref, at, k)
-        ref[at : at + tail_rows, :] = rows_at(tails, w ^ k, tail_rows)
+        ref[at : at + tail_rows, :] = pick(tails[k * pitch : (k + 1) * pitch], w ^ k, tail_rows)
     for j, (outer_ref, sum_ref) in enumerate(fars, 1):
         target = w ^ (2 * j + 1 - s)
         put_outer(outer_ref, target * core_rows, core_rows, True)
         at = put_head(sum_ref, put_head(sum_ref, 0, 2 * j), 2 * j + 1)
-        pitch = -(-tail_rows // 8) * 8
-        sum_ref[at : at + tail_rows, :] = rows_at(tails, s * wide + target, tail_rows)
-        sum_ref[at + pitch : at + pitch + tail_rows, :] = rows_at(tails_other, target, tail_rows)
+        for values, first in ((tails, (j + 1) * pitch), (tails_other, (j - 1) * pitch)):
+            sum_ref[at : at + tail_rows, :] = pick(values[first : first + pitch], target, tail_rows)
+            at += pitch
 
 
 def finish_kernel(wide, cols, scales, tail_ref, x_refs, own_ref, joint, fars, head_out, tail_out, core_out, pieces):
@@ -263,22 +278,23 @@
                         pairs.append(((w * cols + t) * 2 + s, target))
         return lax.ppermute(value, axes, pairs)
 
-    order = list(range(wide - 1, 0, -1))
     core_other = move(core_mats, 0, flip=1)
+    order = [wide - 1] + list(range(1, wide - 1))
     packed = call(
         functools.partial(pack_kernel, wide, cols),
-        (core_lists, labels, head_embed, tail_embed),
-        [(block, half + depth)] * (wide - 1) + [(depth + rows + 8, half), (block, dim), (block + 8, depth)],
+        (core_lists, labels, head_embed, tail_embed, core_mats),
+        [(block, half + depth)] * (wide - 1)
+        + [(depth + rows + 8, half), (block, dim), (block + 8, depth)],
         scratch=[
             pltpu.SMEM(core_lists.shape, jnp.int32),
             pltpu.VMEM(labels.shape, jnp.int32),
             head_embed.shape,
             pltpu.SemaphoreType.DMA((4,)),
         ],
-        hbm=range(4),
+        hbm=range(5),
         limit=FULL_LIMIT,
     )
-    z_out, x_out, head_own, label_own = packed[: wide - 1], packed[-3], packed[-2], packed[-1]
+    z_out, (x_out, head_own, label_own) = packed[: wide - 1], packed[wide - 1 :]
     z_in, z_swap = {}, {}
     for k in order:
         got = []
@@ -287,21 +303,21 @@
             got.append(move(sent, k, (2 * j, (2 * j + 1) % cols)))
         z_in[k] = got
     x_in = [move(x_out, 0, (o, o)) for o in range(1, cols)]
-    query = call(
+    tail_other = move(lax.optimization_barrier((tail_embed, core_other))[0], 0, flip=1)
+    ready = lax.optimization_barrier((x_in, z_in[order[0]]))[0]
+    x_other = [move(value, 0, flip=1) for value in ready]
+    (query,) = call(
         query_kernel,
-        (core_mats, tail_embed, *x_in, z_in[order[0]][0], core_other),
-        [(dim // QUERY_PARTS, cols * depth)] * QUERY_PARTS,
-        hbm=(cols + 1, cols + 2),
-        flops=6 * dim * half * cols * depth,
-    )
-    query_other = [move(value, 0, flip=1) for value in query]
+        (core_mats, core_other, tail_embed, *x_in, tail_other, *x_other),
+        [(dim, cols * depth)],
+    )
     for k in order:
-        ready = z_in[k] if k == order[0] else lax.optimization_barrier((z_in[k], query[0]))[0]
+        ready = z_in[k]
         z_swap[k] = [move(value, 0, flip=1) for value in ready]
 
     per = len(z_in[1])
-    flat_in = [value for k in range(1, wide) for value in z_in[k]]
-    flat_swap = [value for k in range(1, wide) for value in z_swap[k]]
+    flat_in = [value for k in order for value in z_in[k]]
+    flat_swap = [value for k in order for value in z_swap[k]]
     core_rows, tail_rows = dim // wide, depth // wide
     chunks = cols * depth // half
     small = dim // half * chunk + -(-tail_rows // 8) * 8
@@ -309,27 +325,25 @@
     joint_shape = (chunks * core_rows // 2 + small, half)
     pairs = range(1, wide // 2)
 
-    def grads(core_ref, other_ref, *rest):
-        query_refs, query_others, rest = rest[:QUERY_PARTS], rest[QUERY_PARTS : 2 * QUERY_PARTS], rest[2 * QUERY_PARTS :]
-        head_ref, label_ref, *rest = rest
+    def grads(core_ref, other_ref, query_ref, head_ref, label_ref, *rest):
         x_refs, rest = rest[: cols - 1], rest[cols - 1 :]
         count = len(flat_in)
-        group = lambda refs: [refs[i : i + per] for i in range(0, count, per)]
+        group = lambda refs: [refs[order.index(k) * per : order.index(k) * per + per] for k in range(1, wide)]
         z_refs, swap_refs, rest = group(rest[:count]), group(rest[count : 2 * count]), rest[2 * count :]
         own_ref, joint_ref, rest = rest[0], rest[1], rest[2:]
         fars, scratch = list(zip(rest[0 : 2 * len(pairs) : 2], rest[1 : 2 * len(pairs) : 2])), rest[2 * len(pairs) :]
         grad_kernel(
             wide, cols,
-            (core_ref, other_ref, query_refs, query_others, head_ref, label_ref, x_refs, z_refs, swap_refs, own_ref, joint_ref, fars)
+            (core_ref, other_ref, query_ref, head_ref, label_ref, x_refs, z_refs, swap_refs, own_ref, joint_ref, fars)
             + tuple(scratch),
         )
 
     made = call(
         grads,
-        (core_mats, core_other, *query, *query_other, head_own, label_own, *x_in, *flat_in, *flat_swap),
+        (core_mats, core_other, query, head_own, label_own, *x_in, *flat_in, *flat_swap),
         [own_shape, joint_shape] + [(chunks * core_rows, half), (2 * small, half)] * len(pairs),
         scratch=[
-            (wide * block, dim), (wide * block, cols * depth), (dim, cols * depth), (cols * depth, half), (depth, half),
+            (wide * block, dim), (wide * block, cols * depth), (dim, cols * depth), (cols * depth, wide * block),
         ],
         flops=6 * wide * block * dim * cols * depth * 2,
     )

time: 36 us -> 35 us (0.972)
  local copies, waits for them, and re-layouts: 0.92 us -> 0.02 us
  waiting for transfers between devices: 12.1 us -> 12.6 us
  starting transfers between devices: 16.3 us -> 15.9 us
    unnamed x10 -> x8, local copies, waits for them, and re-layouts: 0.92 us -> 0.02 us
    ppermute x18 -> x16, waiting for transfers between devices: 12.1 us -> 12.6 us  [move(): return lax.ppermute(value, axes, pairs)]
    ppermute x18 -> x16, starting transfers between devices: 16.3 us -> 15.9 us  [move(): return lax.ppermute(value, axes, pairs)]
  transfers between devices with their start and end apart: 18 -> 16, of which waited for: 8 -> 8; matrix products, arithmetic and copies ran while one was open for 0% -> 0% of each run, Pallas kernels for 8% -> 9%
where the time goes in v4:
time: 35 us; the launch traced here: 34.9 us
  starting transfers between devices  15.9 us (45%)
  waiting for transfers between devices  12.6 us (36%)
  Pallas kernels  5.69 us (16%)
  between operations  0.72 us (2%)
    ppermute x16, starting transfers between devices, move(): return lax.ppermute(value, axes, pairs)  15.9 us
    ppermute x16, waiting for transfers between devices, move(): return lax.ppermute(value, axes, pairs)  12.6 us
    pallas_call x4, Pallas kernels, call(): pl.pallas_call(kernel, out_shape=tuple((jax.ShapeDtypeStruct(shape, F32)...  5.69 us
  transfers between devices with their start and end apart: 16, of which 8 were waited for; matrix products, arithmetic and copies ran while one was open for 0% of the time, Pallas kernels for 9%

profile of v4, /device:TPU:0, one launch (start us, length us, event | category | flops | bytes accessed | tf_op | source)
XLA Modules:
  0.0 34.9 jit_solution(1346110407414507739)
XLA Ops:
  0.7 0.5 %collective-permute-start.1 = (f32[1,512,256]{2,1,0:T(8,128)}, f32[1,512,256]{2,1,0:T(8,128)S(1)}, u32[]{:S(2)}, u32[]{:S(2)}) collective-permute-start(f32[1,512,256]{2,1,0:T(8,128)} %core_ref.3), channel_id=1, source_target_pairs={{0,1},{1,0},{2,3},{3,2},{4,5},{5,4},{6,7},{7,6},{8,9},{9,8},{10,11... | collective-permute-start | bytes 1572872 | tf_op jit(solution)/shard_map/ppermute | solution.py:279
  1.2 2.5 %shard_map.76 = (f32[64,384]{1,0:T(8,128)}, f32[64,384]{1,0:T(8,128)}, f32[64,384]{1,0:T(8,128)}, f32[168,256]{1,0:T(8,128)}, f32[64,512]{1,0:T(8,128)}, /*index=5*/f32[72,128]{1,0:T(8,128)}) custom-call(s32[1,8]{1,0:T(1,128)} %list_hbm.1, s32[64,8,128]{2,1,0:T(8,128)} %label_hbm.1, f32[64,512]{1,0:T(8,128)} %head_hbm.1, f32[128,256]{1,0:T(8,128)} %tail_ref.1, ...), custom_call_target="tpu_custom_call" | custom-call | bytes 1048608 | tf_op jit(solution)/shard_map/pallas_call | solution.py:249
  3.6 2.6 %collective-permute-start = (f32[168,256]{1,0:T(8,128)}, f32[168,256]{1,0:T(8,128)S(1)}, u32[]{:S(2)}, u32[]{:S(2)}) collective-permute-start(f32[168,256]{1,0:T(8,128)} %get-tuple-element.15), channel_id=1, source_target_pairs={{0,2},{1,3},{2,0},{3,1},{4,6},{5,7},{6,4},{7,5},{8,10},{9,11},{10,... | collective-permute-start | bytes 516104 | tf_op jit(solution)/shard_map/ppermute | solution.py:279
  6.3 3.6 %collective-permute-start.3 = (f32[64,384]{1,0:T(8,128)}, f32[64,384]{1,0:T(8,128)S(1)}, u32[]{:S(2)}, u32[]{:S(2)}) collective-permute-start(f32[64,384]{1,0:T(8,128)} %get-tuple-element.17), channel_id=1, source_target_pairs={{0,12},{1,15},{2,14},{3,13},{4,8},{5,11},{6,10},{7,9},{8,4},{9,7},... | collective-permute-start | bytes 294920 | tf_op jit(solution)/shard_map/ppermute | solution.py:279
  9.9 0.0 collective-permute-start.5
  9.9 0.8 %collective-permute-start.6 = (f32[64,384]{1,0:T(8,128)}, f32[64,384]{1,0:T(8,128)S(1)}, u32[]{:S(2)}, u32[]{:S(2)}) collective-permute-start(f32[64,384]{1,0:T(8,128)} %get-tuple-element.22), channel_id=1, source_target_pairs={{0,8},{1,11},{2,10},{3,9},{4,12},{5,15},{6,14},{7,13},{8,0},{9,3},... | collective-permute-start | bytes 294920 | tf_op jit(solution)/shard_map/ppermute | solution.py:279
  10.7 3.3 %collective-permute-done.3.rest_1_ = f32[64,384]{1,0:T(8,128)S(1)} collective-permute-done((f32[64,384]{1,0:T(8,128)}, f32[64,384]{1,0:T(8,128)S(1)}, u32[]{:S(2)}, u32[]{:S(2)}) %collective-permute-start.3) | collective-permute-done | bytes 98336 | tf_op jit(solution)/shard_map/ppermute | solution.py:279
  14.0 0.5 %collective-permute-start.2 = (f32[128,256]{1,0:T(8,128)S(1)}, f32[128,256]{1,0:T(8,128)S(1)}, u32[]{:S(2)}, u32[]{:S(2)}) collective-permute-start(f32[128,256]{1,0:T(8,128)S(1)} %copy-done.1), channel_id=1, source_target_pairs={{0,1},{1,0},{2,3},{3,2},{4,5},{5,4},{6,7},{7,6},{8,9},{9,8},{10,11... | collective-permute-start | bytes 393224 | tf_op jit(solution)/shard_map/ppermute | solution.py:279
  14.5 0.1 collective-permute-start.7
  14.5 2.4 %collective-permute-done.5.rest_2_ = f32[64,384]{1,0:T(8,128)S(1)} collective-permute-done((f32[64,384]{1,0:T(8,128)}, f32[64,384]{1,0:T(8,128)S(1)}, u32[]{:S(2)}, u32[]{:S(2)}) %collective-permute-start.5) | collective-permute-done | bytes 98336 | tf_op jit(solution)/shard_map/ppermute | solution.py:279
  17.0 1.7 %collective-permute-done.6.rest_3_ = f32[64,384]{1,0:T(8,128)S(1)} collective-permute-done((f32[64,384]{1,0:T(8,128)}, f32[64,384]{1,0:T(8,128)S(1)}, u32[]{:S(2)}, u32[]{:S(2)}) %collective-permute-start.6) | collective-permute-done | bytes 98336 | tf_op jit(solution)/shard_map/ppermute | solution.py:279
  18.7 0.6 %collective-permute-start.9 = (f32[64,384]{1,0:T(8,128)S(1)}, f32[64,384]{1,0:T(8,128)S(1)}, u32[]{:S(2)}, u32[]{:S(2)}) collective-permute-start(f32[64,384]{1,0:T(8,128)S(1)} %collective-permute-done.6.rest_3_), channel_id=1, source_target_pairs={{0,1},{1,0},{2,3},{3,2},{4,5},{5,4},{6,7},{7,6},{8,9},{9,8},{10,11... | collective-permute-start | bytes 294920 | tf_op jit(solution)/shard_map/ppermute | solution.py:279
  19.3 0.6 %shard_map.77.query_ref = f32[512,256]{1,0:T(8,128)S(1)} custom-call(f32[1,512,256]{2,1,0:T(8,128)S(1)} %copy-done, f32[1,512,256]{2,1,0:T(8,128)S(1)} %collective-permute-done.1.core_other.other_ref, f32[128,256]{1,0:T(8,128)S(1)} %copy-done.1, f32[168,256]{1,0:T(8,128)S(1)} %collective-permute-done.refs_1_.rest_0_, ...), custom_call_target="tpu_custom_call" | custom-call | bytes 1654784 | tf_op jit(solution)/shard_map/pallas_call | solution.py:249
  19.9 0.3 collective-permute-done.9.rest_6_
  20.2 1.6 %shard_map.78 = (f32[192,256]{1,0:T(8,128)S(1)}, f32[128,256]{1,0:T(8,128)S(1)}, f32[128,256]{1,0:T(8,128)S(1)}, f32[128,256]{1,0:T(8,128)S(1)}) custom-call(f32[1,512,256]{2,1,0:T(8,128)S(1)} %copy-done, f32[1,512,256]{2,1,0:T(8,128)S(1)} %collective-permute-done.1.core_other.other_ref, f32[512,256]{1,0:T(8,128)S(1)} %shard_map.77.query_ref, ...), custom_call_target="tpu_custom_call" | custom-call | flops 402653184 | bytes 2502656 | tf_op jit(solution)/shard_map/pallas_call | solution.py:249
  21.8 2.5 %collective-permute-start.10 = (f32[128,256]{1,0:T(8,128)S(1)}, f32[128,256]{1,0:T(8,128)S(1)}, u32[]{:S(2)}, u32[]{:S(2)}) collective-permute-start(f32[128,256]{1,0:T(8,128)S(1)} %get-tuple-element.24), channel_id=1, source_target_pairs={{0,12},{1,11},{2,14},{3,9},{4,8},{5,15},{6,10},{7,13},{8,4},{9,3},... | collective-permute-start | bytes 393224 | tf_op jit(solution)/shard_map/ppermute | solution.py:279
  24.3 3.2 %collective-permute-start.14 = (f32[128,256]{1,0:T(8,128)S(1)}, f32[128,256]{1,0:T(8,128)S(1)}, u32[]{:S(2)}, u32[]{:S(2)}) collective-permute-start(f32[128,256]{1,0:T(8,128)S(1)} %get-tuple-element.26), channel_id=1, source_target_pairs={{0,12},{3,9},{4,8},{7,13},{9,3},{10,6},{13,7},{14,2},{16,28},{19,2... | collective-permute-start | bytes 393224 | tf_op jit(solution)/shard_map/ppermute | solution.py:279
  27.6 2.3 %collective-permute-done.10.rest_2_ = f32[128,256]{1,0:T(8,128)S(1)} collective-permute-done((f32[128,256]{1,0:T(8,128)S(1)}, f32[128,256]{1,0:T(8,128)S(1)}, u32[]{:S(2)}, u32[]{:S(2)}) %collective-permute-start.10) | collective-permute-done | bytes 131104 | tf_op jit(solution)/shard_map/ppermute | solution.py:279
  29.9 0.9 %collective-permute-start.11 = (f32[128,256]{1,0:T(8,128)S(1)}, f32[128,256]{1,0:T(8,128)S(1)}, u32[]{:S(2)}, u32[]{:S(2)}) collective-permute-start(f32[128,256]{1,0:T(8,128)S(1)} %collective-permute-done.10.rest_2_), channel_id=1, source_target_pairs={{0,1},{1,0},{2,3},{3,2},{4,5},{5,4},{6,7},{7,6},{8,9},{9,8},{10,11... | collective-permute-start | bytes 393224 | tf_op jit(solution)/shard_map/ppermute | solution.py:279
  30.8 1.5 %collective-permute-done.12.rest_4_ = f32[128,256]{1,0:T(8,128)S(1)} collective-permute-done((f32[128,256]{1,0:T(8,128)S(1)}, f32[128,256]{1,0:T(8,128)S(1)}, u32[]{:S(2)}, u32[]{:S(2)}) %collective-permute-start.12) | collective-permute-done | bytes 131104 | tf_op jit(solution)/shard_map/ppermute | solution.py:279
  32.3 0.5 %collective-permute-start.15 = (f32[128,256]{1,0:T(8,128)S(1)}, f32[128,256]{1,0:T(8,128)S(1)}, u32[]{:S(2)}, u32[]{:S(2)}) collective-permute-start(f32[128,256]{1,0:T(8,128)S(1)} %collective-permute-done.14.rest_6_), channel_id=1, source_target_pairs={{0,1},{1,0},{2,3},{3,2},{4,5},{5,4},{6,7},{7,6},{8,9},{9,8},{10,11... | collective-permute-start | bytes 393224 | tf_op jit(solution)/shard_map/ppermute | solution.py:279
  32.8 0.8 %collective-permute-done.13.rest_5_ = f32[128,256]{1,0:T(8,128)S(1)} collective-permute-done((f32[128,256]{1,0:T(8,128)S(1)}, f32[128,256]{1,0:T(8,128)S(1)}, u32[]{:S(2)}, u32[]{:S(2)}) %collective-permute-start.13) | collective-permute-done | bytes 131104 | tf_op jit(solution)/shard_map/ppermute | solution.py:279
  33.7 0.2 collective-permute-done.15.rest_7_
  33.8 1.0 %shard_map.79 = (f32[16,512]{1,0:T(8,128)}, f32[1,32,256]{2,1,0:T(8,128)}, f32[2,128,256]{2,1,0:T(8,128)}) custom-call(f32[128,256]{1,0:T(8,128)S(1)} %copy-done.1, f32[168,256]{1,0:T(8,128)S(1)} %collective-permute-done.refs_1_.rest_0_, f32[192,256]{1,0:T(8,128)S(1)} %get-tuple-element.23.rest_1_, f32[128,256]{1,0:T(8,128)S(1)} %collective-permute-done.10.rest_2_, ...), custom_call_target="tpu_custom_call" | custom-call | flops 100663296 | bytes 1286144 | tf_op jit(solution)/shard_map/pallas_call | solution.py:249
  (20 shorter events, 0.0 us)
Async XLA Ops:
  0.6 18.6 %copy-start = (f32[1,512,256]{2,1,0:T(8,128)S(1)}, f32[1,512,256]{2,1,0:T(8,128)}, u32[]{:S(2)}) copy-start(f32[1,512,256]{2,1,0:T(8,128)} %core_ref.3) | copy-start | bytes 1572868
  0.6 13.3 %copy-start.1 = (f32[128,256]{1,0:T(8,128)S(1)}, f32[128,256]{1,0:T(8,128)}, u32[]{:S(2)}) copy-start(f32[128,256]{1,0:T(8,128)} %tail_ref.1) | copy-start | bytes 393220
  0.7 13.3 %collective-permute-start.1 = (f32[1,512,256]{2,1,0:T(8,128)}, f32[1,512,256]{2,1,0:T(8,128)S(1)}, u32[]{:S(2)}, u32[]{:S(2)}) collective-permute-start(f32[1,512,256]{2,1,0:T(8,128)} %core_ref.3), channel_id=1, source_target_pairs={{0,1},{1,0},{2,3},{3,2},{4,5},{5,4},{6,7},{7,6},{8,9},{9,8},{10,11... | collective-permute-start | bytes 1572872 | tf_op jit(solution)/shard_map/ppermute | solution.py:279
  3.6 10.3 %collective-permute-start = (f32[168,256]{1,0:T(8,128)}, f32[168,256]{1,0:T(8,128)S(1)}, u32[]{:S(2)}, u32[]{:S(2)}) collective-permute-start(f32[168,256]{1,0:T(8,128)} %get-tuple-element.15), channel_id=1, source_target_pairs={{0,2},{1,3},{2,0},{3,1},{4,6},{5,7},{6,4},{7,5},{8,10},{9,11},{10,... | collective-permute-start | bytes 516104 | tf_op jit(solution)/shard_map/ppermute | solution.py:279
  6.3 7.7 %collective-permute-start.3 = (f32[64,384]{1,0:T(8,128)}, f32[64,384]{1,0:T(8,128)S(1)}, u32[]{:S(2)}, u32[]{:S(2)}) collective-permute-start(f32[64,384]{1,0:T(8,128)} %get-tuple-element.17), channel_id=1, source_target_pairs={{0,12},{1,15},{2,14},{3,13},{4,8},{5,11},{6,10},{7,9},{8,4},{9,7},... | collective-permute-start | bytes 294920 | tf_op jit(solution)/shard_map/ppermute | solution.py:279
  9.9 7.1 %collective-permute-start.5 = (f32[64,384]{1,0:T(8,128)}, f32[64,384]{1,0:T(8,128)S(1)}, u32[]{:S(2)}, u32[]{:S(2)}) collective-permute-start(f32[64,384]{1,0:T(8,128)} %get-tuple-element.21), channel_id=1, source_target_pairs={{0,4},{1,7},{2,6},{3,5},{4,0},{5,3},{6,2},{7,1},{8,12},{9,15},{10,... | collective-permute-start | bytes 294920 | tf_op jit(solution)/shard_map/ppermute | solution.py:279
  9.9 10.3 %copy-start.2 = (f32[64,512]{1,0:T(8,128)S(1)}, f32[64,512]{1,0:T(8,128)}, u32[]{:S(2)}) copy-start(f32[64,512]{1,0:T(8,128)} %get-tuple-element.19.head_ref) | copy-start | bytes 393220
  9.9 10.3 %copy-start.3 = (f32[72,128]{1,0:T(8,128)S(1)}, f32[72,128]{1,0:T(8,128)}, u32[]{:S(2)}) copy-start(f32[72,128]{1,0:T(8,128)} %get-tuple-element.20.label_ref) | copy-start | bytes 110596
  9.9 8.8 %collective-permute-start.6 = (f32[64,384]{1,0:T(8,128)}, f32[64,384]{1,0:T(8,128)S(1)}, u32[]{:S(2)}, u32[]{:S(2)}) collective-permute-start(f32[64,384]{1,0:T(8,128)} %get-tuple-element.22), channel_id=1, source_target_pairs={{0,8},{1,11},{2,10},{3,9},{4,12},{5,15},{6,14},{7,13},{8,0},{9,3},... | collective-permute-start | bytes 294920 | tf_op jit(solution)/shard_map/ppermute | solution.py:279
  14.0 5.3 %collective-permute-start.4 = (f32[168,256]{1,0:T(8,128)S(1)}, f32[168,256]{1,0:T(8,128)S(1)}, u32[]{:S(2)}, u32[]{:S(2)}) collective-permute-start(f32[168,256]{1,0:T(8,128)S(1)} %collective-permute-done.refs_1_.rest_0_), channel_id=1, source_target_pairs={{0,1},{1,0},{2,3},{3,2},{4,5},{5,4},{6,7},{7,6},{8,9},{9,8},{10,11... | collective-permute-start | bytes 516104 | tf_op jit(solution)/shard_map/ppermute | solution.py:279
  14.0 5.3 %collective-permute-start.2 = (f32[128,256]{1,0:T(8,128)S(1)}, f32[128,256]{1,0:T(8,128)S(1)}, u32[]{:S(2)}, u32[]{:S(2)}) collective-permute-start(f32[128,256]{1,0:T(8,128)S(1)} %copy-done.1), channel_id=1, source_target_pairs={{0,1},{1,0},{2,3},{3,2},{4,5},{5,4},{6,7},{7,6},{8,9},{9,8},{10,11... | collective-permute-start | bytes 393224 | tf_op jit(solution)/shard_map/ppermute | solution.py:279
  14.5 5.4 %collective-permute-start.7 = (f32[64,384]{1,0:T(8,128)S(1)}, f32[64,384]{1,0:T(8,128)S(1)}, u32[]{:S(2)}, u32[]{:S(2)}) collective-permute-start(f32[64,384]{1,0:T(8,128)S(1)} %collective-permute-done.3.rest_1_), channel_id=1, source_target_pairs={{0,1},{1,0},{2,3},{3,2},{4,5},{5,4},{6,7},{7,6},{8,9},{9,8},{10,11... | collective-permute-start | bytes 294920 | tf_op jit(solution)/shard_map/ppermute | solution.py:279
  17.0 3.0 %collective-permute-start.8 = (f32[64,384]{1,0:T(8,128)S(1)}, f32[64,384]{1,0:T(8,128)S(1)}, u32[]{:S(2)}, u32[]{:S(2)}) collective-permute-start(f32[64,384]{1,0:T(8,128)S(1)} %collective-permute-done.5.rest_2_), channel_id=1, source_target_pairs={{0,1},{1,0},{2,3},{3,2},{4,5},{5,4},{6,7},{7,6},{8,9},{9,8},{10,11... | collective-permute-start | bytes 294920 | tf_op jit(solution)/shard_map/ppermute | solution.py:279
  18.7 1.5 %collective-permute-start.9 = (f32[64,384]{1,0:T(8,128)S(1)}, f32[64,384]{1,0:T(8,128)S(1)}, u32[]{:S(2)}, u32[]{:S(2)}) collective-permute-start(f32[64,384]{1,0:T(8,128)S(1)} %collective-permute-done.6.rest_3_), channel_id=1, source_target_pairs={{0,1},{1,0},{2,3},{3,2},{4,5},{5,4},{6,7},{7,6},{8,9},{9,8},{10,11... | collective-permute-start | bytes 294920 | tf_op jit(solution)/shard_map/ppermute | solution.py:279
  21.8 8.1 %collective-permute-start.10 = (f32[128,256]{1,0:T(8,128)S(1)}, f32[128,256]{1,0:T(8,128)S(1)}, u32[]{:S(2)}, u32[]{:S(2)}) collective-permute-start(f32[128,256]{1,0:T(8,128)S(1)} %get-tuple-element.24), channel_id=1, source_target_pairs={{0,12},{1,11},{2,14},{3,9},{4,8},{5,15},{6,10},{7,13},{8,4},{9,3},... | collective-permute-start | bytes 393224 | tf_op jit(solution)/shard_map/ppermute | solution.py:279
  24.3 8.0 %collective-permute-start.12 = (f32[128,256]{1,0:T(8,128)S(1)}, f32[128,256]{1,0:T(8,128)S(1)}, u32[]{:S(2)}, u32[]{:S(2)}) collective-permute-start(f32[128,256]{1,0:T(8,128)S(1)} %get-tuple-element.25), channel_id=1, source_target_pairs={{0,4},{1,5},{2,6},{3,7},{4,0},{5,1},{6,2},{7,3},{8,12},{9,13},{10,... | collective-permute-start | bytes 393224 | tf_op jit(solution)/shard_map/ppermute | solution.py:279
  24.3 8.0 %collective-permute-start.14 = (f32[128,256]{1,0:T(8,128)S(1)}, f32[128,256]{1,0:T(8,128)S(1)}, u32[]{:S(2)}, u32[]{:S(2)}) collective-permute-start(f32[128,256]{1,0:T(8,128)S(1)} %get-tuple-element.26), channel_id=1, source_target_pairs={{0,12},{3,9},{4,8},{7,13},{9,3},{10,6},{13,7},{14,2},{16,28},{19,2... | collective-permute-start | bytes 393224 | tf_op jit(solution)/shard_map/ppermute | solution.py:279
  29.9 2.9 %collective-permute-start.11 = (f32[128,256]{1,0:T(8,128)S(1)}, f32[128,256]{1,0:T(8,128)S(1)}, u32[]{:S(2)}, u32[]{:S(2)}) collective-permute-start(f32[128,256]{1,0:T(8,128)S(1)} %collective-permute-done.10.rest_2_), channel_id=1, source_target_pairs={{0,1},{1,0},{2,3},{3,2},{4,5},{5,4},{6,7},{7,6},{8,9},{9,8},{10,11... | collective-permute-start | bytes 393224 | tf_op jit(solution)/shard_map/ppermute | solution.py:279
  32.3 1.3 %collective-permute-start.13 = (f32[128,256]{1,0:T(8,128)S(1)}, f32[128,256]{1,0:T(8,128)S(1)}, u32[]{:S(2)}, u32[]{:S(2)}) collective-permute-start(f32[128,256]{1,0:T(8,128)S(1)} %collective-permute-done.12.rest_4_), channel_id=1, source_target_pairs={{0,1},{1,0},{2,3},{3,2},{4,5},{5,4},{6,7},{7,6},{8,9},{9,8},{10,11... | collective-permute-start | bytes 393224 | tf_op jit(solution)/shard_map/ppermute | solution.py:279
  32.3 1.5 %collective-permute-start.15 = (f32[128,256]{1,0:T(8,128)S(1)}, f32[128,256]{1,0:T(8,128)S(1)}, u32[]{:S(2)}, u32[]{:S(2)}) collective-permute-start(f32[128,256]{1,0:T(8,128)S(1)} %collective-permute-done.14.rest_6_), channel_id=1, source_target_pairs={{0,1},{1,0},{2,3},{3,2},{4,5},{5,4},{6,7},{7,6},{8,9},{9,8},{10,11... | collective-permute-start | bytes 393224 | tf_op jit(solution)/shard_map/ppermute | solution.py:279

commit v5 on v4

--- a/solution.py
+++ b/solution.py
@@ -106,7 +106,7 @@
 
 
 def query_kernel(core_ref, core_other, *refs):
-    tails, others, out_ref = refs[: len(refs) // 2], refs[len(refs) // 2 : -1], refs[-1]
+    others, tails, out_ref = refs[: len(refs) // 2], refs[len(refs) // 2 : -1], refs[-1]
     depth = tails[0].shape[0]
     total = None
     for core, parts in ((core_ref, tails), (core_other, others)):
@@ -156,6 +156,11 @@
             label = jnp.where(s == o % 2, mine, other)
             resid[k * block : (k + 1) * block, lanes] = times * prob[k * block : (k + 1) * block, lanes] - label
     resid_parts = split(resid[...])
+    starts = [k * block + t * chunk for k in range(2)]
+    for j in range(1, wide // 2):
+        starts += [(2 * j + 1 - s) * block + part * rows + (t ^ s) * chunk for part in range(2)]
+    picked = [resid[pl.ds(pl.multiple_of(start, chunk), chunk), :] for start in starts]
+    head_sum = dot3(split(jnp.concatenate(picked, axis=0)), query, NT)
     outer[...] = dot3(head_parts, resid_parts, TN)
     turned[...] = resid[...].T
     tail_rows = width // wide
@@ -164,11 +169,6 @@
     mixed = dot3(split(jnp.concatenate([window(turned, index, tail_rows) for index in asked], axis=0)), head_parts, NN)
     tails = dot3(split(mixed), split(core_ref[0]), NN)
     tails_other = dot3(split(mixed[2 * pitch :]), split(core_other[0]), NN)
-    starts = [k * block + t * chunk for k in range(2)]
-    for j in range(1, wide // 2):
-        starts += [(2 * j + 1 - s) * block + part * rows + (t ^ s) * chunk for part in range(2)]
-    picked = [resid[pl.ds(pl.multiple_of(start, chunk), chunk), :] for start in starts]
-    head_sum = dot3(split(jnp.concatenate(picked, axis=0)), query, NT)
     core_rows = dim // wide
     span = core_rows // 2
 
@@ -240,11 +240,11 @@
         total = total + ref[at : at + tail_rows, :]
     tail_out[0] = total * scales[1]
     tails = split(jnp.concatenate([tail_ref[...]] + [x[0:depth, :] for x in x_refs], axis=0))
-    for i in range(each):
-        core_out[i] = dot3(split(pieces[i]), tails, NN) * scales[2]
-
-
-def call(kernel, inputs, outputs, scratch=(), hbm=(), flops=0, limit=VMEM_LIMIT):
+    whole = pieces[...].reshape(each * core_rows, cols * depth)
+    core_out[...] = (dot3(split(whole), tails, NN) * scales[2]).reshape(each, core_rows, half)
+
+
+def call(kernel, inputs, outputs, scratch=(), hbm=(), flops=0, limit=VMEM_LIMIT, traffic=None):
     vmem, far = pl.BlockSpec(memory_space=pltpu.VMEM), pl.BlockSpec(memory_space=pltpu.HBM)
     return pl.pallas_call(
         kernel,
@@ -253,7 +253,7 @@
         out_specs=tuple(vmem for _ in outputs),
         scratch_shapes=[pltpu.VMEM(item, F32) if isinstance(item, tuple) else item for item in scratch],
         compiler_params=pltpu.CompilerParams(vmem_limit_bytes=limit),
-        cost_estimate=pl.CostEstimate(flops=flops, bytes_accessed=4 * sum(x.size for x in inputs), transcendentals=0),
+        cost_estimate=pl.CostEstimate(flops=flops, bytes_accessed=4 * sum(x.size for x in inputs) if traffic is None else traffic, transcendentals=0),
     )(*inputs)
 
 
@@ -308,8 +308,9 @@
     x_other = [move(value, 0, flip=1) for value in ready]
     (query,) = call(
         query_kernel,
-        (core_mats, core_other, tail_embed, *x_in, tail_other, *x_other),
+        (core_mats, core_other, tail_other, *x_other, tail_embed, *x_in),
         [(dim, cols * depth)],
+        traffic=0,
     )
     for k in order:
         ready = z_in[k]
@@ -362,18 +363,17 @@
     )
     each = wide // cols
 
-    def finish(tail_ref, *rest):
-        x_refs, rest = rest[: cols - 1], rest[cols - 1 :]
-        own_ref, rest = rest[0], rest[1:]
+    def finish(own_ref, *rest):
         far_s, rest = rest[: 2 * len(pairs)], rest[2 * len(pairs) :]
         joint_refs, rest = rest[:2], rest[2:]
         far_u, rest = rest[: 2 * len(pairs)], rest[2 * len(pairs) :]
+        tail_ref, x_refs, rest = rest[0], rest[1:cols], rest[cols:]
         fars = [far_u[2 * i : 2 * i + 2] + far_s[2 * i : 2 * i + 2] for i in range(len(pairs))]
         finish_kernel(wide, cols, scales, tail_ref, x_refs, own_ref, joint_refs, fars, *rest)
 
     return call(
         finish,
-        (tail_embed, *x_in, own, *[v for g in far for v in g[2:]], joint, joint_swap, *[v for g in far for v in g[:2]]),
+        (own, *[v for g in far for v in g[2:]], joint, joint_swap, *[v for g in far for v in g[:2]], tail_embed, *x_in),
         [(chunk, dim), (1, tail_rows, half), (each, core_rows, half)],
         scratch=[(each, core_rows, cols * depth)],
         flops=6 * each * core_rows * cols * depth * half,

time: 35 us -> 34.9 us (level)
  no operation moved by 1% of the time
where the time goes in v5:
time: 34.9 us; the launch traced here: 34.7 us
  starting transfers between devices  15.9 us (46%)
  waiting for transfers between devices  12.6 us (36%)
  Pallas kernels  5.52 us (16%)
  between operations  0.72 us (2%)
    ppermute x16, starting transfers between devices, move(): return lax.ppermute(value, axes, pairs)  15.9 us
    ppermute x16, waiting for transfers between devices, move(): return lax.ppermute(value, axes, pairs)  12.6 us
    pallas_call x4, Pallas kernels, call(): pl.pallas_call(kernel, out_shape=tuple((jax.ShapeDtypeStruct(shape, F32)...  5.52 us
  transfers between devices with their start and end apart: 16, of which 8 were waited for; matrix products, arithmetic and copies ran while one was open for 0% of the time, Pallas kernels for 9%

profile of v5, /device:TPU:0, one launch (start us, length us, event | category | flops | bytes accessed | tf_op | source)
XLA Modules:
  0.0 34.7 jit_solution(6411962714727160806)
XLA Ops:
  0.7 0.5 %collective-permute-start = (f32[1,512,256]{2,1,0:T(8,128)}, f32[1,512,256]{2,1,0:T(8,128)S(1)}, u32[]{:S(2)}, u32[]{:S(2)}) collective-permute-start(f32[1,512,256]{2,1,0:T(8,128)} %core_ref.3), channel_id=1, source_target_pairs={{0,1},{1,0},{2,3},{3,2},{4,5},{5,4},{6,7},{7,6},{8,9},{9,8},{10,11... | collective-permute-start | bytes 1572872 | tf_op jit(solution)/shard_map/ppermute | solution.py:279
  1.2 2.5 %shard_map.76 = (f32[64,384]{1,0:T(8,128)}, f32[64,384]{1,0:T(8,128)}, f32[64,384]{1,0:T(8,128)}, f32[168,256]{1,0:T(8,128)}, f32[64,512]{1,0:T(8,128)}, /*index=5*/f32[72,128]{1,0:T(8,128)}) custom-call(s32[1,8]{1,0:T(1,128)} %list_hbm.1, s32[64,8,128]{2,1,0:T(8,128)} %label_hbm.1, f32[64,512]{1,0:T(8,128)} %head_hbm.1, f32[128,256]{1,0:T(8,128)} %rest_6_.1, ...), custom_call_target="tpu_custom_call" | custom-call | bytes 1048608 | tf_op jit(solution)/shard_map/pallas_call | solution.py:249
  3.6 2.6 %collective-permute-start.2 = (f32[168,256]{1,0:T(8,128)}, f32[168,256]{1,0:T(8,128)S(1)}, u32[]{:S(2)}, u32[]{:S(2)}) collective-permute-start(f32[168,256]{1,0:T(8,128)} %get-tuple-element.16), channel_id=1, source_target_pairs={{0,2},{1,3},{2,0},{3,1},{4,6},{5,7},{6,4},{7,5},{8,10},{9,11},{10,... | collective-permute-start | bytes 516104 | tf_op jit(solution)/shard_map/ppermute | solution.py:279
  6.3 3.6 %collective-permute-start.3 = (f32[64,384]{1,0:T(8,128)}, f32[64,384]{1,0:T(8,128)S(1)}, u32[]{:S(2)}, u32[]{:S(2)}) collective-permute-start(f32[64,384]{1,0:T(8,128)} %get-tuple-element.17), channel_id=1, source_target_pairs={{0,12},{1,15},{2,14},{3,13},{4,8},{5,11},{6,10},{7,9},{8,4},{9,7},... | collective-permute-start | bytes 294920 | tf_op jit(solution)/shard_map/ppermute | solution.py:279
  9.9 0.0 collective-permute-start.5
  9.9 0.8 %collective-permute-start.6 = (f32[64,384]{1,0:T(8,128)}, f32[64,384]{1,0:T(8,128)S(1)}, u32[]{:S(2)}, u32[]{:S(2)}) collective-permute-start(f32[64,384]{1,0:T(8,128)} %get-tuple-element.22), channel_id=1, source_target_pairs={{0,8},{1,11},{2,10},{3,9},{4,12},{5,15},{6,14},{7,13},{8,0},{9,3},... | collective-permute-start | bytes 294920 | tf_op jit(solution)/shard_map/ppermute | solution.py:279
  10.7 3.3 %collective-permute-done.3.rest_1_ = f32[64,384]{1,0:T(8,128)S(1)} collective-permute-done((f32[64,384]{1,0:T(8,128)}, f32[64,384]{1,0:T(8,128)S(1)}, u32[]{:S(2)}, u32[]{:S(2)}) %collective-permute-start.3) | collective-permute-done | bytes 98336 | tf_op jit(solution)/shard_map/ppermute | solution.py:279
  14.0 0.5 %collective-permute-start.1 = (f32[128,256]{1,0:T(8,128)S(1)}, f32[128,256]{1,0:T(8,128)S(1)}, u32[]{:S(2)}, u32[]{:S(2)}) collective-permute-start(f32[128,256]{1,0:T(8,128)S(1)} %copy-done.1), channel_id=1, source_target_pairs={{0,1},{1,0},{2,3},{3,2},{4,5},{5,4},{6,7},{7,6},{8,9},{9,8},{10,11... | collective-permute-start | bytes 393224 | tf_op jit(solution)/shard_map/ppermute | solution.py:279
  14.5 0.1 collective-permute-start.7
  14.5 2.4 %collective-permute-done.5.rest_2_ = f32[64,384]{1,0:T(8,128)S(1)} collective-permute-done((f32[64,384]{1,0:T(8,128)}, f32[64,384]{1,0:T(8,128)S(1)}, u32[]{:S(2)}, u32[]{:S(2)}) %collective-permute-start.5) | collective-permute-done | bytes 98336 | tf_op jit(solution)/shard_map/ppermute | solution.py:279
  17.0 1.7 %collective-permute-done.6.rest_3_ = f32[64,384]{1,0:T(8,128)S(1)} collective-permute-done((f32[64,384]{1,0:T(8,128)}, f32[64,384]{1,0:T(8,128)S(1)}, u32[]{:S(2)}, u32[]{:S(2)}) %collective-permute-start.6) | collective-permute-done | bytes 98336 | tf_op jit(solution)/shard_map/ppermute | solution.py:279
  18.7 0.6 %collective-permute-start.9 = (f32[64,384]{1,0:T(8,128)S(1)}, f32[64,384]{1,0:T(8,128)S(1)}, u32[]{:S(2)}, u32[]{:S(2)}) collective-permute-start(f32[64,384]{1,0:T(8,128)S(1)} %collective-permute-done.6.rest_3_), channel_id=1, source_target_pairs={{0,1},{1,0},{2,3},{3,2},{4,5},{5,4},{6,7},{7,6},{8,9},{9,8},{10,11... | collective-permute-start | bytes 294920 | tf_op jit(solution)/shard_map/ppermute | solution.py:279
  19.3 0.6 %shard_map.77.query_ref = f32[512,256]{1,0:T(8,128)S(1)} custom-call(f32[1,512,256]{2,1,0:T(8,128)S(1)} %copy-done, f32[1,512,256]{2,1,0:T(8,128)S(1)} %collective-permute-done.core_other.other_ref, f32[128,256]{1,0:T(8,128)S(1)} %collective-permute-done.1.refs_0_, f32[168,256]{1,0:T(8,128)S(1)} %collective-permute-done.4.refs_1_, f32[128,256]{1,0:T(8,128)S(1)} %copy-done.1, ...), custom_call_target="tpu_custom_call" | custom-call | tf_op jit(solution)/shard_map/pallas_call | solution.py:249
  19.9 0.3 collective-permute-done.9.rest_6_
  20.2 1.4 %shard_map.78 = (f32[192,256]{1,0:T(8,128)S(1)}, f32[128,256]{1,0:T(8,128)S(1)}, f32[128,256]{1,0:T(8,128)S(1)}, f32[128,256]{1,0:T(8,128)S(1)}) custom-call(f32[1,512,256]{2,1,0:T(8,128)S(1)} %copy-done, f32[1,512,256]{2,1,0:T(8,128)S(1)} %collective-permute-done.core_other.other_ref, f32[512,256]{1,0:T(8,128)S(1)} %shard_map.77.query_ref, ...), custom_call_target="tpu_custom_call" | custom-call | flops 402653184 | bytes 2502656 | tf_op jit(solution)/shard_map/pallas_call | solution.py:249
  21.6 2.5 %collective-permute-start.10 = (f32[128,256]{1,0:T(8,128)S(1)}, f32[128,256]{1,0:T(8,128)S(1)}, u32[]{:S(2)}, u32[]{:S(2)}) collective-permute-start(f32[128,256]{1,0:T(8,128)S(1)} %get-tuple-element.24), channel_id=1, source_target_pairs={{0,12},{1,11},{2,14},{3,9},{4,8},{5,15},{6,10},{7,13},{8,4},{9,3},... | collective-permute-start | bytes 393224 | tf_op jit(solution)/shard_map/ppermute | solution.py:279
  24.1 3.2 %collective-permute-start.14 = (f32[128,256]{1,0:T(8,128)S(1)}, f32[128,256]{1,0:T(8,128)S(1)}, u32[]{:S(2)}, u32[]{:S(2)}) collective-permute-start(f32[128,256]{1,0:T(8,128)S(1)} %get-tuple-element.26), channel_id=1, source_target_pairs={{0,12},{3,9},{4,8},{7,13},{9,3},{10,6},{13,7},{14,2},{16,28},{19,2... | collective-permute-start | bytes 393224 | tf_op jit(solution)/shard_map/ppermute | solution.py:279
  27.4 2.3 %collective-permute-done.10.rest_0_ = f32[128,256]{1,0:T(8,128)S(1)} collective-permute-done((f32[128,256]{1,0:T(8,128)S(1)}, f32[128,256]{1,0:T(8,128)S(1)}, u32[]{:S(2)}, u32[]{:S(2)}) %collective-permute-start.10) | collective-permute-done | bytes 131104 | tf_op jit(solution)/shard_map/ppermute | solution.py:279
  29.7 0.9 %collective-permute-start.11 = (f32[128,256]{1,0:T(8,128)S(1)}, f32[128,256]{1,0:T(8,128)S(1)}, u32[]{:S(2)}, u32[]{:S(2)}) collective-permute-start(f32[128,256]{1,0:T(8,128)S(1)} %collective-permute-done.10.rest_0_), channel_id=1, source_target_pairs={{0,1},{1,0},{2,3},{3,2},{4,5},{5,4},{6,7},{7,6},{8,9},{9,8},{10,11... | collective-permute-start | bytes 393224 | tf_op jit(solution)/shard_map/ppermute | solution.py:279
  30.6 1.5 %collective-permute-done.12.rest_2_ = f32[128,256]{1,0:T(8,128)S(1)} collective-permute-done((f32[128,256]{1,0:T(8,128)S(1)}, f32[128,256]{1,0:T(8,128)S(1)}, u32[]{:S(2)}, u32[]{:S(2)}) %collective-permute-start.12) | collective-permute-done | bytes 131104 | tf_op jit(solution)/shard_map/ppermute | solution.py:279
  32.1 0.5 %collective-permute-start.15 = (f32[128,256]{1,0:T(8,128)S(1)}, f32[128,256]{1,0:T(8,128)S(1)}, u32[]{:S(2)}, u32[]{:S(2)}) collective-permute-start(f32[128,256]{1,0:T(8,128)S(1)} %collective-permute-done.14.rest_4_), channel_id=1, source_target_pairs={{0,1},{1,0},{2,3},{3,2},{4,5},{5,4},{6,7},{7,6},{8,9},{9,8},{10,11... | collective-permute-start | bytes 393224 | tf_op jit(solution)/shard_map/ppermute | solution.py:279
  32.6 0.8 %collective-permute-done.13.rest_3_ = f32[128,256]{1,0:T(8,128)S(1)} collective-permute-done((f32[128,256]{1,0:T(8,128)S(1)}, f32[128,256]{1,0:T(8,128)S(1)}, u32[]{:S(2)}, u32[]{:S(2)}) %collective-permute-start.13) | collective-permute-done | bytes 131104 | tf_op jit(solution)/shard_map/ppermute | solution.py:279
  33.5 0.2 collective-permute-done.15.rest_5_
  33.7 1.0 %shard_map.79 = (f32[16,512]{1,0:T(8,128)}, f32[1,32,256]{2,1,0:T(8,128)}, f32[2,128,256]{2,1,0:T(8,128)}) custom-call(f32[192,256]{1,0:T(8,128)S(1)} %get-tuple-element.23.own_ref, f32[128,256]{1,0:T(8,128)S(1)} %collective-permute-done.10.rest_0_, f32[128,256]{1,0:T(8,128)S(1)} %collective-permute-done.11.rest_1_, ...), custom_call_target="tpu_custom_call" | custom-call | flops 100663296 | bytes 1286144 | tf_op jit(solution)/shard_map/pallas_call | solution.py:249
  (20 shorter events, 0.0 us)
Async XLA Ops:
  0.6 18.6 %copy-start = (f32[1,512,256]{2,1,0:T(8,128)S(1)}, f32[1,512,256]{2,1,0:T(8,128)}, u32[]{:S(2)}) copy-start(f32[1,512,256]{2,1,0:T(8,128)} %core_ref.3) | copy-start | bytes 1572868
  0.6 13.3 %copy-start.1 = (f32[128,256]{1,0:T(8,128)S(1)}, f32[128,256]{1,0:T(8,128)}, u32[]{:S(2)}) copy-start(f32[128,256]{1,0:T(8,128)} %rest_6_.1) | copy-start | bytes 393220
  0.7 13.3 %collective-permute-start = (f32[1,512,256]{2,1,0:T(8,128)}, f32[1,512,256]{2,1,0:T(8,128)S(1)}, u32[]{:S(2)}, u32[]{:S(2)}) collective-permute-start(f32[1,512,256]{2,1,0:T(8,128)} %core_ref.3), channel_id=1, source_target_pairs={{0,1},{1,0},{2,3},{3,2},{4,5},{5,4},{6,7},{7,6},{8,9},{9,8},{10,11... | collective-permute-start | bytes 1572872 | tf_op jit(solution)/shard_map/ppermute | solution.py:279
  3.6 10.3 %collective-permute-start.2 = (f32[168,256]{1,0:T(8,128)}, f32[168,256]{1,0:T(8,128)S(1)}, u32[]{:S(2)}, u32[]{:S(2)}) collective-permute-start(f32[168,256]{1,0:T(8,128)} %get-tuple-element.16), channel_id=1, source_target_pairs={{0,2},{1,3},{2,0},{3,1},{4,6},{5,7},{6,4},{7,5},{8,10},{9,11},{10,... | collective-permute-start | bytes 516104 | tf_op jit(solution)/shard_map/ppermute | solution.py:279
  6.3 7.7 %collective-permute-start.3 = (f32[64,384]{1,0:T(8,128)}, f32[64,384]{1,0:T(8,128)S(1)}, u32[]{:S(2)}, u32[]{:S(2)}) collective-permute-start(f32[64,384]{1,0:T(8,128)} %get-tuple-element.17), channel_id=1, source_target_pairs={{0,12},{1,15},{2,14},{3,13},{4,8},{5,11},{6,10},{7,9},{8,4},{9,7},... | collective-permute-start | bytes 294920 | tf_op jit(solution)/shard_map/ppermute | solution.py:279
  9.9 7.1 %collective-permute-start.5 = (f32[64,384]{1,0:T(8,128)}, f32[64,384]{1,0:T(8,128)S(1)}, u32[]{:S(2)}, u32[]{:S(2)}) collective-permute-start(f32[64,384]{1,0:T(8,128)} %get-tuple-element.21), channel_id=1, source_target_pairs={{0,4},{1,7},{2,6},{3,5},{4,0},{5,3},{6,2},{7,1},{8,12},{9,15},{10,... | collective-permute-start | bytes 294920 | tf_op jit(solution)/shard_map/ppermute | solution.py:279
  9.9 10.3 %copy-start.2 = (f32[64,512]{1,0:T(8,128)S(1)}, f32[64,512]{1,0:T(8,128)}, u32[]{:S(2)}) copy-start(f32[64,512]{1,0:T(8,128)} %get-tuple-element.19.head_ref) | copy-start | bytes 393220
  9.9 10.3 %copy-start.3 = (f32[72,128]{1,0:T(8,128)S(1)}, f32[72,128]{1,0:T(8,128)}, u32[]{:S(2)}) copy-start(f32[72,128]{1,0:T(8,128)} %get-tuple-element.20.label_ref) | copy-start | bytes 110596
  9.9 8.8 %collective-permute-start.6 = (f32[64,384]{1,0:T(8,128)}, f32[64,384]{1,0:T(8,128)S(1)}, u32[]{:S(2)}, u32[]{:S(2)}) collective-permute-start(f32[64,384]{1,0:T(8,128)} %get-tuple-element.22), channel_id=1, source_target_pairs={{0,8},{1,11},{2,10},{3,9},{4,12},{5,15},{6,14},{7,13},{8,0},{9,3},... | collective-permute-start | bytes 294920 | tf_op jit(solution)/shard_map/ppermute | solution.py:279
  14.0 5.3 %collective-permute-start.4 = (f32[168,256]{1,0:T(8,128)S(1)}, f32[168,256]{1,0:T(8,128)S(1)}, u32[]{:S(2)}, u32[]{:S(2)}) collective-permute-start(f32[168,256]{1,0:T(8,128)S(1)} %collective-permute-done.2.refs_3_.rest_0_.rest_7_), channel_id=1, source_target_pairs={{0,1},{1,0},{2,3},{3,2},{4,5},{5,4},{6,7},{7,6},{8,9},{9,8},{10,11... | collective-permute-start | bytes 516104 | tf_op jit(solution)/shard_map/ppermute | solution.py:279
  14.0 5.3 %collective-permute-start.1 = (f32[128,256]{1,0:T(8,128)S(1)}, f32[128,256]{1,0:T(8,128)S(1)}, u32[]{:S(2)}, u32[]{:S(2)}) collective-permute-start(f32[128,256]{1,0:T(8,128)S(1)} %copy-done.1), channel_id=1, source_target_pairs={{0,1},{1,0},{2,3},{3,2},{4,5},{5,4},{6,7},{7,6},{8,9},{9,8},{10,11... | collective-permute-start | bytes 393224 | tf_op jit(solution)/shard_map/ppermute | solution.py:279
  14.5 5.4 %collective-permute-start.7 = (f32[64,384]{1,0:T(8,128)S(1)}, f32[64,384]{1,0:T(8,128)S(1)}, u32[]{:S(2)}, u32[]{:S(2)}) collective-permute-start(f32[64,384]{1,0:T(8,128)S(1)} %collective-permute-done.3.rest_1_), channel_id=1, source_target_pairs={{0,1},{1,0},{2,3},{3,2},{4,5},{5,4},{6,7},{7,6},{8,9},{9,8},{10,11... | collective-permute-start | bytes 294920 | tf_op jit(solution)/shard_map/ppermute | solution.py:279
  17.0 3.0 %collective-permute-start.8 = (f32[64,384]{1,0:T(8,128)S(1)}, f32[64,384]{1,0:T(8,128)S(1)}, u32[]{:S(2)}, u32[]{:S(2)}) collective-permute-start(f32[64,384]{1,0:T(8,128)S(1)} %collective-permute-done.5.rest_2_), channel_id=1, source_target_pairs={{0,1},{1,0},{2,3},{3,2},{4,5},{5,4},{6,7},{7,6},{8,9},{9,8},{10,11... | collective-permute-start | bytes 294920 | tf_op jit(solution)/shard_map/ppermute | solution.py:279
  18.7 1.5 %collective-permute-start.9 = (f32[64,384]{1,0:T(8,128)S(1)}, f32[64,384]{1,0:T(8,128)S(1)}, u32[]{:S(2)}, u32[]{:S(2)}) collective-permute-start(f32[64,384]{1,0:T(8,128)S(1)} %collective-permute-done.6.rest_3_), channel_id=1, source_target_pairs={{0,1},{1,0},{2,3},{3,2},{4,5},{5,4},{6,7},{7,6},{8,9},{9,8},{10,11... | collective-permute-start | bytes 294920 | tf_op jit(solution)/shard_map/ppermute | solution.py:279
  21.6 8.1 %collective-permute-start.10 = (f32[128,256]{1,0:T(8,128)S(1)}, f32[128,256]{1,0:T(8,128)S(1)}, u32[]{:S(2)}, u32[]{:S(2)}) collective-permute-start(f32[128,256]{1,0:T(8,128)S(1)} %get-tuple-element.24), channel_id=1, source_target_pairs={{0,12},{1,11},{2,14},{3,9},{4,8},{5,15},{6,10},{7,13},{8,4},{9,3},... | collective-permute-start | bytes 393224 | tf_op jit(solution)/shard_map/ppermute | solution.py:279
  24.1 8.0 %collective-permute-start.12 = (f32[128,256]{1,0:T(8,128)S(1)}, f32[128,256]{1,0:T(8,128)S(1)}, u32[]{:S(2)}, u32[]{:S(2)}) collective-permute-start(f32[128,256]{1,0:T(8,128)S(1)} %get-tuple-element.25), channel_id=1, source_target_pairs={{0,4},{1,5},{2,6},{3,7},{4,0},{5,1},{6,2},{7,3},{8,12},{9,13},{10,... | collective-permute-start | bytes 393224 | tf_op jit(solution)/shard_map/ppermute | solution.py:279
  24.1 8.0 %collective-permute-start.14 = (f32[128,256]{1,0:T(8,128)S(1)}, f32[128,256]{1,0:T(8,128)S(1)}, u32[]{:S(2)}, u32[]{:S(2)}) collective-permute-start(f32[128,256]{1,0:T(8,128)S(1)} %get-tuple-element.26), channel_id=1, source_target_pairs={{0,12},{3,9},{4,8},{7,13},{9,3},{10,6},{13,7},{14,2},{16,28},{19,2... | collective-permute-start | bytes 393224 | tf_op jit(solution)/shard_map/ppermute | solution.py:279
  29.7 2.9 %collective-permute-start.11 = (f32[128,256]{1,0:T(8,128)S(1)}, f32[128,256]{1,0:T(8,128)S(1)}, u32[]{:S(2)}, u32[]{:S(2)}) collective-permute-start(f32[128,256]{1,0:T(8,128)S(1)} %collective-permute-done.10.rest_0_), channel_id=1, source_target_pairs={{0,1},{1,0},{2,3},{3,2},{4,5},{5,4},{6,7},{7,6},{8,9},{9,8},{10,11... | collective-permute-start | bytes 393224 | tf_op jit(solution)/shard_map/ppermute | solution.py:279
  32.1 1.3 %collective-permute-start.13 = (f32[128,256]{1,0:T(8,128)S(1)}, f32[128,256]{1,0:T(8,128)S(1)}, u32[]{:S(2)}, u32[]{:S(2)}) collective-permute-start(f32[128,256]{1,0:T(8,128)S(1)} %collective-permute-done.12.rest_2_), channel_id=1, source_target_pairs={{0,1},{1,0},{2,3},{3,2},{4,5},{5,4},{6,7},{7,6},{8,9},{9,8},{10,11... | collective-permute-start | bytes 393224 | tf_op jit(solution)/shard_map/ppermute | solution.py:279
  32.1 1.5 %collective-permute-start.15 = (f32[128,256]{1,0:T(8,128)S(1)}, f32[128,256]{1,0:T(8,128)S(1)}, u32[]{:S(2)}, u32[]{:S(2)}) collective-permute-start(f32[128,256]{1,0:T(8,128)S(1)} %collective-permute-done.14.rest_4_), channel_id=1, source_target_pairs={{0,1},{1,0},{2,3},{3,2},{4,5},{5,4},{6,7},{7,6},{8,9},{9,8},{10,11... | collective-permute-start | bytes 393224 | tf_op jit(solution)/shard_map/ppermute | solution.py:279

commit v6 on v5

--- a/solution.py
+++ b/solution.py
@@ -53,7 +53,7 @@
 
 
 def pack_kernel(wide, cols, list_hbm, label_hbm, head_hbm, tail_hbm, core_hbm, *refs):
-    z_refs, (x_ref, head_own, label_own, listed, label_ref, head_ref, sems) = refs[: wide - 1], refs[wide - 1 :]
+    z_refs, (x_ref, label_own, listed, label_ref, head_ref, sems) = refs[: wide - 1], refs[wide - 1 :]
     w, t, s = place()
     block, slots, width = label_ref.shape
     chunk = block // (2 * cols)
@@ -85,7 +85,6 @@
             start = pl.multiple_of((col * 2 + (s ^ part)) * chunk, chunk)
             at = part * rows + col * chunk
             embed = head_ref[pl.ds(start, chunk), :]
-            head_own[at : at + chunk, :] = embed
             slot_labels = [label_ref[pl.ds(start, chunk), j, :] for j in range(slots)]
             for k in range(wide):
                 total = jnp.zeros((chunk, width), jnp.int32)
@@ -125,7 +124,10 @@
     rows = block // 2
     chunk = rows // cols
     half = core_ref.shape[2]
-    heads[0:block, :] = head_own[...]
+    for i in range(2 * cols):
+        part, col = divmod(i, cols)
+        start = pl.multiple_of((col * 2 + (s ^ part)) * chunk, chunk)
+        heads[i * chunk : (i + 1) * chunk, :] = head_own[pl.ds(start, chunk), :]
     for k in range(1, wide):
         at = k * block
         for part, ref in enumerate((z_refs[k - 1][0], swap_refs[k - 1][0])):
@@ -284,7 +286,7 @@
         functools.partial(pack_kernel, wide, cols),
         (core_lists, labels, head_embed, tail_embed, core_mats),
         [(block, half + depth)] * (wide - 1)
-        + [(depth + rows + 8, half), (block, dim), (block + 8, depth)],
+        + [(depth + rows + 8, half), (block + 8, depth)],
         scratch=[
             pltpu.SMEM(core_lists.shape, jnp.int32),
             pltpu.VMEM(labels.shape, jnp.int32),
@@ -294,7 +296,7 @@
         hbm=range(5),
         limit=FULL_LIMIT,
     )
-    z_out, (x_out, head_own, label_own) = packed[: wide - 1], packed[wide - 1 :]
+    z_out, (x_out, label_own) = packed[: wide - 1], packed[wide - 1 :]
     z_in, z_swap = {}, {}
     for k in order:
         got = []
@@ -341,7 +343,7 @@
 
     made = call(
         grads,
-        (core_mats, core_other, query, head_own, label_own, *x_in, *flat_in, *flat_swap),
+        (core_mats, core_other, query, head_embed, label_own, *x_in, *flat_in, *flat_swap),
         [own_shape, joint_shape] + [(chunks * core_rows, half), (2 * small, half)] * len(pairs),
         scratch=[
             (wide * block, dim), (wide * block, cols * depth), (dim, cols * depth), (cols * depth, wide * block),

time: 34.9 us -> 34.8 us (level)
  no operation moved by 1% of the time
where the time goes in v6:
time: 34.8 us; the launch traced here: 34.7 us
  starting transfers between devices  15.9 us (46%)
  waiting for transfers between devices  12.6 us (36%)
  Pallas kernels  5.47 us (16%)
  between operations  0.72 us (2%)
    ppermute x16, starting transfers between devices, move(): return lax.ppermute(value, axes, pairs)  15.9 us
    ppermute x16, waiting for transfers between devices, move(): return lax.ppermute(value, axes, pairs)  12.6 us
    pallas_call x4, Pallas kernels, call(): pl.pallas_call(kernel, out_shape=tuple((jax.ShapeDtypeStruct(shape, F32)...  5.47 us
  transfers between devices with their start and end apart: 16, of which 8 were waited for; matrix products, arithmetic and copies ran while one was open for 0% of the time, Pallas kernels for 9%

profile of v6, /device:TPU:0, one launch (start us, length us, event | category | flops | bytes accessed | tf_op | source)
XLA Modules:
  0.0 34.7 jit_solution(10441819205035371853)
XLA Ops:
  0.7 0.5 %collective-permute-start = (f32[1,512,256]{2,1,0:T(8,128)}, f32[1,512,256]{2,1,0:T(8,128)S(1)}, u32[]{:S(2)}, u32[]{:S(2)}) collective-permute-start(f32[1,512,256]{2,1,0:T(8,128)} %core_ref.3), channel_id=1, source_target_pairs={{0,1},{1,0},{2,3},{3,2},{4,5},{5,4},{6,7},{7,6},{8,9},{9,8},{10,11... | collective-permute-start | bytes 1572872 | tf_op jit(solution)/shard_map/ppermute | solution.py:281
  1.2 2.4 %shard_map.76 = (f32[64,384]{1,0:T(8,128)}, f32[64,384]{1,0:T(8,128)}, f32[64,384]{1,0:T(8,128)}, f32[168,256]{1,0:T(8,128)}, f32[72,128]{1,0:T(8,128)}) custom-call(s32[1,8]{1,0:T(1,128)} %list_hbm.1, s32[64,8,128]{2,1,0:T(8,128)} %label_hbm.1, f32[64,512]{1,0:T(8,128)} %head_ref.1, f32[128,256]{1,0:T(8,128)} %rest_6_.1, f32[1,512,256]{2,1,0:T(8,128)} %core_ref.3), custom_call_target="tpu_custom_call" | custom-call | bytes 1048608 | tf_op jit(solution)/shard_map/pallas_call | solution.py:251
  3.6 2.6 %collective-permute-start.2 = (f32[168,256]{1,0:T(8,128)}, f32[168,256]{1,0:T(8,128)S(1)}, u32[]{:S(2)}, u32[]{:S(2)}) collective-permute-start(f32[168,256]{1,0:T(8,128)} %get-tuple-element.15), channel_id=1, source_target_pairs={{0,2},{1,3},{2,0},{3,1},{4,6},{5,7},{6,4},{7,5},{8,10},{9,11},{10,... | collective-permute-start | bytes 516104 | tf_op jit(solution)/shard_map/ppermute | solution.py:281
  6.2 3.6 %collective-permute-start.3 = (f32[64,384]{1,0:T(8,128)}, f32[64,384]{1,0:T(8,128)S(1)}, u32[]{:S(2)}, u32[]{:S(2)}) collective-permute-start(f32[64,384]{1,0:T(8,128)} %get-tuple-element.16), channel_id=1, source_target_pairs={{0,12},{1,15},{2,14},{3,13},{4,8},{5,11},{6,10},{7,9},{8,4},{9,7},... | collective-permute-start | bytes 294920 | tf_op jit(solution)/shard_map/ppermute | solution.py:281
  9.8 0.0 collective-permute-start.5
  9.8 0.8 %collective-permute-start.6 = (f32[64,384]{1,0:T(8,128)}, f32[64,384]{1,0:T(8,128)S(1)}, u32[]{:S(2)}, u32[]{:S(2)}) collective-permute-start(f32[64,384]{1,0:T(8,128)} %get-tuple-element.20), channel_id=1, source_target_pairs={{0,8},{1,11},{2,10},{3,9},{4,12},{5,15},{6,14},{7,13},{8,0},{9,3},... | collective-permute-start | bytes 294920 | tf_op jit(solution)/shard_map/ppermute | solution.py:281
  10.6 3.3 %collective-permute-done.3.rest_1_ = f32[64,384]{1,0:T(8,128)S(1)} collective-permute-done((f32[64,384]{1,0:T(8,128)}, f32[64,384]{1,0:T(8,128)S(1)}, u32[]{:S(2)}, u32[]{:S(2)}) %collective-permute-start.3) | collective-permute-done | bytes 98336 | tf_op jit(solution)/shard_map/ppermute | solution.py:281
  13.9 0.5 %collective-permute-start.1 = (f32[128,256]{1,0:T(8,128)S(1)}, f32[128,256]{1,0:T(8,128)S(1)}, u32[]{:S(2)}, u32[]{:S(2)}) collective-permute-start(f32[128,256]{1,0:T(8,128)S(1)} %copy-done.1), channel_id=1, source_target_pairs={{0,1},{1,0},{2,3},{3,2},{4,5},{5,4},{6,7},{7,6},{8,9},{9,8},{10,11... | collective-permute-start | bytes 393224 | tf_op jit(solution)/shard_map/ppermute | solution.py:281
  14.4 0.1 collective-permute-start.7
  14.5 2.4 %collective-permute-done.5.rest_2_ = f32[64,384]{1,0:T(8,128)S(1)} collective-permute-done((f32[64,384]{1,0:T(8,128)}, f32[64,384]{1,0:T(8,128)S(1)}, u32[]{:S(2)}, u32[]{:S(2)}) %collective-permute-start.5) | collective-permute-done | bytes 98336 | tf_op jit(solution)/shard_map/ppermute | solution.py:281
  16.9 1.7 %collective-permute-done.6.rest_3_ = f32[64,384]{1,0:T(8,128)S(1)} collective-permute-done((f32[64,384]{1,0:T(8,128)}, f32[64,384]{1,0:T(8,128)S(1)}, u32[]{:S(2)}, u32[]{:S(2)}) %collective-permute-start.6) | collective-permute-done | bytes 98336 | tf_op jit(solution)/shard_map/ppermute | solution.py:281
  18.6 0.6 %collective-permute-start.9 = (f32[64,384]{1,0:T(8,128)S(1)}, f32[64,384]{1,0:T(8,128)S(1)}, u32[]{:S(2)}, u32[]{:S(2)}) collective-permute-start(f32[64,384]{1,0:T(8,128)S(1)} %collective-permute-done.6.rest_3_), channel_id=1, source_target_pairs={{0,1},{1,0},{2,3},{3,2},{4,5},{5,4},{6,7},{7,6},{8,9},{9,8},{10,11... | collective-permute-start | bytes 294920 | tf_op jit(solution)/shard_map/ppermute | solution.py:281
  19.2 0.6 %shard_map.77.query_ref = f32[512,256]{1,0:T(8,128)S(1)} custom-call(f32[1,512,256]{2,1,0:T(8,128)S(1)} %copy-done, f32[1,512,256]{2,1,0:T(8,128)S(1)} %collective-permute-done.core_other.other_ref, f32[128,256]{1,0:T(8,128)S(1)} %collective-permute-done.1.refs_0_, f32[168,256]{1,0:T(8,128)S(1)} %collective-permute-done.4.refs_1_, f32[128,256]{1,0:T(8,128)S(1)} %copy-done.1, ...), custom_call_target="tpu_custom_call" | custom-call | tf_op jit(solution)/shard_map/pallas_call | solution.py:251
  19.9 0.3 collective-permute-done.9.rest_6_
  20.2 1.4 %shard_map.78 = (f32[192,256]{1,0:T(8,128)S(1)}, f32[128,256]{1,0:T(8,128)S(1)}, f32[128,256]{1,0:T(8,128)S(1)}, f32[128,256]{1,0:T(8,128)S(1)}) custom-call(f32[1,512,256]{2,1,0:T(8,128)S(1)} %copy-done, f32[1,512,256]{2,1,0:T(8,128)S(1)} %collective-permute-done.core_other.other_ref, f32[512,256]{1,0:T(8,128)S(1)} %shard_map.77.query_ref, ...), custom_call_target="tpu_custom_call" | custom-call | flops 402653184 | bytes 2502656 | tf_op jit(solution)/shard_map/pallas_call | solution.py:251
  21.6 2.5 %collective-permute-start.10 = (f32[128,256]{1,0:T(8,128)S(1)}, f32[128,256]{1,0:T(8,128)S(1)}, u32[]{:S(2)}, u32[]{:S(2)}) collective-permute-start(f32[128,256]{1,0:T(8,128)S(1)} %get-tuple-element.22), channel_id=1, source_target_pairs={{0,12},{1,11},{2,14},{3,9},{4,8},{5,15},{6,10},{7,13},{8,4},{9,3},... | collective-permute-start | bytes 393224 | tf_op jit(solution)/shard_map/ppermute | solution.py:281
  24.1 3.2 %collective-permute-start.14 = (f32[128,256]{1,0:T(8,128)S(1)}, f32[128,256]{1,0:T(8,128)S(1)}, u32[]{:S(2)}, u32[]{:S(2)}) collective-permute-start(f32[128,256]{1,0:T(8,128)S(1)} %get-tuple-element.24), channel_id=1, source_target_pairs={{0,12},{3,9},{4,8},{7,13},{9,3},{10,6},{13,7},{14,2},{16,28},{19,2... | collective-permute-start | bytes 393224 | tf_op jit(solution)/shard_map/ppermute | solution.py:281
  27.4 2.3 %collective-permute-done.10.rest_0_ = f32[128,256]{1,0:T(8,128)S(1)} collective-permute-done((f32[128,256]{1,0:T(8,128)S(1)}, f32[128,256]{1,0:T(8,128)S(1)}, u32[]{:S(2)}, u32[]{:S(2)}) %collective-permute-start.10) | collective-permute-done | bytes 131104 | tf_op jit(solution)/shard_map/ppermute | solution.py:281
  29.7 0.9 %collective-permute-start.11 = (f32[128,256]{1,0:T(8,128)S(1)}, f32[128,256]{1,0:T(8,128)S(1)}, u32[]{:S(2)}, u32[]{:S(2)}) collective-permute-start(f32[128,256]{1,0:T(8,128)S(1)} %collective-permute-done.10.rest_0_), channel_id=1, source_target_pairs={{0,1},{1,0},{2,3},{3,2},{4,5},{5,4},{6,7},{7,6},{8,9},{9,8},{10,11... | collective-permute-start | bytes 393224 | tf_op jit(solution)/shard_map/ppermute | solution.py:281
  30.6 1.5 %collective-permute-done.12.rest_2_ = f32[128,256]{1,0:T(8,128)S(1)} collective-permute-done((f32[128,256]{1,0:T(8,128)S(1)}, f32[128,256]{1,0:T(8,128)S(1)}, u32[]{:S(2)}, u32[]{:S(2)}) %collective-permute-start.12) | collective-permute-done | bytes 131104 | tf_op jit(solution)/shard_map/ppermute | solution.py:281
  32.1 0.5 %collective-permute-start.15 = (f32[128,256]{1,0:T(8,128)S(1)}, f32[128,256]{1,0:T(8,128)S(1)}, u32[]{:S(2)}, u32[]{:S(2)}) collective-permute-start(f32[128,256]{1,0:T(8,128)S(1)} %collective-permute-done.14.rest_4_), channel_id=1, source_target_pairs={{0,1},{1,0},{2,3},{3,2},{4,5},{5,4},{6,7},{7,6},{8,9},{9,8},{10,11... | collective-permute-start | bytes 393224 | tf_op jit(solution)/shard_map/ppermute | solution.py:281
  32.6 0.8 %collective-permute-done.13.rest_3_ = f32[128,256]{1,0:T(8,128)S(1)} collective-permute-done((f32[128,256]{1,0:T(8,128)S(1)}, f32[128,256]{1,0:T(8,128)S(1)}, u32[]{:S(2)}, u32[]{:S(2)}) %collective-permute-start.13) | collective-permute-done | bytes 131104 | tf_op jit(solution)/shard_map/ppermute | solution.py:281
  33.4 0.2 collective-permute-done.15.rest_5_
  33.6 1.0 %shard_map.79 = (f32[16,512]{1,0:T(8,128)}, f32[1,32,256]{2,1,0:T(8,128)}, f32[2,128,256]{2,1,0:T(8,128)}) custom-call(f32[192,256]{1,0:T(8,128)S(1)} %get-tuple-element.21.own_ref, f32[128,256]{1,0:T(8,128)S(1)} %collective-permute-done.10.rest_0_, f32[128,256]{1,0:T(8,128)S(1)} %collective-permute-done.11.rest_1_, ...), custom_call_target="tpu_custom_call" | custom-call | flops 100663296 | bytes 1286144 | tf_op jit(solution)/shard_map/pallas_call | solution.py:251
  (20 shorter events, 0.0 us)
Async XLA Ops:
  0.6 18.6 %copy-start = (f32[1,512,256]{2,1,0:T(8,128)S(1)}, f32[1,512,256]{2,1,0:T(8,128)}, u32[]{:S(2)}) copy-start(f32[1,512,256]{2,1,0:T(8,128)} %core_ref.3) | copy-start | bytes 1572868
  0.6 13.3 %copy-start.1 = (f32[128,256]{1,0:T(8,128)S(1)}, f32[128,256]{1,0:T(8,128)}, u32[]{:S(2)}) copy-start(f32[128,256]{1,0:T(8,128)} %rest_6_.1) | copy-start | bytes 393220
  0.7 13.3 %collective-permute-start = (f32[1,512,256]{2,1,0:T(8,128)}, f32[1,512,256]{2,1,0:T(8,128)S(1)}, u32[]{:S(2)}, u32[]{:S(2)}) collective-permute-start(f32[1,512,256]{2,1,0:T(8,128)} %core_ref.3), channel_id=1, source_target_pairs={{0,1},{1,0},{2,3},{3,2},{4,5},{5,4},{6,7},{7,6},{8,9},{9,8},{10,11... | collective-permute-start | bytes 1572872 | tf_op jit(solution)/shard_map/ppermute | solution.py:281
  3.6 10.3 %collective-permute-start.2 = (f32[168,256]{1,0:T(8,128)}, f32[168,256]{1,0:T(8,128)S(1)}, u32[]{:S(2)}, u32[]{:S(2)}) collective-permute-start(f32[168,256]{1,0:T(8,128)} %get-tuple-element.15), channel_id=1, source_target_pairs={{0,2},{1,3},{2,0},{3,1},{4,6},{5,7},{6,4},{7,5},{8,10},{9,11},{10,... | collective-permute-start | bytes 516104 | tf_op jit(solution)/shard_map/ppermute | solution.py:281
  6.2 7.7 %collective-permute-start.3 = (f32[64,384]{1,0:T(8,128)}, f32[64,384]{1,0:T(8,128)S(1)}, u32[]{:S(2)}, u32[]{:S(2)}) collective-permute-start(f32[64,384]{1,0:T(8,128)} %get-tuple-element.16), channel_id=1, source_target_pairs={{0,12},{1,15},{2,14},{3,13},{4,8},{5,11},{6,10},{7,9},{8,4},{9,7},... | collective-permute-start | bytes 294920 | tf_op jit(solution)/shard_map/ppermute | solution.py:281
  9.8 7.1 %collective-permute-start.5 = (f32[64,384]{1,0:T(8,128)}, f32[64,384]{1,0:T(8,128)S(1)}, u32[]{:S(2)}, u32[]{:S(2)}) collective-permute-start(f32[64,384]{1,0:T(8,128)} %get-tuple-element.19), channel_id=1, source_target_pairs={{0,4},{1,7},{2,6},{3,5},{4,0},{5,3},{6,2},{7,1},{8,12},{9,15},{10,... | collective-permute-start | bytes 294920 | tf_op jit(solution)/shard_map/ppermute | solution.py:281
  9.8 10.3 %copy-start.2 = (f32[64,512]{1,0:T(8,128)S(1)}, f32[64,512]{1,0:T(8,128)}, u32[]{:S(2)}) copy-start(f32[64,512]{1,0:T(8,128)} %head_ref.1) | copy-start | bytes 393220
  9.8 10.3 %copy-start.3 = (f32[72,128]{1,0:T(8,128)S(1)}, f32[72,128]{1,0:T(8,128)}, u32[]{:S(2)}) copy-start(f32[72,128]{1,0:T(8,128)} %get-tuple-element.18.label_ref) | copy-start | bytes 110596
  9.8 8.8 %collective-permute-start.6 = (f32[64,384]{1,0:T(8,128)}, f32[64,384]{1,0:T(8,128)S(1)}, u32[]{:S(2)}, u32[]{:S(2)}) collective-permute-start(f32[64,384]{1,0:T(8,128)} %get-tuple-element.20), channel_id=1, source_target_pairs={{0,8},{1,11},{2,10},{3,9},{4,12},{5,15},{6,14},{7,13},{8,0},{9,3},... | collective-permute-start | bytes 294920 | tf_op jit(solution)/shard_map/ppermute | solution.py:281
  13.9 5.3 %collective-permute-start.4 = (f32[168,256]{1,0:T(8,128)S(1)}, f32[168,256]{1,0:T(8,128)S(1)}, u32[]{:S(2)}, u32[]{:S(2)}) collective-permute-start(f32[168,256]{1,0:T(8,128)S(1)} %collective-permute-done.2.refs_3_.rest_0_.rest_7_), channel_id=1, source_target_pairs={{0,1},{1,0},{2,3},{3,2},{4,5},{5,4},{6,7},{7,6},{8,9},{9,8},{10,11... | collective-permute-start | bytes 516104 | tf_op jit(solution)/shard_map/ppermute | solution.py:281
  13.9 5.3 %collective-permute-start.1 = (f32[128,256]{1,0:T(8,128)S(1)}, f32[128,256]{1,0:T(8,128)S(1)}, u32[]{:S(2)}, u32[]{:S(2)}) collective-permute-start(f32[128,256]{1,0:T(8,128)S(1)} %copy-done.1), channel_id=1, source_target_pairs={{0,1},{1,0},{2,3},{3,2},{4,5},{5,4},{6,7},{7,6},{8,9},{9,8},{10,11... | collective-permute-start | bytes 393224 | tf_op jit(solution)/shard_map/ppermute | solution.py:281
  14.4 5.4 %collective-permute-start.7 = (f32[64,384]{1,0:T(8,128)S(1)}, f32[64,384]{1,0:T(8,128)S(1)}, u32[]{:S(2)}, u32[]{:S(2)}) collective-permute-start(f32[64,384]{1,0:T(8,128)S(1)} %collective-permute-done.3.rest_1_), channel_id=1, source_target_pairs={{0,1},{1,0},{2,3},{3,2},{4,5},{5,4},{6,7},{7,6},{8,9},{9,8},{10,11... | collective-permute-start | bytes 294920 | tf_op jit(solution)/shard_map/ppermute | solution.py:281
  16.9 3.0 %collective-permute-start.8 = (f32[64,384]{1,0:T(8,128)S(1)}, f32[64,384]{1,0:T(8,128)S(1)}, u32[]{:S(2)}, u32[]{:S(2)}) collective-permute-start(f32[64,384]{1,0:T(8,128)S(1)} %collective-permute-done.5.rest_2_), channel_id=1, source_target_pairs={{0,1},{1,0},{2,3},{3,2},{4,5},{5,4},{6,7},{7,6},{8,9},{9,8},{10,11... | collective-permute-start | bytes 294920 | tf_op jit(solution)/shard_map/ppermute | solution.py:281
  18.6 1.5 %collective-permute-start.9 = (f32[64,384]{1,0:T(8,128)S(1)}, f32[64,384]{1,0:T(8,128)S(1)}, u32[]{:S(2)}, u32[]{:S(2)}) collective-permute-start(f32[64,384]{1,0:T(8,128)S(1)} %collective-permute-done.6.rest_3_), channel_id=1, source_target_pairs={{0,1},{1,0},{2,3},{3,2},{4,5},{5,4},{6,7},{7,6},{8,9},{9,8},{10,11... | collective-permute-start | bytes 294920 | tf_op jit(solution)/shard_map/ppermute | solution.py:281
  21.6 8.1 %collective-permute-start.10 = (f32[128,256]{1,0:T(8,128)S(1)}, f32[128,256]{1,0:T(8,128)S(1)}, u32[]{:S(2)}, u32[]{:S(2)}) collective-permute-start(f32[128,256]{1,0:T(8,128)S(1)} %get-tuple-element.22), channel_id=1, source_target_pairs={{0,12},{1,11},{2,14},{3,9},{4,8},{5,15},{6,10},{7,13},{8,4},{9,3},... | collective-permute-start | bytes 393224 | tf_op jit(solution)/shard_map/ppermute | solution.py:281
  24.1 8.0 %collective-permute-start.12 = (f32[128,256]{1,0:T(8,128)S(1)}, f32[128,256]{1,0:T(8,128)S(1)}, u32[]{:S(2)}, u32[]{:S(2)}) collective-permute-start(f32[128,256]{1,0:T(8,128)S(1)} %get-tuple-element.23), channel_id=1, source_target_pairs={{0,4},{1,5},{2,6},{3,7},{4,0},{5,1},{6,2},{7,3},{8,12},{9,13},{10,... | collective-permute-start | bytes 393224 | tf_op jit(solution)/shard_map/ppermute | solution.py:281
  24.1 8.0 %collective-permute-start.14 = (f32[128,256]{1,0:T(8,128)S(1)}, f32[128,256]{1,0:T(8,128)S(1)}, u32[]{:S(2)}, u32[]{:S(2)}) collective-permute-start(f32[128,256]{1,0:T(8,128)S(1)} %get-tuple-element.24), channel_id=1, source_target_pairs={{0,12},{3,9},{4,8},{7,13},{9,3},{10,6},{13,7},{14,2},{16,28},{19,2... | collective-permute-start | bytes 393224 | tf_op jit(solution)/shard_map/ppermute | solution.py:281
  29.7 2.9 %collective-permute-start.11 = (f32[128,256]{1,0:T(8,128)S(1)}, f32[128,256]{1,0:T(8,128)S(1)}, u32[]{:S(2)}, u32[]{:S(2)}) collective-permute-start(f32[128,256]{1,0:T(8,128)S(1)} %collective-permute-done.10.rest_0_), channel_id=1, source_target_pairs={{0,1},{1,0},{2,3},{3,2},{4,5},{5,4},{6,7},{7,6},{8,9},{9,8},{10,11... | collective-permute-start | bytes 393224 | tf_op jit(solution)/shard_map/ppermute | solution.py:281
  32.1 1.3 %collective-permute-start.13 = (f32[128,256]{1,0:T(8,128)S(1)}, f32[128,256]{1,0:T(8,128)S(1)}, u32[]{:S(2)}, u32[]{:S(2)}) collective-permute-start(f32[128,256]{1,0:T(8,128)S(1)} %collective-permute-done.12.rest_2_), channel_id=1, source_target_pairs={{0,1},{1,0},{2,3},{3,2},{4,5},{5,4},{6,7},{7,6},{8,9},{9,8},{10,11... | collective-permute-start | bytes 393224 | tf_op jit(solution)/shard_map/ppermute | solution.py:281
  32.1 1.5 %collective-permute-start.15 = (f32[128,256]{1,0:T(8,128)S(1)}, f32[128,256]{1,0:T(8,128)S(1)}, u32[]{:S(2)}, u32[]{:S(2)}) collective-permute-start(f32[128,256]{1,0:T(8,128)S(1)} %collective-permute-done.14.rest_4_), channel_id=1, source_target_pairs={{0,1},{1,0},{2,3},{3,2},{4,5},{5,4},{6,7},{7,6},{8,9},{9,8},{10,11... | collective-permute-start | bytes 393224 | tf_op jit(solution)/shard_map/ppermute | solution.py:281

commit v7 on v6

--- a/solution.py
+++ b/solution.py
@@ -59,17 +59,11 @@
     chunk = block // (2 * cols)
     rows = block // 2
     depth, half = tail_hbm.shape
-    copies = [
-        pltpu.make_async_copy(source, target, sems.at[i])
-        for i, (source, target) in enumerate(
-            (
-                (list_hbm, listed),
-                (label_hbm, label_ref),
-                (head_hbm, head_ref),
-                (tail_hbm, x_ref.at[0:depth]),
-            )
-        )
-    ]
+    starts = [pl.multiple_of((col * 2 + (s ^ part)) * chunk, chunk) for part in range(2) for col in range(cols)]
+    rooms = [pl.ds(start, chunk) for start in starts]
+    whole = ((list_hbm, listed), (head_hbm, head_ref), (tail_hbm, x_ref.at[0:depth]))
+    sources = whole[:1] + tuple((label_hbm.at[room], label_ref.at[room]) for room in rooms) + whole[1:]
+    copies = [pltpu.make_async_copy(source, target, sems.at[i]) for i, (source, target) in enumerate(sources)]
     for copy in copies:
         copy.start()
     copies[0].wait()
@@ -78,11 +72,11 @@
         count = count + (listed[0, j] == w).astype(jnp.int32)
     x_ref[depth + rows :, :] = jnp.full((8, half), count.astype(F32), F32)
     label_own[block:, :] = jnp.full((8, width), count.astype(F32), F32)
-    copies[1].wait()
-    copies[2].wait()
+    copies[-2].wait()
     for part in range(2):
         for col in range(cols):
-            start = pl.multiple_of((col * 2 + (s ^ part)) * chunk, chunk)
+            start = starts[part * cols + col]
+            copies[1 + part * cols + col].wait()
             at = part * rows + col * chunk
             embed = head_ref[pl.ds(start, chunk), :]
             slot_labels = [label_ref[pl.ds(start, chunk), j, :] for j in range(slots)]
@@ -101,7 +95,7 @@
                     if part == 0:
                         z_refs[k - 1][at : at + chunk, 0:half] = embed[:, 0:half]
                         z_refs[k - 1][rows + at : rows + at + chunk, 0:half] = embed[:, half:]
-    copies[3].wait()
+    copies[-1].wait()
 
 
 def query_kernel(core_ref, core_other, *refs):
@@ -291,7 +285,7 @@
             pltpu.SMEM(core_lists.shape, jnp.int32),
             pltpu.VMEM(labels.shape, jnp.int32),
             head_embed.shape,
-            pltpu.SemaphoreType.DMA((4,)),
+            pltpu.SemaphoreType.DMA((3 + 2 * cols,)),
         ],
         hbm=range(5),
         limit=FULL_LIMIT,

time: 34.8 us -> 34.9 us (level)
  no operation moved by 1% of the time
where the time goes in v7:
time: 34.9 us; the launch traced here: 34.8 us
  starting transfers between devices  15.9 us (46%)
  waiting for transfers between devices  12.6 us (36%)
  Pallas kernels  5.59 us (16%)
  between operations  0.72 us (2%)
    ppermute x16, starting transfers between devices, move(): return lax.ppermute(value, axes, pairs)  15.9 us
    ppermute x16, waiting for transfers between devices, move(): return lax.ppermute(value, axes, pairs)  12.6 us
    pallas_call x4, Pallas kernels, call(): pl.pallas_call(kernel, out_shape=tuple((jax.ShapeDtypeStruct(shape, F32)...  5.59 us
  transfers between devices with their start and end apart: 16, of which 8 were waited for; matrix products, arithmetic and copies ran while one was open for 0% of the time, Pallas kernels for 9%

profile of v7, /device:TPU:0, one launch (start us, length us, event | category | flops | bytes accessed | tf_op | source)
XLA Modules:
  0.0 34.8 jit_solution(1034399482781747318)
XLA Ops:
  0.7 0.5 %collective-permute-start = (f32[1,512,256]{2,1,0:T(8,128)}, f32[1,512,256]{2,1,0:T(8,128)S(1)}, u32[]{:S(2)}, u32[]{:S(2)}) collective-permute-start(f32[1,512,256]{2,1,0:T(8,128)} %core_ref.3), channel_id=1, source_target_pairs={{0,1},{1,0},{2,3},{3,2},{4,5},{5,4},{6,7},{7,6},{8,9},{9,8},{10,11... | collective-permute-start | bytes 1572872 | tf_op jit(solution)/shard_map/ppermute | solution.py:275
  1.2 2.5 %shard_map.76 = (f32[64,384]{1,0:T(8,128)}, f32[64,384]{1,0:T(8,128)}, f32[64,384]{1,0:T(8,128)}, f32[168,256]{1,0:T(8,128)}, f32[72,128]{1,0:T(8,128)}) custom-call(s32[1,8]{1,0:T(1,128)} %list_hbm.1, s32[64,8,128]{2,1,0:T(8,128)} %label_hbm.1, f32[64,512]{1,0:T(8,128)} %head_ref.1, f32[128,256]{1,0:T(8,128)} %rest_6_.1, f32[1,512,256]{2,1,0:T(8,128)} %core_ref.3), custom_call_target="tpu_custom_call" | custom-call | bytes 1048608 | tf_op jit(solution)/shard_map/pallas_call | solution.py:245
  3.7 2.6 %collective-permute-start.2 = (f32[168,256]{1,0:T(8,128)}, f32[168,256]{1,0:T(8,128)S(1)}, u32[]{:S(2)}, u32[]{:S(2)}) collective-permute-start(f32[168,256]{1,0:T(8,128)} %get-tuple-element.15), channel_id=1, source_target_pairs={{0,2},{1,3},{2,0},{3,1},{4,6},{5,7},{6,4},{7,5},{8,10},{9,11},{10,... | collective-permute-start | bytes 516104 | tf_op jit(solution)/shard_map/ppermute | solution.py:275
  6.3 3.6 %collective-permute-start.3 = (f32[64,384]{1,0:T(8,128)}, f32[64,384]{1,0:T(8,128)S(1)}, u32[]{:S(2)}, u32[]{:S(2)}) collective-permute-start(f32[64,384]{1,0:T(8,128)} %get-tuple-element.16), channel_id=1, source_target_pairs={{0,12},{1,15},{2,14},{3,13},{4,8},{5,11},{6,10},{7,9},{8,4},{9,7},... | collective-permute-start | bytes 294920 | tf_op jit(solution)/shard_map/ppermute | solution.py:275
  9.9 0.0 collective-permute-start.5
  9.9 0.8 %collective-permute-start.6 = (f32[64,384]{1,0:T(8,128)}, f32[64,384]{1,0:T(8,128)S(1)}, u32[]{:S(2)}, u32[]{:S(2)}) collective-permute-start(f32[64,384]{1,0:T(8,128)} %get-tuple-element.20), channel_id=1, source_target_pairs={{0,8},{1,11},{2,10},{3,9},{4,12},{5,15},{6,14},{7,13},{8,0},{9,3},... | collective-permute-start | bytes 294920 | tf_op jit(solution)/shard_map/ppermute | solution.py:275
  10.7 3.3 %collective-permute-done.3.rest_1_ = f32[64,384]{1,0:T(8,128)S(1)} collective-permute-done((f32[64,384]{1,0:T(8,128)}, f32[64,384]{1,0:T(8,128)S(1)}, u32[]{:S(2)}, u32[]{:S(2)}) %collective-permute-start.3) | collective-permute-done | bytes 98336 | tf_op jit(solution)/shard_map/ppermute | solution.py:275
  14.0 0.5 %collective-permute-start.1 = (f32[128,256]{1,0:T(8,128)S(1)}, f32[128,256]{1,0:T(8,128)S(1)}, u32[]{:S(2)}, u32[]{:S(2)}) collective-permute-start(f32[128,256]{1,0:T(8,128)S(1)} %copy-done.1), channel_id=1, source_target_pairs={{0,1},{1,0},{2,3},{3,2},{4,5},{5,4},{6,7},{7,6},{8,9},{9,8},{10,11... | collective-permute-start | bytes 393224 | tf_op jit(solution)/shard_map/ppermute | solution.py:275
  14.5 0.1 collective-permute-start.7
  14.6 2.4 %collective-permute-done.5.rest_2_ = f32[64,384]{1,0:T(8,128)S(1)} collective-permute-done((f32[64,384]{1,0:T(8,128)}, f32[64,384]{1,0:T(8,128)S(1)}, u32[]{:S(2)}, u32[]{:S(2)}) %collective-permute-start.5) | collective-permute-done | bytes 98336 | tf_op jit(solution)/shard_map/ppermute | solution.py:275
  17.0 1.7 %collective-permute-done.6.rest_3_ = f32[64,384]{1,0:T(8,128)S(1)} collective-permute-done((f32[64,384]{1,0:T(8,128)}, f32[64,384]{1,0:T(8,128)S(1)}, u32[]{:S(2)}, u32[]{:S(2)}) %collective-permute-start.6) | collective-permute-done | bytes 98336 | tf_op jit(solution)/shard_map/ppermute | solution.py:275
  18.8 0.6 %collective-permute-start.9 = (f32[64,384]{1,0:T(8,128)S(1)}, f32[64,384]{1,0:T(8,128)S(1)}, u32[]{:S(2)}, u32[]{:S(2)}) collective-permute-start(f32[64,384]{1,0:T(8,128)S(1)} %collective-permute-done.6.rest_3_), channel_id=1, source_target_pairs={{0,1},{1,0},{2,3},{3,2},{4,5},{5,4},{6,7},{7,6},{8,9},{9,8},{10,11... | collective-permute-start | bytes 294920 | tf_op jit(solution)/shard_map/ppermute | solution.py:275
  19.4 0.6 %shard_map.77.query_ref = f32[512,256]{1,0:T(8,128)S(1)} custom-call(f32[1,512,256]{2,1,0:T(8,128)S(1)} %copy-done, f32[1,512,256]{2,1,0:T(8,128)S(1)} %collective-permute-done.core_other.other_ref, f32[128,256]{1,0:T(8,128)S(1)} %collective-permute-done.1.refs_0_, f32[168,256]{1,0:T(8,128)S(1)} %collective-permute-done.4.refs_1_, f32[128,256]{1,0:T(8,128)S(1)} %copy-done.1, ...), custom_call_target="tpu_custom_call" | custom-call | tf_op jit(solution)/shard_map/pallas_call | solution.py:245
  20.0 0.3 collective-permute-done.9.rest_6_
  20.3 1.4 %shard_map.78 = (f32[192,256]{1,0:T(8,128)S(1)}, f32[128,256]{1,0:T(8,128)S(1)}, f32[128,256]{1,0:T(8,128)S(1)}, f32[128,256]{1,0:T(8,128)S(1)}) custom-call(f32[1,512,256]{2,1,0:T(8,128)S(1)} %copy-done, f32[1,512,256]{2,1,0:T(8,128)S(1)} %collective-permute-done.core_other.other_ref, f32[512,256]{1,0:T(8,128)S(1)} %shard_map.77.query_ref, ...), custom_call_target="tpu_custom_call" | custom-call | flops 402653184 | bytes 2502656 | tf_op jit(solution)/shard_map/pallas_call | solution.py:245
  21.7 2.5 %collective-permute-start.10 = (f32[128,256]{1,0:T(8,128)S(1)}, f32[128,256]{1,0:T(8,128)S(1)}, u32[]{:S(2)}, u32[]{:S(2)}) collective-permute-start(f32[128,256]{1,0:T(8,128)S(1)} %get-tuple-element.22), channel_id=1, source_target_pairs={{0,12},{1,11},{2,14},{3,9},{4,8},{5,15},{6,10},{7,13},{8,4},{9,3},... | collective-permute-start | bytes 393224 | tf_op jit(solution)/shard_map/ppermute | solution.py:275
  24.2 3.2 %collective-permute-start.14 = (f32[128,256]{1,0:T(8,128)S(1)}, f32[128,256]{1,0:T(8,128)S(1)}, u32[]{:S(2)}, u32[]{:S(2)}) collective-permute-start(f32[128,256]{1,0:T(8,128)S(1)} %get-tuple-element.24), channel_id=1, source_target_pairs={{0,12},{3,9},{4,8},{7,13},{9,3},{10,6},{13,7},{14,2},{16,28},{19,2... | collective-permute-start | bytes 393224 | tf_op jit(solution)/shard_map/ppermute | solution.py:275
  27.5 2.3 %collective-permute-done.10.rest_0_ = f32[128,256]{1,0:T(8,128)S(1)} collective-permute-done((f32[128,256]{1,0:T(8,128)S(1)}, f32[128,256]{1,0:T(8,128)S(1)}, u32[]{:S(2)}, u32[]{:S(2)}) %collective-permute-start.10) | collective-permute-done | bytes 131104 | tf_op jit(solution)/shard_map/ppermute | solution.py:275
  29.8 0.9 %collective-permute-start.11 = (f32[128,256]{1,0:T(8,128)S(1)}, f32[128,256]{1,0:T(8,128)S(1)}, u32[]{:S(2)}, u32[]{:S(2)}) collective-permute-start(f32[128,256]{1,0:T(8,128)S(1)} %collective-permute-done.10.rest_0_), channel_id=1, source_target_pairs={{0,1},{1,0},{2,3},{3,2},{4,5},{5,4},{6,7},{7,6},{8,9},{9,8},{10,11... | collective-permute-start | bytes 393224 | tf_op jit(solution)/shard_map/ppermute | solution.py:275
  30.7 1.5 %collective-permute-done.12.rest_2_ = f32[128,256]{1,0:T(8,128)S(1)} collective-permute-done((f32[128,256]{1,0:T(8,128)S(1)}, f32[128,256]{1,0:T(8,128)S(1)}, u32[]{:S(2)}, u32[]{:S(2)}) %collective-permute-start.12) | collective-permute-done | bytes 131104 | tf_op jit(solution)/shard_map/ppermute | solution.py:275
  32.2 0.5 %collective-permute-start.15 = (f32[128,256]{1,0:T(8,128)S(1)}, f32[128,256]{1,0:T(8,128)S(1)}, u32[]{:S(2)}, u32[]{:S(2)}) collective-permute-start(f32[128,256]{1,0:T(8,128)S(1)} %collective-permute-done.14.rest_4_), channel_id=1, source_target_pairs={{0,1},{1,0},{2,3},{3,2},{4,5},{5,4},{6,7},{7,6},{8,9},{9,8},{10,11... | collective-permute-start | bytes 393224 | tf_op jit(solution)/shard_map/ppermute | solution.py:275
  32.7 0.8 %collective-permute-done.13.rest_3_ = f32[128,256]{1,0:T(8,128)S(1)} collective-permute-done((f32[128,256]{1,0:T(8,128)S(1)}, f32[128,256]{1,0:T(8,128)S(1)}, u32[]{:S(2)}, u32[]{:S(2)}) %collective-permute-start.13) | collective-permute-done | bytes 131104 | tf_op jit(solution)/shard_map/ppermute | solution.py:275
  33.5 0.2 collective-permute-done.15.rest_5_
  33.7 1.0 %shard_map.79 = (f32[16,512]{1,0:T(8,128)}, f32[1,32,256]{2,1,0:T(8,128)}, f32[2,128,256]{2,1,0:T(8,128)}) custom-call(f32[192,256]{1,0:T(8,128)S(1)} %get-tuple-element.21.own_ref, f32[128,256]{1,0:T(8,128)S(1)} %collective-permute-done.10.rest_0_, f32[128,256]{1,0:T(8,128)S(1)} %collective-permute-done.11.rest_1_, ...), custom_call_target="tpu_custom_call" | custom-call | flops 100663296 | bytes 1286144 | tf_op jit(solution)/shard_map/pallas_call | solution.py:245
  (20 shorter events, 0.0 us)
Async XLA Ops:
  0.6 18.7 %copy-start = (f32[1,512,256]{2,1,0:T(8,128)S(1)}, f32[1,512,256]{2,1,0:T(8,128)}, u32[]{:S(2)}) copy-start(f32[1,512,256]{2,1,0:T(8,128)} %core_ref.3) | copy-start | bytes 1572868
  0.6 13.4 %copy-start.1 = (f32[128,256]{1,0:T(8,128)S(1)}, f32[128,256]{1,0:T(8,128)}, u32[]{:S(2)}) copy-start(f32[128,256]{1,0:T(8,128)} %rest_6_.1) | copy-start | bytes 393220
  0.7 13.4 %collective-permute-start = (f32[1,512,256]{2,1,0:T(8,128)}, f32[1,512,256]{2,1,0:T(8,128)S(1)}, u32[]{:S(2)}, u32[]{:S(2)}) collective-permute-start(f32[1,512,256]{2,1,0:T(8,128)} %core_ref.3), channel_id=1, source_target_pairs={{0,1},{1,0},{2,3},{3,2},{4,5},{5,4},{6,7},{7,6},{8,9},{9,8},{10,11... | collective-permute-start | bytes 1572872 | tf_op jit(solution)/shard_map/ppermute | solution.py:275
  3.7 10.3 %collective-permute-start.2 = (f32[168,256]{1,0:T(8,128)}, f32[168,256]{1,0:T(8,128)S(1)}, u32[]{:S(2)}, u32[]{:S(2)}) collective-permute-start(f32[168,256]{1,0:T(8,128)} %get-tuple-element.15), channel_id=1, source_target_pairs={{0,2},{1,3},{2,0},{3,1},{4,6},{5,7},{6,4},{7,5},{8,10},{9,11},{10,... | collective-permute-start | bytes 516104 | tf_op jit(solution)/shard_map/ppermute | solution.py:275
  6.3 7.7 %collective-permute-start.3 = (f32[64,384]{1,0:T(8,128)}, f32[64,384]{1,0:T(8,128)S(1)}, u32[]{:S(2)}, u32[]{:S(2)}) collective-permute-start(f32[64,384]{1,0:T(8,128)} %get-tuple-element.16), channel_id=1, source_target_pairs={{0,12},{1,15},{2,14},{3,13},{4,8},{5,11},{6,10},{7,9},{8,4},{9,7},... | collective-permute-start | bytes 294920 | tf_op jit(solution)/shard_map/ppermute | solution.py:275
  9.9 7.1 %collective-permute-start.5 = (f32[64,384]{1,0:T(8,128)}, f32[64,384]{1,0:T(8,128)S(1)}, u32[]{:S(2)}, u32[]{:S(2)}) collective-permute-start(f32[64,384]{1,0:T(8,128)} %get-tuple-element.19), channel_id=1, source_target_pairs={{0,4},{1,7},{2,6},{3,5},{4,0},{5,3},{6,2},{7,1},{8,12},{9,15},{10,... | collective-permute-start | bytes 294920 | tf_op jit(solution)/shard_map/ppermute | solution.py:275
  9.9 10.3 %copy-start.2 = (f32[64,512]{1,0:T(8,128)S(1)}, f32[64,512]{1,0:T(8,128)}, u32[]{:S(2)}) copy-start(f32[64,512]{1,0:T(8,128)} %head_ref.1) | copy-start | bytes 393220
  9.9 10.3 %copy-start.3 = (f32[72,128]{1,0:T(8,128)S(1)}, f32[72,128]{1,0:T(8,128)}, u32[]{:S(2)}) copy-start(f32[72,128]{1,0:T(8,128)} %get-tuple-element.18.label_ref) | copy-start | bytes 110596
  9.9 8.8 %collective-permute-start.6 = (f32[64,384]{1,0:T(8,128)}, f32[64,384]{1,0:T(8,128)S(1)}, u32[]{:S(2)}, u32[]{:S(2)}) collective-permute-start(f32[64,384]{1,0:T(8,128)} %get-tuple-element.20), channel_id=1, source_target_pairs={{0,8},{1,11},{2,10},{3,9},{4,12},{5,15},{6,14},{7,13},{8,0},{9,3},... | collective-permute-start | bytes 294920 | tf_op jit(solution)/shard_map/ppermute | solution.py:275
  14.0 5.3 %collective-permute-start.4 = (f32[168,256]{1,0:T(8,128)S(1)}, f32[168,256]{1,0:T(8,128)S(1)}, u32[]{:S(2)}, u32[]{:S(2)}) collective-permute-start(f32[168,256]{1,0:T(8,128)S(1)} %collective-permute-done.2.refs_3_.rest_0_.rest_7_), channel_id=1, source_target_pairs={{0,1},{1,0},{2,3},{3,2},{4,5},{5,4},{6,7},{7,6},{8,9},{9,8},{10,11... | collective-permute-start | bytes 516104 | tf_op jit(solution)/shard_map/ppermute | solution.py:275
  14.0 5.3 %collective-permute-start.1 = (f32[128,256]{1,0:T(8,128)S(1)}, f32[128,256]{1,0:T(8,128)S(1)}, u32[]{:S(2)}, u32[]{:S(2)}) collective-permute-start(f32[128,256]{1,0:T(8,128)S(1)} %copy-done.1), channel_id=1, source_target_pairs={{0,1},{1,0},{2,3},{3,2},{4,5},{5,4},{6,7},{7,6},{8,9},{9,8},{10,11... | collective-permute-start | bytes 393224 | tf_op jit(solution)/shard_map/ppermute | solution.py:275
  14.5 5.4 %collective-permute-start.7 = (f32[64,384]{1,0:T(8,128)S(1)}, f32[64,384]{1,0:T(8,128)S(1)}, u32[]{:S(2)}, u32[]{:S(2)}) collective-permute-start(f32[64,384]{1,0:T(8,128)S(1)} %collective-permute-done.3.rest_1_), channel_id=1, source_target_pairs={{0,1},{1,0},{2,3},{3,2},{4,5},{5,4},{6,7},{7,6},{8,9},{9,8},{10,11... | collective-permute-start | bytes 294920 | tf_op jit(solution)/shard_map/ppermute | solution.py:275
  17.0 3.0 %collective-permute-start.8 = (f32[64,384]{1,0:T(8,128)S(1)}, f32[64,384]{1,0:T(8,128)S(1)}, u32[]{:S(2)}, u32[]{:S(2)}) collective-permute-start(f32[64,384]{1,0:T(8,128)S(1)} %collective-permute-done.5.rest_2_), channel_id=1, source_target_pairs={{0,1},{1,0},{2,3},{3,2},{4,5},{5,4},{6,7},{7,6},{8,9},{9,8},{10,11... | collective-permute-start | bytes 294920 | tf_op jit(solution)/shard_map/ppermute | solution.py:275
  18.8 1.5 %collective-permute-start.9 = (f32[64,384]{1,0:T(8,128)S(1)}, f32[64,384]{1,0:T(8,128)S(1)}, u32[]{:S(2)}, u32[]{:S(2)}) collective-permute-start(f32[64,384]{1,0:T(8,128)S(1)} %collective-permute-done.6.rest_3_), channel_id=1, source_target_pairs={{0,1},{1,0},{2,3},{3,2},{4,5},{5,4},{6,7},{7,6},{8,9},{9,8},{10,11... | collective-permute-start | bytes 294920 | tf_op jit(solution)/shard_map/ppermute | solution.py:275
  21.7 8.1 %collective-permute-start.10 = (f32[128,256]{1,0:T(8,128)S(1)}, f32[128,256]{1,0:T(8,128)S(1)}, u32[]{:S(2)}, u32[]{:S(2)}) collective-permute-start(f32[128,256]{1,0:T(8,128)S(1)} %get-tuple-element.22), channel_id=1, source_target_pairs={{0,12},{1,11},{2,14},{3,9},{4,8},{5,15},{6,10},{7,13},{8,4},{9,3},... | collective-permute-start | bytes 393224 | tf_op jit(solution)/shard_map/ppermute | solution.py:275
  24.2 8.0 %collective-permute-start.12 = (f32[128,256]{1,0:T(8,128)S(1)}, f32[128,256]{1,0:T(8,128)S(1)}, u32[]{:S(2)}, u32[]{:S(2)}) collective-permute-start(f32[128,256]{1,0:T(8,128)S(1)} %get-tuple-element.23), channel_id=1, source_target_pairs={{0,4},{1,5},{2,6},{3,7},{4,0},{5,1},{6,2},{7,3},{8,12},{9,13},{10,... | collective-permute-start | bytes 393224 | tf_op jit(solution)/shard_map/ppermute | solution.py:275
  24.2 8.0 %collective-permute-start.14 = (f32[128,256]{1,0:T(8,128)S(1)}, f32[128,256]{1,0:T(8,128)S(1)}, u32[]{:S(2)}, u32[]{:S(2)}) collective-permute-start(f32[128,256]{1,0:T(8,128)S(1)} %get-tuple-element.24), channel_id=1, source_target_pairs={{0,12},{3,9},{4,8},{7,13},{9,3},{10,6},{13,7},{14,2},{16,28},{19,2... | collective-permute-start | bytes 393224 | tf_op jit(solution)/shard_map/ppermute | solution.py:275
  29.8 2.9 %collective-permute-start.11 = (f32[128,256]{1,0:T(8,128)S(1)}, f32[128,256]{1,0:T(8,128)S(1)}, u32[]{:S(2)}, u32[]{:S(2)}) collective-permute-start(f32[128,256]{1,0:T(8,128)S(1)} %collective-permute-done.10.rest_0_), channel_id=1, source_target_pairs={{0,1},{1,0},{2,3},{3,2},{4,5},{5,4},{6,7},{7,6},{8,9},{9,8},{10,11... | collective-permute-start | bytes 393224 | tf_op jit(solution)/shard_map/ppermute | solution.py:275
  32.2 1.3 %collective-permute-start.13 = (f32[128,256]{1,0:T(8,128)S(1)}, f32[128,256]{1,0:T(8,128)S(1)}, u32[]{:S(2)}, u32[]{:S(2)}) collective-permute-start(f32[128,256]{1,0:T(8,128)S(1)} %collective-permute-done.12.rest_2_), channel_id=1, source_target_pairs={{0,1},{1,0},{2,3},{3,2},{4,5},{5,4},{6,7},{7,6},{8,9},{9,8},{10,11... | collective-permute-start | bytes 393224 | tf_op jit(solution)/shard_map/ppermute | solution.py:275
  32.2 1.5 %collective-permute-start.15 = (f32[128,256]{1,0:T(8,128)S(1)}, f32[128,256]{1,0:T(8,128)S(1)}, u32[]{:S(2)}, u32[]{:S(2)}) collective-permute-start(f32[128,256]{1,0:T(8,128)S(1)} %collective-permute-done.14.rest_4_), channel_id=1, source_target_pairs={{0,1},{1,0},{2,3},{3,2},{4,5},{5,4},{6,7},{7,6},{8,9},{9,8},{10,11... | collective-permute-start | bytes 393224 | tf_op jit(solution)/shard_map/ppermute | solution.py:275

commit v8 on v5

--- a/solution.py
+++ b/solution.py
@@ -279,7 +279,7 @@
         return lax.ppermute(value, axes, pairs)
 
     core_other = move(core_mats, 0, flip=1)
-    order = [wide - 1] + list(range(1, wide - 1))
+    order = [1] + list(range(wide - 1, 1, -1))
     packed = call(
         functools.partial(pack_kernel, wide, cols),
         (core_lists, labels, head_embed, tail_embed, core_mats),
@@ -304,7 +304,7 @@
         z_in[k] = got
     x_in = [move(x_out, 0, (o, o)) for o in range(1, cols)]
     tail_other = move(lax.optimization_barrier((tail_embed, core_other))[0], 0, flip=1)
-    ready = lax.optimization_barrier((x_in, z_in[order[0]]))[0]
+    ready = lax.optimization_barrier((x_in, z_in[wide - 1]))[0]
     x_other = [move(value, 0, flip=1) for value in ready]
     (query,) = call(
         query_kernel,

time: 34.9 us -> 34.9 us (level)
  no operation moved by 1% of the time
where the time goes in v8:
time: 34.9 us; the launch traced here: 34.7 us
  starting transfers between devices  15.9 us (46%)
  waiting for transfers between devices  12.6 us (36%)
  Pallas kernels  5.52 us (16%)
  between operations  0.72 us (2%)
    ppermute x16, starting transfers between devices, move(): return lax.ppermute(value, axes, pairs)  15.9 us
    ppermute x16, waiting for transfers between devices, move(): return lax.ppermute(value, axes, pairs)  12.6 us
    pallas_call x4, Pallas kernels, call(): pl.pallas_call(kernel, out_shape=tuple((jax.ShapeDtypeStruct(shape, F32)...  5.52 us
  transfers between devices with their start and end apart: 16, of which 8 were waited for; matrix products, arithmetic and copies ran while one was open for 0% of the time, Pallas kernels for 9%

profile of v8, /device:TPU:0, one launch (start us, length us, event | category | flops | bytes accessed | tf_op | source)
XLA Modules:
  0.0 34.7 jit_solution(16119836584707651876)
XLA Ops:
  0.7 0.5 %collective-permute-start = (f32[1,512,256]{2,1,0:T(8,128)}, f32[1,512,256]{2,1,0:T(8,128)S(1)}, u32[]{:S(2)}, u32[]{:S(2)}) collective-permute-start(f32[1,512,256]{2,1,0:T(8,128)} %core_ref.3), channel_id=1, source_target_pairs={{0,1},{1,0},{2,3},{3,2},{4,5},{5,4},{6,7},{7,6},{8,9},{9,8},{10,11... | collective-permute-start | bytes 1572872 | tf_op jit(solution)/shard_map/ppermute | solution.py:279
  1.2 2.5 %shard_map.76 = (f32[64,384]{1,0:T(8,128)}, f32[64,384]{1,0:T(8,128)}, f32[64,384]{1,0:T(8,128)}, f32[168,256]{1,0:T(8,128)}, f32[64,512]{1,0:T(8,128)}, /*index=5*/f32[72,128]{1,0:T(8,128)}) custom-call(s32[1,8]{1,0:T(1,128)} %list_hbm.1, s32[64,8,128]{2,1,0:T(8,128)} %label_hbm.1, f32[64,512]{1,0:T(8,128)} %head_hbm.1, f32[128,256]{1,0:T(8,128)} %rest_6_.1, ...), custom_call_target="tpu_custom_call" | custom-call | bytes 1048608 | tf_op jit(solution)/shard_map/pallas_call | solution.py:249
  3.6 2.6 %collective-permute-start.2 = (f32[168,256]{1,0:T(8,128)}, f32[168,256]{1,0:T(8,128)S(1)}, u32[]{:S(2)}, u32[]{:S(2)}) collective-permute-start(f32[168,256]{1,0:T(8,128)} %get-tuple-element.16), channel_id=1, source_target_pairs={{0,2},{1,3},{2,0},{3,1},{4,6},{5,7},{6,4},{7,5},{8,10},{9,11},{10,... | collective-permute-start | bytes 516104 | tf_op jit(solution)/shard_map/ppermute | solution.py:279
  6.3 3.6 %collective-permute-start.3 = (f32[64,384]{1,0:T(8,128)}, f32[64,384]{1,0:T(8,128)S(1)}, u32[]{:S(2)}, u32[]{:S(2)}) collective-permute-start(f32[64,384]{1,0:T(8,128)} %get-tuple-element.17), channel_id=1, source_target_pairs={{0,12},{1,15},{2,14},{3,13},{4,8},{5,11},{6,10},{7,9},{8,4},{9,7},... | collective-permute-start | bytes 294920 | tf_op jit(solution)/shard_map/ppermute | solution.py:279
  9.9 0.0 collective-permute-start.5
  9.9 0.8 %collective-permute-start.6 = (f32[64,384]{1,0:T(8,128)}, f32[64,384]{1,0:T(8,128)S(1)}, u32[]{:S(2)}, u32[]{:S(2)}) collective-permute-start(f32[64,384]{1,0:T(8,128)} %get-tuple-element.22), channel_id=1, source_target_pairs={{0,8},{1,11},{2,10},{3,9},{4,12},{5,15},{6,14},{7,13},{8,0},{9,3},... | collective-permute-start | bytes 294920 | tf_op jit(solution)/shard_map/ppermute | solution.py:279
  10.7 3.3 %collective-permute-done.3.rest_2_ = f32[64,384]{1,0:T(8,128)S(1)} collective-permute-done((f32[64,384]{1,0:T(8,128)}, f32[64,384]{1,0:T(8,128)S(1)}, u32[]{:S(2)}, u32[]{:S(2)}) %collective-permute-start.3) | collective-permute-done | bytes 98336 | tf_op jit(solution)/shard_map/ppermute | solution.py:279
  14.0 0.5 %collective-permute-start.1 = (f32[128,256]{1,0:T(8,128)S(1)}, f32[128,256]{1,0:T(8,128)S(1)}, u32[]{:S(2)}, u32[]{:S(2)}) collective-permute-start(f32[128,256]{1,0:T(8,128)S(1)} %copy-done.1), channel_id=1, source_target_pairs={{0,1},{1,0},{2,3},{3,2},{4,5},{5,4},{6,7},{7,6},{8,9},{9,8},{10,11... | collective-permute-start | bytes 393224 | tf_op jit(solution)/shard_map/ppermute | solution.py:279
  14.5 0.1 collective-permute-start.8
  14.5 2.4 %collective-permute-done.5.rest_1_ = f32[64,384]{1,0:T(8,128)S(1)} collective-permute-done((f32[64,384]{1,0:T(8,128)}, f32[64,384]{1,0:T(8,128)S(1)}, u32[]{:S(2)}, u32[]{:S(2)}) %collective-permute-start.5) | collective-permute-done | bytes 98336 | tf_op jit(solution)/shard_map/ppermute | solution.py:279
  17.0 1.7 %collective-permute-done.6.rest_3_ = f32[64,384]{1,0:T(8,128)S(1)} collective-permute-done((f32[64,384]{1,0:T(8,128)}, f32[64,384]{1,0:T(8,128)S(1)}, u32[]{:S(2)}, u32[]{:S(2)}) %collective-permute-start.6) | collective-permute-done | bytes 98336 | tf_op jit(solution)/shard_map/ppermute | solution.py:279
  18.7 0.6 %collective-permute-start.9 = (f32[64,384]{1,0:T(8,128)S(1)}, f32[64,384]{1,0:T(8,128)S(1)}, u32[]{:S(2)}, u32[]{:S(2)}) collective-permute-start(f32[64,384]{1,0:T(8,128)S(1)} %collective-permute-done.6.rest_3_), channel_id=1, source_target_pairs={{0,1},{1,0},{2,3},{3,2},{4,5},{5,4},{6,7},{7,6},{8,9},{9,8},{10,11... | collective-permute-start | bytes 294920 | tf_op jit(solution)/shard_map/ppermute | solution.py:279
  19.3 0.6 %shard_map.77.query_ref = f32[512,256]{1,0:T(8,128)S(1)} custom-call(f32[1,512,256]{2,1,0:T(8,128)S(1)} %copy-done, f32[1,512,256]{2,1,0:T(8,128)S(1)} %collective-permute-done.core_other.other_ref, f32[128,256]{1,0:T(8,128)S(1)} %collective-permute-done.1.refs_0_, f32[168,256]{1,0:T(8,128)S(1)} %collective-permute-done.4.refs_1_, f32[128,256]{1,0:T(8,128)S(1)} %copy-done.1, ...), custom_call_target="tpu_custom_call" | custom-call | tf_op jit(solution)/shard_map/pallas_call | solution.py:249
  19.9 0.3 collective-permute-done.9.rest_6_
  20.2 1.4 %shard_map.78 = (f32[192,256]{1,0:T(8,128)S(1)}, f32[128,256]{1,0:T(8,128)S(1)}, f32[128,256]{1,0:T(8,128)S(1)}, f32[128,256]{1,0:T(8,128)S(1)}) custom-call(f32[1,512,256]{2,1,0:T(8,128)S(1)} %copy-done, f32[1,512,256]{2,1,0:T(8,128)S(1)} %collective-permute-done.core_other.other_ref, f32[512,256]{1,0:T(8,128)S(1)} %shard_map.77.query_ref, ...), custom_call_target="tpu_custom_call" | custom-call | flops 402653184 | bytes 2502656 | tf_op jit(solution)/shard_map/pallas_call | solution.py:249
  21.6 2.5 %collective-permute-start.10 = (f32[128,256]{1,0:T(8,128)S(1)}, f32[128,256]{1,0:T(8,128)S(1)}, u32[]{:S(2)}, u32[]{:S(2)}) collective-permute-start(f32[128,256]{1,0:T(8,128)S(1)} %get-tuple-element.24), channel_id=1, source_target_pairs={{0,12},{1,11},{2,14},{3,9},{4,8},{5,15},{6,10},{7,13},{8,4},{9,3},... | collective-permute-start | bytes 393224 | tf_op jit(solution)/shard_map/ppermute | solution.py:279
  24.1 3.2 %collective-permute-start.14 = (f32[128,256]{1,0:T(8,128)S(1)}, f32[128,256]{1,0:T(8,128)S(1)}, u32[]{:S(2)}, u32[]{:S(2)}) collective-permute-start(f32[128,256]{1,0:T(8,128)S(1)} %get-tuple-element.26), channel_id=1, source_target_pairs={{0,12},{3,9},{4,8},{7,13},{9,3},{10,6},{13,7},{14,2},{16,28},{19,2... | collective-permute-start | bytes 393224 | tf_op jit(solution)/shard_map/ppermute | solution.py:279
  27.4 2.3 %collective-permute-done.10.rest_0_ = f32[128,256]{1,0:T(8,128)S(1)} collective-permute-done((f32[128,256]{1,0:T(8,128)S(1)}, f32[128,256]{1,0:T(8,128)S(1)}, u32[]{:S(2)}, u32[]{:S(2)}) %collective-permute-start.10) | collective-permute-done | bytes 131104 | tf_op jit(solution)/shard_map/ppermute | solution.py:279
  29.8 0.9 %collective-permute-start.11 = (f32[128,256]{1,0:T(8,128)S(1)}, f32[128,256]{1,0:T(8,128)S(1)}, u32[]{:S(2)}, u32[]{:S(2)}) collective-permute-start(f32[128,256]{1,0:T(8,128)S(1)} %collective-permute-done.10.rest_0_), channel_id=1, source_target_pairs={{0,1},{1,0},{2,3},{3,2},{4,5},{5,4},{6,7},{7,6},{8,9},{9,8},{10,11... | collective-permute-start | bytes 393224 | tf_op jit(solution)/shard_map/ppermute | solution.py:279
  30.6 1.5 %collective-permute-done.12.rest_2_ = f32[128,256]{1,0:T(8,128)S(1)} collective-permute-done((f32[128,256]{1,0:T(8,128)S(1)}, f32[128,256]{1,0:T(8,128)S(1)}, u32[]{:S(2)}, u32[]{:S(2)}) %collective-permute-start.12) | collective-permute-done | bytes 131104 | tf_op jit(solution)/shard_map/ppermute | solution.py:279
  32.1 0.5 %collective-permute-start.15 = (f32[128,256]{1,0:T(8,128)S(1)}, f32[128,256]{1,0:T(8,128)S(1)}, u32[]{:S(2)}, u32[]{:S(2)}) collective-permute-start(f32[128,256]{1,0:T(8,128)S(1)} %collective-permute-done.14.rest_4_), channel_id=1, source_target_pairs={{0,1},{1,0},{2,3},{3,2},{4,5},{5,4},{6,7},{7,6},{8,9},{9,8},{10,11... | collective-permute-start | bytes 393224 | tf_op jit(solution)/shard_map/ppermute | solution.py:279
  32.7 0.8 %collective-permute-done.13.rest_3_ = f32[128,256]{1,0:T(8,128)S(1)} collective-permute-done((f32[128,256]{1,0:T(8,128)S(1)}, f32[128,256]{1,0:T(8,128)S(1)}, u32[]{:S(2)}, u32[]{:S(2)}) %collective-permute-start.13) | collective-permute-done | bytes 131104 | tf_op jit(solution)/shard_map/ppermute | solution.py:279
  33.5 0.2 collective-permute-done.15.rest_5_
  33.7 1.0 %shard_map.79 = (f32[16,512]{1,0:T(8,128)}, f32[1,32,256]{2,1,0:T(8,128)}, f32[2,128,256]{2,1,0:T(8,128)}) custom-call(f32[192,256]{1,0:T(8,128)S(1)} %get-tuple-element.23.own_ref, f32[128,256]{1,0:T(8,128)S(1)} %collective-permute-done.10.rest_0_, f32[128,256]{1,0:T(8,128)S(1)} %collective-permute-done.11.rest_1_, ...), custom_call_target="tpu_custom_call" | custom-call | flops 100663296 | bytes 1286144 | tf_op jit(solution)/shard_map/pallas_call | solution.py:249
  (20 shorter events, 0.0 us)
Async XLA Ops:
  0.6 18.6 %copy-start = (f32[1,512,256]{2,1,0:T(8,128)S(1)}, f32[1,512,256]{2,1,0:T(8,128)}, u32[]{:S(2)}) copy-start(f32[1,512,256]{2,1,0:T(8,128)} %core_ref.3) | copy-start | bytes 1572868
  0.6 13.3 %copy-start.1 = (f32[128,256]{1,0:T(8,128)S(1)}, f32[128,256]{1,0:T(8,128)}, u32[]{:S(2)}) copy-start(f32[128,256]{1,0:T(8,128)} %rest_6_.1) | copy-start | bytes 393220
  0.7 13.3 %collective-permute-start = (f32[1,512,256]{2,1,0:T(8,128)}, f32[1,512,256]{2,1,0:T(8,128)S(1)}, u32[]{:S(2)}, u32[]{:S(2)}) collective-permute-start(f32[1,512,256]{2,1,0:T(8,128)} %core_ref.3), channel_id=1, source_target_pairs={{0,1},{1,0},{2,3},{3,2},{4,5},{5,4},{6,7},{7,6},{8,9},{9,8},{10,11... | collective-permute-start | bytes 1572872 | tf_op jit(solution)/shard_map/ppermute | solution.py:279
  3.6 10.3 %collective-permute-start.2 = (f32[168,256]{1,0:T(8,128)}, f32[168,256]{1,0:T(8,128)S(1)}, u32[]{:S(2)}, u32[]{:S(2)}) collective-permute-start(f32[168,256]{1,0:T(8,128)} %get-tuple-element.16), channel_id=1, source_target_pairs={{0,2},{1,3},{2,0},{3,1},{4,6},{5,7},{6,4},{7,5},{8,10},{9,11},{10,... | collective-permute-start | bytes 516104 | tf_op jit(solution)/shard_map/ppermute | solution.py:279
  6.3 7.7 %collective-permute-start.3 = (f32[64,384]{1,0:T(8,128)}, f32[64,384]{1,0:T(8,128)S(1)}, u32[]{:S(2)}, u32[]{:S(2)}) collective-permute-start(f32[64,384]{1,0:T(8,128)} %get-tuple-element.17), channel_id=1, source_target_pairs={{0,12},{1,15},{2,14},{3,13},{4,8},{5,11},{6,10},{7,9},{8,4},{9,7},... | collective-permute-start | bytes 294920 | tf_op jit(solution)/shard_map/ppermute | solution.py:279
  9.9 7.1 %collective-permute-start.5 = (f32[64,384]{1,0:T(8,128)}, f32[64,384]{1,0:T(8,128)S(1)}, u32[]{:S(2)}, u32[]{:S(2)}) collective-permute-start(f32[64,384]{1,0:T(8,128)} %get-tuple-element.21), channel_id=1, source_target_pairs={{0,4},{1,7},{2,6},{3,5},{4,0},{5,3},{6,2},{7,1},{8,12},{9,15},{10,... | collective-permute-start | bytes 294920 | tf_op jit(solution)/shard_map/ppermute | solution.py:279
  9.9 10.3 %copy-start.2 = (f32[64,512]{1,0:T(8,128)S(1)}, f32[64,512]{1,0:T(8,128)}, u32[]{:S(2)}) copy-start(f32[64,512]{1,0:T(8,128)} %get-tuple-element.19.head_ref) | copy-start | bytes 393220
  9.9 10.3 %copy-start.3 = (f32[72,128]{1,0:T(8,128)S(1)}, f32[72,128]{1,0:T(8,128)}, u32[]{:S(2)}) copy-start(f32[72,128]{1,0:T(8,128)} %get-tuple-element.20.label_ref) | copy-start | bytes 110596
  9.9 8.8 %collective-permute-start.6 = (f32[64,384]{1,0:T(8,128)}, f32[64,384]{1,0:T(8,128)S(1)}, u32[]{:S(2)}, u32[]{:S(2)}) collective-permute-start(f32[64,384]{1,0:T(8,128)} %get-tuple-element.22), channel_id=1, source_target_pairs={{0,8},{1,11},{2,10},{3,9},{4,12},{5,15},{6,14},{7,13},{8,0},{9,3},... | collective-permute-start | bytes 294920 | tf_op jit(solution)/shard_map/ppermute | solution.py:279
  14.0 5.3 %collective-permute-start.4 = (f32[168,256]{1,0:T(8,128)S(1)}, f32[168,256]{1,0:T(8,128)S(1)}, u32[]{:S(2)}, u32[]{:S(2)}) collective-permute-start(f32[168,256]{1,0:T(8,128)S(1)} %collective-permute-done.2.refs_3_.rest_0_.rest_7_), channel_id=1, source_target_pairs={{0,1},{1,0},{2,3},{3,2},{4,5},{5,4},{6,7},{7,6},{8,9},{9,8},{10,11... | collective-permute-start | bytes 516104 | tf_op jit(solution)/shard_map/ppermute | solution.py:279
  14.0 5.3 %collective-permute-start.1 = (f32[128,256]{1,0:T(8,128)S(1)}, f32[128,256]{1,0:T(8,128)S(1)}, u32[]{:S(2)}, u32[]{:S(2)}) collective-permute-start(f32[128,256]{1,0:T(8,128)S(1)} %copy-done.1), channel_id=1, source_target_pairs={{0,1},{1,0},{2,3},{3,2},{4,5},{5,4},{6,7},{7,6},{8,9},{9,8},{10,11... | collective-permute-start | bytes 393224 | tf_op jit(solution)/shard_map/ppermute | solution.py:279
  14.5 5.4 %collective-permute-start.8 = (f32[64,384]{1,0:T(8,128)S(1)}, f32[64,384]{1,0:T(8,128)S(1)}, u32[]{:S(2)}, u32[]{:S(2)}) collective-permute-start(f32[64,384]{1,0:T(8,128)S(1)} %collective-permute-done.3.rest_2_), channel_id=1, source_target_pairs={{0,1},{1,0},{2,3},{3,2},{4,5},{5,4},{6,7},{7,6},{8,9},{9,8},{10,11... | collective-permute-start | bytes 294920 | tf_op jit(solution)/shard_map/ppermute | solution.py:279
  17.0 3.0 %collective-permute-start.7 = (f32[64,384]{1,0:T(8,128)S(1)}, f32[64,384]{1,0:T(8,128)S(1)}, u32[]{:S(2)}, u32[]{:S(2)}) collective-permute-start(f32[64,384]{1,0:T(8,128)S(1)} %collective-permute-done.5.rest_1_), channel_id=1, source_target_pairs={{0,1},{1,0},{2,3},{3,2},{4,5},{5,4},{6,7},{7,6},{8,9},{9,8},{10,11... | collective-permute-start | bytes 294920 | tf_op jit(solution)/shard_map/ppermute | solution.py:279
  18.7 1.5 %collective-permute-start.9 = (f32[64,384]{1,0:T(8,128)S(1)}, f32[64,384]{1,0:T(8,128)S(1)}, u32[]{:S(2)}, u32[]{:S(2)}) collective-permute-start(f32[64,384]{1,0:T(8,128)S(1)} %collective-permute-done.6.rest_3_), channel_id=1, source_target_pairs={{0,1},{1,0},{2,3},{3,2},{4,5},{5,4},{6,7},{7,6},{8,9},{9,8},{10,11... | collective-permute-start | bytes 294920 | tf_op jit(solution)/shard_map/ppermute | solution.py:279
  21.6 8.1 %collective-permute-start.10 = (f32[128,256]{1,0:T(8,128)S(1)}, f32[128,256]{1,0:T(8,128)S(1)}, u32[]{:S(2)}, u32[]{:S(2)}) collective-permute-start(f32[128,256]{1,0:T(8,128)S(1)} %get-tuple-element.24), channel_id=1, source_target_pairs={{0,12},{1,11},{2,14},{3,9},{4,8},{5,15},{6,10},{7,13},{8,4},{9,3},... | collective-permute-start | bytes 393224 | tf_op jit(solution)/shard_map/ppermute | solution.py:279
  24.1 8.0 %collective-permute-start.12 = (f32[128,256]{1,0:T(8,128)S(1)}, f32[128,256]{1,0:T(8,128)S(1)}, u32[]{:S(2)}, u32[]{:S(2)}) collective-permute-start(f32[128,256]{1,0:T(8,128)S(1)} %get-tuple-element.25), channel_id=1, source_target_pairs={{0,4},{1,5},{2,6},{3,7},{4,0},{5,1},{6,2},{7,3},{8,12},{9,13},{10,... | collective-permute-start | bytes 393224 | tf_op jit(solution)/shard_map/ppermute | solution.py:279
  24.1 8.0 %collective-permute-start.14 = (f32[128,256]{1,0:T(8,128)S(1)}, f32[128,256]{1,0:T(8,128)S(1)}, u32[]{:S(2)}, u32[]{:S(2)}) collective-permute-start(f32[128,256]{1,0:T(8,128)S(1)} %get-tuple-element.26), channel_id=1, source_target_pairs={{0,12},{3,9},{4,8},{7,13},{9,3},{10,6},{13,7},{14,2},{16,28},{19,2... | collective-permute-start | bytes 393224 | tf_op jit(solution)/shard_map/ppermute | solution.py:279
  29.8 2.9 %collective-permute-start.11 = (f32[128,256]{1,0:T(8,128)S(1)}, f32[128,256]{1,0:T(8,128)S(1)}, u32[]{:S(2)}, u32[]{:S(2)}) collective-permute-start(f32[128,256]{1,0:T(8,128)S(1)} %collective-permute-done.10.rest_0_), channel_id=1, source_target_pairs={{0,1},{1,0},{2,3},{3,2},{4,5},{5,4},{6,7},{7,6},{8,9},{9,8},{10,11... | collective-permute-start | bytes 393224 | tf_op jit(solution)/shard_map/ppermute | solution.py:279
  32.1 1.3 %collective-permute-start.13 = (f32[128,256]{1,0:T(8,128)S(1)}, f32[128,256]{1,0:T(8,128)S(1)}, u32[]{:S(2)}, u32[]{:S(2)}) collective-permute-start(f32[128,256]{1,0:T(8,128)S(1)} %collective-permute-done.12.rest_2_), channel_id=1, source_target_pairs={{0,1},{1,0},{2,3},{3,2},{4,5},{5,4},{6,7},{7,6},{8,9},{9,8},{10,11... | collective-permute-start | bytes 393224 | tf_op jit(solution)/shard_map/ppermute | solution.py:279
  32.1 1.5 %collective-permute-start.15 = (f32[128,256]{1,0:T(8,128)S(1)}, f32[128,256]{1,0:T(8,128)S(1)}, u32[]{:S(2)}, u32[]{:S(2)}) collective-permute-start(f32[128,256]{1,0:T(8,128)S(1)} %collective-permute-done.14.rest_4_), channel_id=1, source_target_pairs={{0,1},{1,0},{2,3},{3,2},{4,5},{5,4},{6,7},{7,6},{8,9},{9,8},{10,11... | collective-permute-start | bytes 393224 | tf_op jit(solution)/shard_map/ppermute | solution.py:279
